TPU v7x, 128 devices: a whole 4x4x4 slice. The times are simulated.
128 devices in a mesh: section: 32 (over z, x_hi, y), tensor: 4 (over x_lo, core).
Axes of the slice: x: 4 (x_hi: 2, x_lo: 2; x = x_hi * 2 + x_lo), y: 4, z: 4, core: 2. Of those that a mesh axis runs over, the one named last changes fastest.
Arguments:
- act: bfloat16 [32, 1024, 2048], P('section', 'tensor'), may hold values from -6 to 6
- group_of: int32 [32], P('section'), may hold values from 0 to 1, as said below
- gain: bfloat16 [32, 2, 2048], P('section'), may hold values from 0.5 to 1.5
- w_in: bfloat16 [32, 2, 2048, 4096], P('section', None, None, 'tensor'), may hold values from -0.125 to 0.125
- w_out: bfloat16 [32, 2, 4096, 2048], P('section', None, 'tensor'), may hold values from -0.09375 to 0.09375
Outputs:
- next_act: bfloat16 [32, 1024, 2048], P('section', 'tensor')
- parked: bfloat16 [32, 1024, 2048], P('section', 'tensor')
Inputs may be any that keep to these rules, and one draw needn't show every extreme that they name: `group_of`: every entry is 0 or 1; the entry of the last section is 0.
All inputs are finite; a program needn't handle non-finite values.
Results may differ from a plain program's by a relative error of at most 0.017.
Values may be sent and summed in bfloat16 or wider, within the bound.
No kernel may reach another device: no remote copies, remote signals or barrier semaphores. Data moves between devices by JAX's collectives and lax.ppermute only.
A program may use at most 128 MiB of HBM per device.

v0:
```python
import jax
import jax.numpy as jnp
from jax import lax
from jax.sharding import PartitionSpec as P

eps = 1e-05


def from_behind(x, axis, by):
    devices = lax.axis_size(axis)
    return lax.ppermute(x, axis, [(i, (i + by) % devices) for i in range(devices)])


def partner(block, axis, stride):
    count = lax.axis_size(axis)
    route = []
    for low in range(count):
        high = low | 1 << stride
        if high != low and high < count:
            route += [(low, high), (high, low)]
    return lax.ppermute(block, axis, route)


def normalize(row_block, gain_row):
    as_float = row_block.astype(jnp.float32)
    centred = as_float - jnp.mean(as_float, axis=-1, keepdims=True)
    spread = jnp.mean(centred * centred, axis=-1, keepdims=True)
    return (centred * lax.rsqrt(spread + eps) * gain_row.astype(jnp.float32)).astype(jnp.bfloat16)


def select(packed_table, group_id):
    return lax.dynamic_index_in_dim(packed_table[0], group_id, 0, keepdims=False)


def activate(normed, w_first):
    return jax.nn.gelu(
        jnp.dot(normed, w_first, preferred_element_type=jnp.float32), approximate=True
    ).astype(jnp.bfloat16)


def contract(hidden, w_second, own_rows):
    summed = lax.psum_scatter(
        jnp.dot(hidden, w_second, preferred_element_type=jnp.float32).astype(jnp.bfloat16),
        "tensor",
        scatter_dimension=0,
        tiled=True,
    ).astype(jnp.float32)
    return (own_rows.astype(jnp.float32) + summed).astype(jnp.bfloat16)


def body(act, group_of, gain, w_in, w_out):
    shard_rows = act[0]
    share_rows = shard_rows.shape[0]
    group_now = group_of[0]
    section_place = lax.axis_index("section")
    gain_first = select(gain, group_now)
    first_in = select(w_in, group_now)
    first_out = select(w_out, group_now)
    whole_rows = lax.all_gather(shard_rows, "tensor", axis=0, tiled=True)
    hidden_one = activate(normalize(whole_rows, gain_first), first_in)
    branch = lax.psum(
        jnp.dot(hidden_one, first_out, preferred_element_type=jnp.float32).astype(jnp.bfloat16),
        "tensor",
    ).astype(jnp.float32)
    first_result = (whole_rows.astype(jnp.float32) + branch).astype(jnp.bfloat16)
    arrived, prior_group = from_behind((first_result, group_of), "section", 1)
    group_two = jnp.where(section_place == 0, 1, prior_group[0]).astype(jnp.int32)
    gain_second = select(gain, group_two)
    second_in = select(w_in, group_two)
    second_out = select(w_out, group_two)
    own_start = lax.axis_index("tensor") * share_rows
    own_rows = lax.dynamic_slice_in_dim(arrived, own_start, share_rows, 0)
    hidden_two = activate(normalize(arrived, gain_second), second_in)
    second_result = contract(hidden_two, second_out, own_rows)
    levels = lax.axis_size("section").bit_length() - 1
    bit_order = list(range(levels))
    stashed = own_rows
    for swap_bit in bit_order:
        stashed = partner(stashed, "section", swap_bit)
    return (second_result[None], stashed[None])


def solution(mesh):
    placed = (
        P("section", "tensor", None),
        P("section"),
        P("section", None, None),
        P("section", None, None, "tensor"),
        P("section", None, "tensor", None),
    )
    return jax.shard_map(
        body,
        mesh=mesh,
        in_specs=placed,
        out_specs=(P("section", "tensor", None), P("section", "tensor", None)),
        check_vma=False,
    )
```

profile of v0, /device:TPU:0, one launch (start us, length us, event | category | flops | bytes accessed | tf_op | source)
XLA Modules:
  0.0 468.4 jit_solution(9216411662059197953)
XLA Ops:
  7.9 1.7 collective-permute-start.1
  10.4 8.4 %collective-permute-done.1 = s32[1]{0:T(128)} collective-permute-done((s32[1]{0:T(128)}, s32[1]{0:T(128)}, u32[]{:S(2)}, u32[]{:S(2)}) %collective-permute-start.1) | collective-permute-done | bytes 36 | tf_op jit(solution)/shard_map/ppermute | solution.py:11
  20.2 38.0 %all-gather.3.cloned.1.call-done = bf16[1,1024,2048]{2,1,0:T(8,128)(2,1)} async-done(((bf16[1,256,2048]{2,1,0:T(8,128)(2,1)}), bf16[1,1024,2048]{2,1,0:T(8,128)(2,1)}) %all-gather.3.cloned.1.call-update) | async-done | bytes 4194320 | tf_op jit(solution)/shard_map/all_gather | solution.py:59
  58.2 3.0 convert_reduce_fusion
  61.6 1.2 fusion.6
  62.8 15.5 %fusion.49 = bf16[1024,2048]{1,0:T(8,128)(2,1)} fusion(bf16[1,2,1024,2048]{3,2,1,0:T(8,128)(2,1)} %param.9, s32[]{:T(128)S(6)} %select_n.20, bf16[1,2,2048,1024]{3,2,1,0:T(8,128)(2,1)} %param.8, bf16[1,1024,2048]{2,1,0:T(8,128)(2,1)} %all-gather.3.cloned.1.call-done, f32[2048]{0:T(1024)S(1)} %bitcast.59, f32[1024]{0:T(1024)S(1)} %add_rsqrt_fusion.1, ...), kind=kOutput, calls=%fused_computation.53 | convolution fusion | flops 8611954688 | bytes 16794624 | tf_op jit(solution)/shard_map/dot_general | solution.py:62
  78.4 92.9 %all-reduce.2.cloned.1.call-done = bf16[1024,2048]{1,0:T(8,128)(2,1)} async-done(((bf16[1024,2048]{1,0:T(8,128)(2,1)}), bf16[1024,2048]{1,0:T(8,128)(2,1)}) %all-reduce.2.cloned.1.call-update) | async-done | bytes 4194320 | tf_op jit(solution)/shard_map/psum | solution.py:61
  171.3 5.4 %fusion.12 = bf16[1024,2048]{1,0:T(8,128)(2,1)S(1)} fusion(bf16[1,1024,2048]{2,1,0:T(8,128)(2,1)} %all-gather.3.cloned.1.call-done, bf16[1024,2048]{1,0:T(8,128)(2,1)} %all-reduce.2.cloned.1.call-done), kind=kLoop, calls=%fused_computation.16 | loop fusion | flops 8388608 | bytes 12582912 | tf_op jit(solution)/shard_map/convert_element_type | solution.py:65
  176.7 1.7 collective-permute-start
  178.4 97.0 %collective-permute-done = bf16[1024,2048]{1,0:T(8,128)(2,1)S(1)} collective-permute-done((bf16[1024,2048]{1,0:T(8,128)(2,1)S(1)}, bf16[1024,2048]{1,0:T(8,128)(2,1)S(1)}, u32[]{:S(2)}, u32[]{:S(2)}) %collective-permute-start) | collective-permute-done | bytes 4194336 | tf_op jit(solution)/shard_map/ppermute | solution.py:11
  276.0 1.2 fusion.9
  277.3 15.5 %fusion.52 = bf16[1024,2048]{1,0:T(8,128)(2,1)} fusion(bf16[1,2,1024,2048]{3,2,1,0:T(8,128)(2,1)} %param.9, s32[]{:T(128)S(6)} %select_n.23, bf16[1,2,2048,1024]{3,2,1,0:T(8,128)(2,1)} %param.8, bf16[1024,2048]{1,0:T(8,128)(2,1)} %copy-done.1, f32[2048]{0:T(1024)S(1)} %bitcast.58, f32[1024]{0:T(1024)S(1)} %add_rsqrt_fusion, f32[1024]{0:T(1024)S(1)} %broadcast_multiply_fusion), kind=kOutput, calls=%fused_computation.54 | convolution fusion | flops 8611954688 | bytes 16794624 | tf_op jit(solution)/shard_map/dot_general | solution.py:43
  292.9 41.9 %reduce-scatter.2.cloned.1.call-done = bf16[256,2048]{1,0:T(8,128)(2,1)} async-done(((bf16[1024,2048]{1,0:T(8,128)(2,1)}), bf16[256,2048]{1,0:T(8,128)(2,1)}) %reduce-scatter.2.cloned.1.call-update) | async-done | bytes 1048592 | tf_op jit(solution)/shard_map/reduce_scatter | solution.py:42
  334.8 2.9 fusion.75
  337.7 1.5 collective-permute-start.2
  339.2 23.7 %collective-permute-done.2 = bf16[256,2048]{1,0:T(8,128)(2,1)S(1)} collective-permute-done((bf16[256,2048]{1,0:T(8,128)(2,1)S(1)}, bf16[256,2048]{1,0:T(8,128)(2,1)S(1)}, u32[]{:S(2)}, u32[]{:S(2)}) %collective-permute-start.2) | collective-permute-done | bytes 1048608 | tf_op jit(solution)/shard_map/ppermute | solution.py:21
  362.9 3.0 collective-permute-start.3
  365.9 22.8 %collective-permute-done.3 = bf16[256,2048]{1,0:T(8,128)(2,1)S(1)} collective-permute-done((bf16[256,2048]{1,0:T(8,128)(2,1)S(1)}, bf16[256,2048]{1,0:T(8,128)(2,1)S(1)}, u32[]{:S(2)}, u32[]{:S(2)}) %collective-permute-start.3) | collective-permute-done | bytes 1048608 | tf_op jit(solution)/shard_map/ppermute | solution.py:21
  388.7 2.7 collective-permute-start.4
  391.4 22.2 %collective-permute-done.4 = bf16[256,2048]{1,0:T(8,128)(2,1)S(1)} collective-permute-done((bf16[256,2048]{1,0:T(8,128)(2,1)S(1)}, bf16[256,2048]{1,0:T(8,128)(2,1)S(1)}, u32[]{:S(2)}, u32[]{:S(2)}) %collective-permute-start.4) | collective-permute-done | bytes 1048608 | tf_op jit(solution)/shard_map/ppermute | solution.py:21
  413.6 1.6 collective-permute-start.5
  415.2 20.9 %collective-permute-done.5 = bf16[256,2048]{1,0:T(8,128)(2,1)S(1)} collective-permute-done((bf16[256,2048]{1,0:T(8,128)(2,1)S(1)}, bf16[256,2048]{1,0:T(8,128)(2,1)S(1)}, u32[]{:S(2)}, u32[]{:S(2)}) %collective-permute-start.5) | collective-permute-done | bytes 1048608 | tf_op jit(solution)/shard_map/ppermute | solution.py:21
  436.1 3.6 collective-permute-start.6
  439.7 21.2 %collective-permute-done.6 = bf16[256,2048]{1,0:T(8,128)(2,1)S(1)} collective-permute-done((bf16[256,2048]{1,0:T(8,128)(2,1)S(1)}, bf16[256,2048]{1,0:T(8,128)(2,1)S(1)}, u32[]{:S(2)}, u32[]{:S(2)}) %collective-permute-start.6) | collective-permute-done | bytes 1048608 | tf_op jit(solution)/shard_map/ppermute | solution.py:21
  (17 shorter events, 3.8 us)
Async XLA Ops:
  7.2 51.0 %all-gather.3.cloned.1.call-start = ((), (), s32[]{:S(2)}) async-start(), calls=%async_computation.3 | async-start | bytes 5242880 | tf_op jit(solution)/shard_map/all_gather | solution.py:59
  7.9 163.4 %all-reduce.2.cloned.1.call-start = ((), (), s32[]{:S(2)}) async-start(), calls=%async_computation.1 | async-start | bytes 8388608 | tf_op jit(solution)/shard_map/psum | solution.py:61
  7.9 10.9 %collective-permute-start.1 = (s32[1]{0:T(128)}, s32[1]{0:T(128)}, u32[]{:S(2)}, u32[]{:S(2)}) collective-permute-start(s32[1]{0:T(128)} %param.6), channel_id=1, source_target_pairs={{0,4},{4,8},{8,12},{12,16},{16,20},{20,24},{24,28},{28,32},{32,36}... | collective-permute-start | bytes 20 | tf_op jit(solution)/shard_map/ppermute | solution.py:11
  58.2 3.4 copy-start
  78.4 256.4 %reduce-scatter.2.cloned.1.call-start = ((), (), s32[]{:S(2)}) async-start(), calls=%async_computation.2 | async-start | bytes 5242880 | tf_op jit(solution)/shard_map/reduce_scatter | solution.py:42
  176.7 98.7 %collective-permute-start = (bf16[1024,2048]{1,0:T(8,128)(2,1)S(1)}, bf16[1024,2048]{1,0:T(8,128)(2,1)S(1)}, u32[]{:S(2)}, u32[]{:S(2)}) collective-permute-start(bf16[1024,2048]{1,0:T(8,128)(2,1)S(1)} %fusion.12), channel_id=1, source_target_pairs={{0,4},{4,8},{8,12},{12,16},{16,20},{20,24},{24,28},{28,32},{32,36}... | collective-permute-start | bytes 12582920 | tf_op jit(solution)/shard_map/ppermute | solution.py:11
  275.4 1.9 copy-start.1
  337.7 25.2 %collective-permute-start.2 = (bf16[256,2048]{1,0:T(8,128)(2,1)S(1)}, bf16[256,2048]{1,0:T(8,128)(2,1)S(1)}, u32[]{:S(2)}, u32[]{:S(2)}) collective-permute-start(bf16[256,2048]{1,0:T(8,128)(2,1)S(1)} %get-tuple-element.3), channel_id=1, source_target_pairs={{0,4},{4,0},{8,12},{12,8},{16,20},{20,16},{24,28},{28,24},{32,36},... | collective-permute-start | bytes 3145736 | tf_op jit(solution)/shard_map/ppermute | solution.py:21
  362.9 25.8 %collective-permute-start.3 = (bf16[256,2048]{1,0:T(8,128)(2,1)S(1)}, bf16[256,2048]{1,0:T(8,128)(2,1)S(1)}, u32[]{:S(2)}, u32[]{:S(2)}) collective-permute-start(bf16[256,2048]{1,0:T(8,128)(2,1)S(1)} %collective-permute-done.2), channel_id=1, source_target_pairs={{0,8},{8,0},{4,12},{12,4},{16,24},{24,16},{20,28},{28,20},{32,40},... | collective-permute-start | bytes 3145736 | tf_op jit(solution)/shard_map/ppermute | solution.py:21
  388.7 24.9 %collective-permute-start.4 = (bf16[256,2048]{1,0:T(8,128)(2,1)S(1)}, bf16[256,2048]{1,0:T(8,128)(2,1)S(1)}, u32[]{:S(2)}, u32[]{:S(2)}) collective-permute-start(bf16[256,2048]{1,0:T(8,128)(2,1)S(1)} %collective-permute-done.3), channel_id=1, source_target_pairs={{0,16},{16,0},{4,20},{20,4},{8,24},{24,8},{12,28},{28,12},{32,48},... | collective-permute-start | bytes 3145736 | tf_op jit(solution)/shard_map/ppermute | solution.py:21
  413.6 22.5 %collective-permute-start.5 = (bf16[256,2048]{1,0:T(8,128)(2,1)S(1)}, bf16[256,2048]{1,0:T(8,128)(2,1)S(1)}, u32[]{:S(2)}, u32[]{:S(2)}) collective-permute-start(bf16[256,2048]{1,0:T(8,128)(2,1)S(1)} %collective-permute-done.4), channel_id=1, source_target_pairs={{0,32},{32,0},{4,36},{36,4},{8,40},{40,8},{12,44},{44,12},{16,48},... | collective-permute-start | bytes 3145736 | tf_op jit(solution)/shard_map/ppermute | solution.py:21
  436.1 24.8 %collective-permute-start.6 = (bf16[256,2048]{1,0:T(8,128)(2,1)S(1)}, bf16[256,2048]{1,0:T(8,128)(2,1)S(1)}, u32[]{:S(2)}, u32[]{:S(2)}) collective-permute-start(bf16[256,2048]{1,0:T(8,128)(2,1)S(1)} %collective-permute-done.5), channel_id=1, source_target_pairs={{0,64},{64,0},{4,68},{68,4},{8,72},{72,8},{12,76},{76,12},{16,80},... | collective-permute-start | bytes 3145736 | tf_op jit(solution)/shard_map/ppermute | solution.py:21
Sparse Core Ops, SparseCore 0:
  9.7 48.4 all-gather.2
  78.5 92.7 all-reduce.1
  293.0 41.7 reduce-scatter.1
where the time goes:
time: 469 us; the launch traced here: 468 us
  waiting for transfers between devices  390 us (83%)
  matrix products  31 us (7%)
  starting transfers between devices  15.9 us (3%)
  other arithmetic  15.2 us (3%)
  between operations  15.1 us (3%)
    ppermute x5, waiting for transfers between devices, partner(): return lax.ppermute(block, axis, route)  111 us
    ppermute x2, waiting for transfers between devices, from_behind(): lax.ppermute(x, axis, [(i, (i + by) % devices) for i in range(devices)])  105 us
    psum x1, waiting for transfers between devices, body(): lax.psum(jnp.dot(hidden_one, first_out, preferred_element_type=jnp.float3...  92.9 us
    reduce_scatter x1, waiting for transfers between devices, contract(): lax.psum_scatter(jnp.dot(hidden, w_second, preferred_element_type=jnp.flo...  41.9 us
    all_gather x1, waiting for transfers between devices, body(): whole_rows = lax.all_gather(shard_rows, 'tensor', axis=0, tiled=True)  38 us
    dot_general x1, matrix products, contract(): jnp.dot(hidden, w_second, preferred_element_type=jnp.float32)  15.5 us
    dot_general x1, matrix products, body(): jnp.dot(hidden_one, first_out, preferred_element_type=jnp.float32)  15.5 us
    ppermute x5, starting transfers between devices, partner(): return lax.ppermute(block, axis, route)  12.3 us
  transfers between devices with their start and end apart: 10, of which 10 were waited for; matrix products, arithmetic and copies ran while one was open for 0% of the time, Pallas kernels for 0%

commit v1 on v0

v1 whole, which is shorter than its diff:
```python
import functools

import jax
import jax.numpy as jnp
from jax import lax
from jax.experimental import pallas as pl
from jax.experimental.pallas import tpu as pltpu
from jax.sharding import PartitionSpec as P

eps = 1e-05
AXES = ("section", "tensor")
Y = 4
CHUNKS = (64, 64, 64, 64)
HB = 512
VMEM_LIMIT = 8 * 2**20


def route(x, to):
    sections, tensors = (lax.axis_size(a) for a in AXES)
    pairs = []
    for s in range(sections):
        for t in range(tensors):
            ds, dt = to(s, t, sections)
            pairs.append((s * tensors + t, ds * tensors + dt))
    return lax.ppermute(x, AXES, pairs)


def to_x_neighbour(s, t, n):
    return s, t ^ 2


def to_other_core(s, t, n):
    return s, t ^ 1


def to_next_section(s, t, n):
    return (s + 1) % n, (t ^ 2 if s % Y == Y - 1 else t)


def to_next_plain(s, t, n):
    return (s + 1) % n, t


def to_mirror(s, t, n):
    return n - 1 - s, t ^ 2


def pick_kernel(idx, w_in, w_out, in_sel, out_sel, sems):
    g = idx[0]
    parts = 4
    copies = []
    for k in range(parts):
        a = w_in.shape[2] // parts
        b = w_out.shape[2] // parts
        copies.append(pltpu.make_async_copy(w_in.at[0, g, pl.ds(k * a, a)], in_sel.at[pl.ds(k * a, a)], sems.at[2 * k]))
        copies.append(pltpu.make_async_copy(w_out.at[0, g, pl.ds(k * b, b)], out_sel.at[pl.ds(k * b, b)], sems.at[2 * k + 1]))
    for c in copies:
        c.start()
    for c in copies:
        c.wait()


def in_vmem(x):
    return pltpu.with_memory_space_constraint(x, pltpu.VMEM)


def in_hbm(x):
    return pltpu.with_memory_space_constraint(x, pltpu.HBM)


def pick(group, w_in, w_out):
    hbm = pl.BlockSpec(memory_space=pltpu.HBM)
    vmem = pl.BlockSpec(memory_space=pltpu.VMEM)
    return pl.pallas_call(
        pick_kernel,
        out_shape=(
            pltpu.VMEM(w_in.shape[2:], w_in.dtype),
            pltpu.VMEM(w_out.shape[2:], w_out.dtype),
        ),
        in_specs=[pl.BlockSpec(memory_space=pltpu.SMEM), hbm, hbm],
        out_specs=(vmem, vmem),
        scratch_shapes=[pltpu.SemaphoreType.DMA((8,))],
        compiler_params=pltpu.CompilerParams(vmem_limit_bytes=2**20),
        cost_estimate=pl.CostEstimate(flops=0, bytes_accessed=8 * 2**20, transcendentals=0),
        name="pick_group",
    )(group.reshape(1), in_hbm(w_in), in_hbm(w_out))


def block_kernel(idx, own, par, gain, w_in, w_out, r_in, r_out, *refs):
    give, keep, normed, total = refs[-4:]
    g, swap = idx[0], idx[1]
    rows = own.shape[0]
    per = r_in.shape[1] // HB
    swapped = swap == 1
    gain_row = jnp.where(g == 0, gain[0, 0:1, :], gain[0, 1:2, :]).astype(jnp.float32)
    x_own = own[...].astype(jnp.float32)
    x_par = par[...].astype(jnp.float32)
    x_keep = jnp.where(swapped, x_par, x_own)
    x_give = jnp.where(swapped, x_own, x_par)
    for k, x in enumerate((x_keep, x_give)):
        centred = x - jnp.mean(x, axis=-1, keepdims=True)
        spread = jnp.mean(centred * centred, axis=-1, keepdims=True)
        normed[pl.ds(k * rows, rows), :] = (centred * lax.rsqrt(spread + eps) * gain_row).astype(jnp.bfloat16)
    for b in range(2 * per):
        first, second = (w_in, w_out) if b < per else (r_in, r_out)
        lo = (b % per) * HB
        up = jnp.dot(normed[...], first[:, pl.ds(lo, HB)], preferred_element_type=jnp.float32)
        hidden = jax.nn.gelu(up, approximate=True).astype(jnp.bfloat16)
        part = jnp.dot(hidden, second[pl.ds(lo, HB), :], preferred_element_type=jnp.float32)
        if b == 0:
            total[...] = part
        elif b < 2 * per - 1:
            total[...] += part
        else:
            give[...] = (total[pl.ds(rows, rows), :] + part[rows:]).astype(jnp.bfloat16)
            kept = jnp.where(swapped, par[...].astype(jnp.float32), own[...].astype(jnp.float32))
            keep[...] = kept + (total[pl.ds(0, rows), :] + part[:rows])


def block(idx, own, par, gain, w_in, w_out, r_in, r_out, *behind):
    rows, d = own.shape
    hid = r_in.shape[1]
    vmem = pl.BlockSpec(memory_space=pltpu.VMEM)
    return pl.pallas_call(
        block_kernel,
        out_shape=(
            jax.ShapeDtypeStruct((rows, d), jnp.bfloat16),
            jax.ShapeDtypeStruct((rows, d), jnp.float32),
        ),
        in_specs=[pl.BlockSpec(memory_space=pltpu.SMEM)] + [vmem] * 7 + [pl.BlockSpec(memory_space=pl.ANY)] * len(behind),
        out_specs=(vmem, vmem),
        scratch_shapes=[
            pltpu.VMEM((2 * rows, d), jnp.bfloat16),
            pltpu.VMEM((2 * rows, d), jnp.float32),
        ],
        compiler_params=pltpu.CompilerParams(vmem_limit_bytes=VMEM_LIMIT),
        cost_estimate=pl.CostEstimate(
            flops=2 * 2 * (2 * rows) * d * 2 * hid, bytes_accessed=4 * 2 * hid * d, transcendentals=2 * rows * 2 * hid
        ),
        name="block",
    )(idx, own, par, gain, *(in_vmem(w) for w in (w_in, w_out, r_in, r_out)), *behind)


def join_kernel(keep, got, *refs):
    refs[-1][...] = (keep[...] + got[...].astype(jnp.float32)).astype(jnp.bfloat16)


def join(keep, got, *behind):
    vmem = pl.BlockSpec(memory_space=pltpu.VMEM)
    return pl.pallas_call(
        join_kernel,
        out_shape=jax.ShapeDtypeStruct(got.shape, jnp.bfloat16),
        in_specs=[vmem, vmem] + [pl.BlockSpec(memory_space=pl.ANY)] * len(behind),
        out_specs=vmem,
        compiler_params=pltpu.CompilerParams(vmem_limit_bytes=4 * 2**20),
        cost_estimate=pl.CostEstimate(flops=got.size, bytes_accessed=8 * got.size, transcendentals=0),
        name="join",
    )(keep, got, *behind)


def body(act, group_of, gain, w_in, w_out):
    place = lax.axis_index("section")
    g1 = group_of[0]
    prior = route(group_of, to_next_plain)[0]
    g2 = jnp.where(place == 0, 1, prior).astype(jnp.int32)
    swap = (place % Y == Y - 1).astype(jnp.int32)
    none = jnp.zeros((), jnp.int32)
    starts = [sum(CHUNKS[:k]) for k in range(len(CHUNKS))]

    own1 = [act[0, lo : lo + n] for lo, n in zip(starts, CHUNKS)]
    par1 = [route(x, to_x_neighbour) for x in own1]
    r_in, r_out = route(w_in, to_other_core), route(w_out, to_other_core)
    w1 = pick(g1, w_in, w_out) + pick(g1, r_in, r_out)
    w2 = pick(g2, w_in, w_out) + pick(g2, r_in, r_out)

    idx1, idx2 = jnp.stack([g1, swap, g2]), jnp.stack([g2, none, none])
    last = len(CHUNKS) - 1

    own2 = []
    for k, (x, y) in enumerate(zip(own1, par1)):
        give, keep = block(idx1, x, y, gain, *w1)
        behind = w2 if k == last else ()
        own2.append(route(join(keep, route(give, to_x_neighbour), *behind), to_next_section))

    halves, parked = [], []
    for k, x in enumerate(own2):
        y = route(x, to_x_neighbour)
        parked.append(route(y, to_mirror))
        give, keep = block(idx2, x, y, gain, *w2, *parked[: max(k - 1, 0)][-1:])
        halves.append((keep, route(give, to_x_neighbour)))
    outs = [join(*halves[k], *parked[k + last - 1 :][:1]) for k in range(len(halves))]
    return jnp.concatenate(outs)[None], jnp.concatenate(parked)[None]


def solution(mesh):
    placed = (
        P("section", "tensor", None),
        P("section"),
        P("section", None, None),
        P("section", None, None, "tensor"),
        P("section", None, "tensor", None),
    )
    return jax.shard_map(
        body,
        mesh=mesh,
        in_specs=placed,
        out_specs=(P("section", "tensor", None), P("section", "tensor", None)),
        check_vma=False,
    )
```

time: 469 us -> 125 us (0.27)
  waiting for transfers between devices: 390 us -> 28.9 us
  Pallas kernels: 0 us -> 45.7 us
  matrix products: 31 us -> 0 us
  starting transfers between devices: 15.9 us -> 38.2 us
  other arithmetic: 15.2 us -> 2.2 us
  between operations: 15.1 us -> 2.21 us
  local copies, waits for them, and re-layouts: 1.53 us -> 7.54 us
    ppermute x7 -> x27, waiting for transfers between devices: 216 us -> 28.9 us  [route(): return lax.ppermute(x, AXES, pairs)]
    psum x1 -> x0, waiting for transfers between devices: 92.9 us -> none  [body(): lax.psum(jnp.dot(hidden_one, first_out, preferred_element_type=jnp.float3...]
    pallas_call x0 -> x20, Pallas kernels: none -> 45.7 us  [the longest x8 31.2 us: block(): pl.pallas_call(block_kernel, out_shape=(jax.ShapeDtypeStruct((rows, d), j...]
    reduce_scatter x1 -> x0, waiting for transfers between devices: 41.9 us -> none  [contract(): lax.psum_scatter(jnp.dot(hidden, w_second, preferred_element_type=jnp.flo...]
    all_gather x1 -> x0, waiting for transfers between devices: 38 us -> none  [body(): whole_rows = lax.all_gather(shard_rows, 'tensor', axis=0, tiled=True)]
    dot_general x2 -> x0, matrix products: 31 us -> none  [the longest x1 15.5 us: contract(): jnp.dot(hidden, w_second, preferred_element_type=jnp.float32)]
    ppermute x7 -> x27, starting transfers between devices: 15.8 us -> 38.2 us  [route(): return lax.ppermute(x, AXES, pairs)]
    convert_element_type x2 -> x0, other arithmetic: 6.18 us -> none  [the longest x1 5.39 us: body(): (whole_rows.astype(jnp.float32) + branch).astype(jnp.bfloat16)]
  transfers between devices with their start and end apart: 10 -> 27, of which waited for: 10 -> 9; matrix products, arithmetic and copies ran while one was open for 0% -> 2% of each run, Pallas kernels for 0% -> 37%
where the time goes in v1:
time: 125 us
  Pallas kernels  45.7 us (37%)
  starting transfers between devices  38.2 us (31%)
  waiting for transfers between devices  28.9 us (23%)
  local copies, waits for them, and re-layouts  7.54 us (6%)
  between operations  2.21 us (2%)
  other arithmetic  2.2 us (2%)
    ppermute x27, starting transfers between devices, route(): return lax.ppermute(x, AXES, pairs)  38.2 us
    pallas_call x8, Pallas kernels, block(): pl.pallas_call(block_kernel, out_shape=(jax.ShapeDtypeStruct((rows, d), j...  31.2 us
    ppermute x27, waiting for transfers between devices, route(): return lax.ppermute(x, AXES, pairs)  28.9 us
    pallas_call x4, Pallas kernels, pick(): pl.pallas_call(pick_kernel, out_shape=(pltpu.VMEM(w_in.shape[2:], w_in.dt...  14 us
    unnamed x10, local copies, waits for them, and re-layouts  6.28 us
  transfers between devices with their start and end apart: 27, of which 9 were waited for; matrix products, arithmetic and copies ran while one was open for 2% of the time, Pallas kernels for 37%

profile of v1, /device:TPU:0, one launch (start us, length us, event | category | flops | bytes accessed | tf_op | source)
XLA Modules:
  0.0 124.6 jit_solution(14200403170123247976)
XLA Ops:
  6.9 3.5 %pick_group.4 = (bf16[2048,1024]{1,0:T(8,128)(2,1)S(1)}, bf16[1024,2048]{1,0:T(8,128)(2,1)S(1)}) custom-call(s32[1]{0:T(128)S(6)} %copy.7.idx, bf16[1,2,2048,1024]{3,2,1,0:T(8,128)(2,1)} %w_in.3, bf16[1,2,1024,2048]{3,2,1,0:T(8,128)(2,1)} %w_out.3), custom_call_target="tpu_custom_call" | custom-call | bytes 8388608 | tf_op jit(solution)/shard_map/pick_group/pallas_call | solution.py:74
  12.4 2.0 %copy-done.2 = bf16[1024,2048]{1,0:T(8,128)(2,1)} copy-done((bf16[1024,2048]{1,0:T(8,128)(2,1)}, bf16[1024,2048]{1,0:T(8,128)(2,1)S(1)}, u32[]{:S(2)}) %copy-start.2) | copy-done | bytes 4194328
  14.4 5.5 %collective-permute-done = s32[1]{0:T(128)} collective-permute-done((s32[1]{0:T(128)}, s32[1]{0:T(128)}, u32[]{:S(2)}, u32[]{:S(2)}) %collective-permute-start) | collective-permute-done | bytes 36 | tf_op jit(solution)/shard_map/ppermute | solution.py:25
  22.7 3.5 %collective-permute-done.3.w_out = bf16[1,2,1024,2048]{3,2,1,0:T(8,128)(2,1)} collective-permute-done((bf16[1,2,1024,2048]{3,2,1,0:T(8,128)(2,1)}, bf16[1,2,1024,2048]{3,2,1,0:T(8,128)(2,1)}, u32[]{:S(2)}, u32[]{:S(2)}) %collective-permute-start.3) | collective-permute-done | bytes 8388640 | tf_op jit(solution)/shard_map/ppermute | solution.py:25
  26.2 3.6 %pick_group.5 = (bf16[2048,1024]{1,0:T(8,128)(2,1)S(1)}, bf16[1024,2048]{1,0:T(8,128)(2,1)S(1)}) custom-call(s32[1]{0:T(128)S(6)} %copy.7.idx, bf16[1,2,2048,1024]{3,2,1,0:T(8,128)(2,1)} %collective-permute-done.2.w_in, bf16[1,2,1024,2048]{3,2,1,0:T(8,128)(2,1)} %collective-permute-done.3.w_out), custom_call_target="tpu_custom_call" | custom-call | bytes 8388608 | tf_op jit(solution)/shard_map/pick_group/pallas_call | solution.py:74
  32.1 3.9 %block.8 = (bf16[64,2048]{1,0:T(8,128)(2,1)S(1)}, f32[64,2048]{1,0:T(8,128)S(1)}) custom-call(s32[3]{0:T(128)S(1)} %pad_add_fusion.idx, bf16[64,2048]{1,0:T(8,128)(2,1)S(1)} %get-tuple-element.50.own, bf16[64,2048]{1,0:T(8,128)(2,1)S(1)} %collective-permute-done.1.par, bf16[1,2,2048]{2,1,0:T(2,128)(2,1)S(1)} %copy-done.4, bf16[2048,1024]{1,0:T(8,128)(2,1)S(1)} %copy-done.1, ...), custom_call_target="tpu_custom_call" | custom-call | flops 2147483648 | bytes 16777216 | tf_op jit(solution)/shard_map/block/pallas_call | solution.py:124
  37.7 3.9 %block.10 = (bf16[64,2048]{1,0:T(8,128)(2,1)S(1)}, f32[64,2048]{1,0:T(8,128)S(1)}) custom-call(s32[3]{0:T(128)S(1)} %pad_add_fusion.idx, bf16[64,2048]{1,0:T(8,128)(2,1)S(1)} %get-tuple-element.51.own, bf16[64,2048]{1,0:T(8,128)(2,1)S(1)} %collective-permute-done.8.par, bf16[1,2,2048]{2,1,0:T(2,128)(2,1)S(1)} %copy-done.4, bf16[2048,1024]{1,0:T(8,128)(2,1)S(1)} %copy-done.1, ...), custom_call_target="tpu_custom_call" | custom-call | flops 2147483648 | bytes 16777216 | tf_op jit(solution)/shard_map/block/pallas_call | solution.py:124
  42.1 3.9 %block.11 = (bf16[64,2048]{1,0:T(8,128)(2,1)S(1)}, f32[64,2048]{1,0:T(8,128)S(1)}) custom-call(s32[3]{0:T(128)S(1)} %pad_add_fusion.idx, bf16[64,2048]{1,0:T(8,128)(2,1)S(1)} %get-tuple-element.53.own, bf16[64,2048]{1,0:T(8,128)(2,1)S(1)} %collective-permute-done.13.par, bf16[1,2,2048]{2,1,0:T(2,128)(2,1)S(1)} %copy-done.4, ...), custom_call_target="tpu_custom_call" | custom-call | flops 2147483648 | bytes 16777216 | tf_op jit(solution)/shard_map/block/pallas_call | solution.py:124
  47.9 3.9 %block.13 = (bf16[64,2048]{1,0:T(8,128)(2,1)S(1)}, f32[64,2048]{1,0:T(8,128)S(1)}) custom-call(s32[3]{0:T(128)S(1)} %pad_add_fusion.idx, bf16[64,2048]{1,0:T(8,128)(2,1)S(1)} %get-tuple-element.52.own, bf16[64,2048]{1,0:T(8,128)(2,1)S(1)} %collective-permute-done.18.par, bf16[1,2,2048]{2,1,0:T(2,128)(2,1)S(1)} %copy-done.4, ...), custom_call_target="tpu_custom_call" | custom-call | flops 2147483648 | bytes 16777216 | tf_op jit(solution)/shard_map/block/pallas_call | solution.py:124
  54.1 2.4 %collective-permute-done.14.got = bf16[64,2048]{1,0:T(8,128)(2,1)S(1)} collective-permute-done((bf16[64,2048]{1,0:T(8,128)(2,1)S(1)}, bf16[64,2048]{1,0:T(8,128)(2,1)S(1)}, u32[]{:S(2)}, u32[]{:S(2)}) %collective-permute-start.14) | collective-permute-done | bytes 262176 | tf_op jit(solution)/shard_map/ppermute | solution.py:25
  58.2 3.5 %pick_group.6 = (bf16[2048,1024]{1,0:T(8,128)(2,1)S(1)}, bf16[1024,2048]{1,0:T(8,128)(2,1)S(1)}) custom-call(s32[1]{0:T(128)} %bitcast.1.idx, bf16[1,2,2048,1024]{3,2,1,0:T(8,128)(2,1)} %w_in.3, bf16[1,2,1024,2048]{3,2,1,0:T(8,128)(2,1)} %w_out.3), custom_call_target="tpu_custom_call" | custom-call | bytes 8388608 | tf_op jit(solution)/shard_map/pick_group/pallas_call | solution.py:74
  61.7 3.5 %pick_group.7 = (bf16[2048,1024]{1,0:T(8,128)(2,1)S(1)}, bf16[1024,2048]{1,0:T(8,128)(2,1)S(1)}) custom-call(s32[1]{0:T(128)} %bitcast.1.idx, bf16[1,2,2048,1024]{3,2,1,0:T(8,128)(2,1)} %collective-permute-done.2.w_in, bf16[1,2,1024,2048]{3,2,1,0:T(8,128)(2,1)} %collective-permute-done.3.w_out), custom_call_target="tpu_custom_call" | custom-call | bytes 8388608 | tf_op jit(solution)/shard_map/pick_group/pallas_call | solution.py:74
  69.9 2.7 %collective-permute-done.15.own = bf16[64,2048]{1,0:T(8,128)(2,1)S(1)} collective-permute-done((bf16[64,2048]{1,0:T(8,128)(2,1)S(1)}, bf16[64,2048]{1,0:T(8,128)(2,1)S(1)}, u32[]{:S(2)}, u32[]{:S(2)}) %collective-permute-start.15) | collective-permute-done | bytes 262176 | tf_op jit(solution)/shard_map/ppermute | solution.py:25
  72.7 7.3 %collective-permute-done.10.own = bf16[64,2048]{1,0:T(8,128)(2,1)S(1)} collective-permute-done((bf16[64,2048]{1,0:T(8,128)(2,1)S(1)}, bf16[64,2048]{1,0:T(8,128)(2,1)S(1)}, u32[]{:S(2)}, u32[]{:S(2)}) %collective-permute-start.10) | collective-permute-done | bytes 262176 | tf_op jit(solution)/shard_map/ppermute | solution.py:25
  80.3 3.2 %collective-permute-done.20.own = bf16[64,2048]{1,0:T(8,128)(2,1)S(1)} collective-permute-done((bf16[64,2048]{1,0:T(8,128)(2,1)S(1)}, bf16[64,2048]{1,0:T(8,128)(2,1)S(1)}, u32[]{:S(2)}, u32[]{:S(2)}) %collective-permute-start.20) | collective-permute-done | bytes 262176 | tf_op jit(solution)/shard_map/ppermute | solution.py:25
  83.7 2.3 %collective-permute-start.23 = (bf16[64,2048]{1,0:T(8,128)(2,1)S(1)}, bf16[64,2048]{1,0:T(8,128)(2,1)S(1)}, u32[]{:S(2)}, u32[]{:S(2)}) collective-permute-start(bf16[64,2048]{1,0:T(8,128)(2,1)S(1)} %collective-permute-done.6.par), channel_id=1, source_target_pairs={{0,126},{1,127},{2,124},{3,125},{4,122},{5,123},{6,120},{7,121},{8... | collective-permute-start | bytes 786440 | tf_op jit(solution)/shard_map/ppermute | solution.py:25
  86.1 3.9 %block.9 = (bf16[64,2048]{1,0:T(8,128)(2,1)S(1)}, f32[64,2048]{1,0:T(8,128)S(1)}) custom-call(s32[3]{0:T(128)S(1)} %stack.17.idx, bf16[64,2048]{1,0:T(8,128)(2,1)S(1)} %collective-permute-done.5.own, bf16[64,2048]{1,0:T(8,128)(2,1)S(1)} %collective-permute-done.6.par, bf16[1,2,2048]{2,1,0:T(2,128)(2,1)S(1)} %copy-done.4, ...), custom_call_target="tpu_custom_call" | custom-call | flops 2147483648 | bytes 16777216 | tf_op jit(solution)/shard_map/block/pallas_call | solution.py:124
  90.7 5.7 %collective-permute-start.25 = (bf16[64,2048]{1,0:T(8,128)(2,1)S(1)}, bf16[64,2048]{1,0:T(8,128)(2,1)S(1)}, u32[]{:S(2)}, u32[]{:S(2)}) collective-permute-start(bf16[64,2048]{1,0:T(8,128)(2,1)S(1)} %collective-permute-done.16.par), channel_id=1, source_target_pairs={{0,126},{1,127},{2,124},{3,125},{4,122},{5,123},{6,120},{7,121},{8... | collective-permute-start | bytes 786440 | tf_op jit(solution)/shard_map/ppermute | solution.py:25
  96.4 3.9 %block.12 = (bf16[64,2048]{1,0:T(8,128)(2,1)S(1)}, f32[64,2048]{1,0:T(8,128)S(1)}) custom-call(s32[3]{0:T(128)S(1)} %stack.17.idx, bf16[64,2048]{1,0:T(8,128)(2,1)S(1)} %collective-permute-done.15.own, bf16[64,2048]{1,0:T(8,128)(2,1)S(1)} %collective-permute-done.16.par, bf16[1,2,2048]{2,1,0:T(2,128)(2,1)S(1)} %copy-done.4, ...), custom_call_target="tpu_custom_call" | custom-call | flops 2147483648 | bytes 16777216 | tf_op jit(solution)/shard_map/block/pallas_call | solution.py:124
  100.6 2.3 %collective-permute-start.12 = (bf16[64,2048]{1,0:T(8,128)(2,1)S(1)}, bf16[64,2048]{1,0:T(8,128)(2,1)S(1)}, u32[]{:S(2)}, u32[]{:S(2)}) collective-permute-start(bf16[64,2048]{1,0:T(8,128)(2,1)S(1)} %collective-permute-done.11.par), channel_id=1, source_target_pairs={{0,126},{1,127},{2,124},{3,125},{4,122},{5,123},{6,120},{7,121},{8... | collective-permute-start | bytes 786440 | tf_op jit(solution)/shard_map/ppermute | solution.py:25
  102.9 5.1 %collective-permute-start.22 = (bf16[64,2048]{1,0:T(8,128)(2,1)S(1)}, bf16[64,2048]{1,0:T(8,128)(2,1)S(1)}, u32[]{:S(2)}, u32[]{:S(2)}) collective-permute-start(bf16[64,2048]{1,0:T(8,128)(2,1)S(1)} %collective-permute-done.21.par), channel_id=1, source_target_pairs={{0,126},{1,127},{2,124},{3,125},{4,122},{5,123},{6,120},{7,121},{8... | collective-permute-start | bytes 786440 | tf_op jit(solution)/shard_map/ppermute | solution.py:25
  108.1 3.9 %block.14 = (bf16[64,2048]{1,0:T(8,128)(2,1)S(1)}, f32[64,2048]{1,0:T(8,128)S(1)}) custom-call(s32[3]{0:T(128)S(1)} %stack.17.idx, bf16[64,2048]{1,0:T(8,128)(2,1)S(1)} %collective-permute-done.10.own, bf16[64,2048]{1,0:T(8,128)(2,1)S(1)} %collective-permute-done.11.par, bf16[1,2,2048]{2,1,0:T(2,128)(2,1)S(1)} %copy-done.4, ...), custom_call_target="tpu_custom_call" | custom-call | flops 2147483648 | bytes 16777216 | tf_op jit(solution)/shard_map/block/pallas_call | solution.py:124
  112.7 3.9 %block.15 = (bf16[64,2048]{1,0:T(8,128)(2,1)S(1)}, f32[64,2048]{1,0:T(8,128)S(1)}) custom-call(s32[3]{0:T(128)S(1)} %stack.17.idx, bf16[64,2048]{1,0:T(8,128)(2,1)S(1)} %collective-permute-done.20.own, bf16[64,2048]{1,0:T(8,128)(2,1)S(1)} %collective-permute-done.21.par, bf16[1,2,2048]{2,1,0:T(2,128)(2,1)S(1)} %copy-done.4, ...), custom_call_target="tpu_custom_call" | custom-call | flops 2147483648 | bytes 16777216 | tf_op jit(solution)/shard_map/block/pallas_call | solution.py:124
  120.8 2.8 %collective-permute-done.26.got = bf16[64,2048]{1,0:T(8,128)(2,1)S(1)} collective-permute-done((bf16[64,2048]{1,0:T(8,128)(2,1)S(1)}, bf16[64,2048]{1,0:T(8,128)(2,1)S(1)}, u32[]{:S(2)}, u32[]{:S(2)}) %collective-permute-start.26) | collective-permute-done | bytes 262176 | tf_op jit(solution)/shard_map/ppermute | solution.py:25
  (65 shorter events, 32.4 us)
Async XLA Ops:
  0.6 20.2 %collective-permute-start.2 = (bf16[1,2,2048,1024]{3,2,1,0:T(8,128)(2,1)}, bf16[1,2,2048,1024]{3,2,1,0:T(8,128)(2,1)}, u32[]{:S(2)}, u32[]{:S(2)}) collective-permute-start(bf16[1,2,2048,1024]{3,2,1,0:T(8,128)(2,1)} %w_in.3), channel_id=1, source_target_pairs={{0,1},{1,0},{2,3},{3,2},{4,5},{5,4},{6,7},{7,6},{8,9},{9,8},{10,11... | collective-permute-start | bytes 25165832 | tf_op jit(solution)/shard_map/ppermute | solution.py:25
  0.7 25.5 %collective-permute-start.3 = (bf16[1,2,1024,2048]{3,2,1,0:T(8,128)(2,1)}, bf16[1,2,1024,2048]{3,2,1,0:T(8,128)(2,1)}, u32[]{:S(2)}, u32[]{:S(2)}) collective-permute-start(bf16[1,2,1024,2048]{3,2,1,0:T(8,128)(2,1)} %w_out.3), channel_id=1, source_target_pairs={{0,1},{1,0},{2,3},{3,2},{4,5},{5,4},{6,7},{7,6},{8,9},{9,8},{10,11... | collective-permute-start | bytes 25165832 | tf_op jit(solution)/shard_map/ppermute | solution.py:25
  2.5 27.4 %collective-permute-start.1 = (bf16[64,2048]{1,0:T(8,128)(2,1)S(1)}, bf16[64,2048]{1,0:T(8,128)(2,1)S(1)}, u32[]{:S(2)}, u32[]{:S(2)}) collective-permute-start(bf16[64,2048]{1,0:T(8,128)(2,1)S(1)} %get-tuple-element.50.own), channel_id=1, source_target_pairs={{0,2},{1,3},{2,0},{3,1},{4,6},{5,7},{6,4},{7,5},{8,10},{9,11},{10,... | collective-permute-start | bytes 786440 | tf_op jit(solution)/shard_map/ppermute | solution.py:25
  4.1 15.7 %collective-permute-start = (s32[1]{0:T(128)}, s32[1]{0:T(128)}, u32[]{:S(2)}, u32[]{:S(2)}) collective-permute-start(s32[1]{0:T(128)} %param.6), channel_id=1, source_target_pairs={{0,4},{1,5},{2,6},{3,7},{4,8},{5,9},{6,10},{7,11},{8,12},{9,13},{1... | collective-permute-start | bytes 20 | tf_op jit(solution)/shard_map/ppermute | solution.py:25
  5.7 32.0 %collective-permute-start.8 = (bf16[64,2048]{1,0:T(8,128)(2,1)S(1)}, bf16[64,2048]{1,0:T(8,128)(2,1)S(1)}, u32[]{:S(2)}, u32[]{:S(2)}) collective-permute-start(bf16[64,2048]{1,0:T(8,128)(2,1)S(1)} %get-tuple-element.51.own), channel_id=1, source_target_pairs={{0,2},{1,3},{2,0},{3,1},{4,6},{5,7},{6,4},{7,5},{8,10},{9,11},{10,... | collective-permute-start | bytes 786440 | tf_op jit(solution)/shard_map/ppermute | solution.py:25
  19.9 22.3 %collective-permute-start.13 = (bf16[64,2048]{1,0:T(8,128)(2,1)S(1)}, bf16[64,2048]{1,0:T(8,128)(2,1)S(1)}, u32[]{:S(2)}, u32[]{:S(2)}) collective-permute-start(bf16[64,2048]{1,0:T(8,128)(2,1)S(1)} %get-tuple-element.53.own), channel_id=1, source_target_pairs={{0,2},{1,3},{2,0},{3,1},{4,6},{5,7},{6,4},{7,5},{8,10},{9,11},{10,... | collective-permute-start | bytes 786440 | tf_op jit(solution)/shard_map/ppermute | solution.py:25
  20.9 27.0 %collective-permute-start.18 = (bf16[64,2048]{1,0:T(8,128)(2,1)S(1)}, bf16[64,2048]{1,0:T(8,128)(2,1)S(1)}, u32[]{:S(2)}, u32[]{:S(2)}) collective-permute-start(bf16[64,2048]{1,0:T(8,128)(2,1)S(1)} %get-tuple-element.52.own), channel_id=1, source_target_pairs={{0,2},{1,3},{2,0},{3,1},{4,6},{5,7},{6,4},{7,5},{8,10},{9,11},{10,... | collective-permute-start | bytes 786440 | tf_op jit(solution)/shard_map/ppermute | solution.py:25
  36.0 16.3 %collective-permute-start.4 = (bf16[64,2048]{1,0:T(8,128)(2,1)S(1)}, bf16[64,2048]{1,0:T(8,128)(2,1)S(1)}, u32[]{:S(2)}, u32[]{:S(2)}) collective-permute-start(bf16[64,2048]{1,0:T(8,128)(2,1)S(1)} %get-tuple-element.31), channel_id=1, source_target_pairs={{0,2},{1,3},{2,0},{3,1},{4,6},{5,7},{6,4},{7,5},{8,10},{9,11},{10,... | collective-permute-start | bytes 786440 | tf_op jit(solution)/shard_map/ppermute | solution.py:25
  41.6 23.6 %collective-permute-start.9 = (bf16[64,2048]{1,0:T(8,128)(2,1)S(1)}, bf16[64,2048]{1,0:T(8,128)(2,1)S(1)}, u32[]{:S(2)}, u32[]{:S(2)}) collective-permute-start(bf16[64,2048]{1,0:T(8,128)(2,1)S(1)} %get-tuple-element.39), channel_id=1, source_target_pairs={{0,2},{1,3},{2,0},{3,1},{4,6},{5,7},{6,4},{7,5},{8,10},{9,11},{10,... | collective-permute-start | bytes 786440 | tf_op jit(solution)/shard_map/ppermute | solution.py:25
  51.8 15.1 %collective-permute-start.19 = (bf16[64,2048]{1,0:T(8,128)(2,1)S(1)}, bf16[64,2048]{1,0:T(8,128)(2,1)S(1)}, u32[]{:S(2)}, u32[]{:S(2)}) collective-permute-start(bf16[64,2048]{1,0:T(8,128)(2,1)S(1)} %get-tuple-element.45), channel_id=1, source_target_pairs={{0,2},{1,3},{2,0},{3,1},{4,6},{5,7},{6,4},{7,5},{8,10},{9,11},{10,... | collective-permute-start | bytes 786440 | tf_op jit(solution)/shard_map/ppermute | solution.py:25
  52.3 16.0 %collective-permute-start.5 = (bf16[64,2048]{1,0:T(8,128)(2,1)S(1)}, bf16[64,2048]{1,0:T(8,128)(2,1)S(1)}, u32[]{:S(2)}, u32[]{:S(2)}) collective-permute-start(bf16[64,2048]{1,0:T(8,128)(2,1)S(1)} %join.8), channel_id=1, source_target_pairs={{0,4},{1,5},{2,6},{3,7},{4,8},{5,9},{6,10},{7,11},{8,12},{9,13},{1... | collective-permute-start | bytes 786440 | tf_op jit(solution)/shard_map/ppermute | solution.py:25
  56.5 16.1 %collective-permute-start.15 = (bf16[64,2048]{1,0:T(8,128)(2,1)S(1)}, bf16[64,2048]{1,0:T(8,128)(2,1)S(1)}, u32[]{:S(2)}, u32[]{:S(2)}) collective-permute-start(bf16[64,2048]{1,0:T(8,128)(2,1)S(1)} %join.11), channel_id=1, source_target_pairs={{0,4},{1,5},{2,6},{3,7},{4,8},{5,9},{6,10},{7,11},{8,12},{9,13},{1... | collective-permute-start | bytes 786440 | tf_op jit(solution)/shard_map/ppermute | solution.py:25
  65.2 14.7 %collective-permute-start.10 = (bf16[64,2048]{1,0:T(8,128)(2,1)S(1)}, bf16[64,2048]{1,0:T(8,128)(2,1)S(1)}, u32[]{:S(2)}, u32[]{:S(2)}) collective-permute-start(bf16[64,2048]{1,0:T(8,128)(2,1)S(1)} %join.9), channel_id=1, source_target_pairs={{0,4},{1,5},{2,6},{3,7},{4,8},{5,9},{6,10},{7,11},{8,12},{9,13},{1... | collective-permute-start | bytes 786440 | tf_op jit(solution)/shard_map/ppermute | solution.py:25
  66.9 16.6 %collective-permute-start.20 = (bf16[64,2048]{1,0:T(8,128)(2,1)S(1)}, bf16[64,2048]{1,0:T(8,128)(2,1)S(1)}, u32[]{:S(2)}, u32[]{:S(2)}) collective-permute-start(bf16[64,2048]{1,0:T(8,128)(2,1)S(1)} %join.12), channel_id=1, source_target_pairs={{0,4},{1,5},{2,6},{3,7},{4,8},{5,9},{6,10},{7,11},{8,12},{9,13},{1... | collective-permute-start | bytes 786440 | tf_op jit(solution)/shard_map/ppermute | solution.py:25
  68.4 15.3 %collective-permute-start.6 = (bf16[64,2048]{1,0:T(8,128)(2,1)S(1)}, bf16[64,2048]{1,0:T(8,128)(2,1)S(1)}, u32[]{:S(2)}, u32[]{:S(2)}) collective-permute-start(bf16[64,2048]{1,0:T(8,128)(2,1)S(1)} %collective-permute-done.5.own), channel_id=1, source_target_pairs={{0,2},{1,3},{2,0},{3,1},{4,6},{5,7},{6,4},{7,5},{8,10},{9,11},{10,... | collective-permute-start | bytes 786440 | tf_op jit(solution)/shard_map/ppermute | solution.py:25
  72.6 18.1 %collective-permute-start.16 = (bf16[64,2048]{1,0:T(8,128)(2,1)S(1)}, bf16[64,2048]{1,0:T(8,128)(2,1)S(1)}, u32[]{:S(2)}, u32[]{:S(2)}) collective-permute-start(bf16[64,2048]{1,0:T(8,128)(2,1)S(1)} %collective-permute-done.15.own), channel_id=1, source_target_pairs={{0,2},{1,3},{2,0},{3,1},{4,6},{5,7},{6,4},{7,5},{8,10},{9,11},{10,... | collective-permute-start | bytes 786440 | tf_op jit(solution)/shard_map/ppermute | solution.py:25
  80.0 20.3 %collective-permute-start.11 = (bf16[64,2048]{1,0:T(8,128)(2,1)S(1)}, bf16[64,2048]{1,0:T(8,128)(2,1)S(1)}, u32[]{:S(2)}, u32[]{:S(2)}) collective-permute-start(bf16[64,2048]{1,0:T(8,128)(2,1)S(1)} %collective-permute-done.10.own), channel_id=1, source_target_pairs={{0,2},{1,3},{2,0},{3,1},{4,6},{5,7},{6,4},{7,5},{8,10},{9,11},{10,... | collective-permute-start | bytes 786440 | tf_op jit(solution)/shard_map/ppermute | solution.py:25
  83.5 17.1 %collective-permute-start.21 = (bf16[64,2048]{1,0:T(8,128)(2,1)S(1)}, bf16[64,2048]{1,0:T(8,128)(2,1)S(1)}, u32[]{:S(2)}, u32[]{:S(2)}) collective-permute-start(bf16[64,2048]{1,0:T(8,128)(2,1)S(1)} %collective-permute-done.20.own), channel_id=1, source_target_pairs={{0,2},{1,3},{2,0},{3,1},{4,6},{5,7},{6,4},{7,5},{8,10},{9,11},{10,... | collective-permute-start | bytes 786440 | tf_op jit(solution)/shard_map/ppermute | solution.py:25
  83.7 19.2 %collective-permute-start.23 = (bf16[64,2048]{1,0:T(8,128)(2,1)S(1)}, bf16[64,2048]{1,0:T(8,128)(2,1)S(1)}, u32[]{:S(2)}, u32[]{:S(2)}) collective-permute-start(bf16[64,2048]{1,0:T(8,128)(2,1)S(1)} %collective-permute-done.6.par), channel_id=1, source_target_pairs={{0,126},{1,127},{2,124},{3,125},{4,122},{5,123},{6,120},{7,121},{8... | collective-permute-start | bytes 786440 | tf_op jit(solution)/shard_map/ppermute | solution.py:25
  90.0 28.1 %collective-permute-start.7 = (bf16[64,2048]{1,0:T(8,128)(2,1)S(1)}, bf16[64,2048]{1,0:T(8,128)(2,1)S(1)}, u32[]{:S(2)}, u32[]{:S(2)}) collective-permute-start(bf16[64,2048]{1,0:T(8,128)(2,1)S(1)} %get-tuple-element.37), channel_id=1, source_target_pairs={{0,2},{1,3},{2,0},{3,1},{4,6},{5,7},{6,4},{7,5},{8,10},{9,11},{10,... | collective-permute-start | bytes 786440 | tf_op jit(solution)/shard_map/ppermute | solution.py:25
  90.7 21.3 %collective-permute-start.25 = (bf16[64,2048]{1,0:T(8,128)(2,1)S(1)}, bf16[64,2048]{1,0:T(8,128)(2,1)S(1)}, u32[]{:S(2)}, u32[]{:S(2)}) collective-permute-start(bf16[64,2048]{1,0:T(8,128)(2,1)S(1)} %collective-permute-done.16.par), channel_id=1, source_target_pairs={{0,126},{1,127},{2,124},{3,125},{4,122},{5,123},{6,120},{7,121},{8... | collective-permute-start | bytes 786440 | tf_op jit(solution)/shard_map/ppermute | solution.py:25
  100.3 17.9 %collective-permute-start.17 = (bf16[64,2048]{1,0:T(8,128)(2,1)S(1)}, bf16[64,2048]{1,0:T(8,128)(2,1)S(1)}, u32[]{:S(2)}, u32[]{:S(2)}) collective-permute-start(bf16[64,2048]{1,0:T(8,128)(2,1)S(1)} %get-tuple-element.43), channel_id=1, source_target_pairs={{0,2},{1,3},{2,0},{3,1},{4,6},{5,7},{6,4},{7,5},{8,10},{9,11},{10,... | collective-permute-start | bytes 786440 | tf_op jit(solution)/shard_map/ppermute | solution.py:25
  100.6 16.0 %collective-permute-start.12 = (bf16[64,2048]{1,0:T(8,128)(2,1)S(1)}, bf16[64,2048]{1,0:T(8,128)(2,1)S(1)}, u32[]{:S(2)}, u32[]{:S(2)}) collective-permute-start(bf16[64,2048]{1,0:T(8,128)(2,1)S(1)} %collective-permute-done.11.par), channel_id=1, source_target_pairs={{0,126},{1,127},{2,124},{3,125},{4,122},{5,123},{6,120},{7,121},{8... | collective-permute-start | bytes 786440 | tf_op jit(solution)/shard_map/ppermute | solution.py:25
  102.9 15.2 %collective-permute-start.22 = (bf16[64,2048]{1,0:T(8,128)(2,1)S(1)}, bf16[64,2048]{1,0:T(8,128)(2,1)S(1)}, u32[]{:S(2)}, u32[]{:S(2)}) collective-permute-start(bf16[64,2048]{1,0:T(8,128)(2,1)S(1)} %collective-permute-done.21.par), channel_id=1, source_target_pairs={{0,126},{1,127},{2,124},{3,125},{4,122},{5,123},{6,120},{7,121},{8... | collective-permute-start | bytes 786440 | tf_op jit(solution)/shard_map/ppermute | solution.py:25
  (8 other events, 49.7 us)

commit v2 on v0

v2 whole, which is shorter than its diff:
```python
import functools

import jax
import jax.numpy as jnp
from jax import lax
from jax.experimental import pallas as pl
from jax.experimental.pallas import tpu as pltpu
from jax.sharding import PartitionSpec as P

eps = 1e-05
AXES = ("section", "tensor")
Y = 4
HB = 512
MIB = 2**20
ROWS = 64


def route(x, to):
    sections, tensors = (lax.axis_size(a) for a in AXES)
    pairs = []
    for s in range(sections):
        for t in range(tensors):
            ds, dt = to(s, t, sections)
            pairs.append((s * tensors + t, ds * tensors + dt))
    return lax.ppermute(x, AXES, pairs)


def to_x_neighbour(s, t, n):
    return s, t ^ 2


def to_other_core(s, t, n):
    return s, t ^ 1


def to_next_section(s, t, n):
    return (s + 1) % n, (t ^ 2 if s % Y == Y - 1 else t)


def to_mirror(s, t, n):
    return n - 1 - s, t ^ 2


def in_vmem(x):
    return pltpu.with_memory_space_constraint(x, pltpu.VMEM)


def in_hbm(x):
    return pltpu.with_memory_space_constraint(x, pltpu.HBM)


class Order:
    def __init__(self):
        self.token = jnp.zeros((8, 128), jnp.float32)

    def call(self, kernel, name, outs, specs, args, scratch=(), vmem=4 * MIB, us=0.1, behind=()):
        vmem_spec = pl.BlockSpec(memory_space=pltpu.VMEM)

        def with_token(*refs):
            ins = refs[: len(args)]
            rest = refs[len(args) + 1 + len(behind) :]
            rest[len(outs)][...] = jnp.zeros((8, 128), jnp.float32)
            kernel(*ins, *rest[: len(outs)], *rest[len(outs) + 1 :])

        *results, self.token = pl.pallas_call(
            with_token,
            out_shape=tuple(outs) + (jax.ShapeDtypeStruct((8, 128), jnp.float32),),
            in_specs=list(specs) + [pl.BlockSpec(memory_space=pl.ANY)] * (1 + len(behind)),
            out_specs=(vmem_spec,) * (len(outs) + 1),
            scratch_shapes=list(scratch),
            compiler_params=pltpu.CompilerParams(vmem_limit_bytes=vmem),
            cost_estimate=pl.CostEstimate(flops=int(us * 1.15e9), bytes_accessed=2**14, transcendentals=0),
            name=name,
        )(*args, self.token, *behind)
        return results


SMEM_SPEC = pl.BlockSpec(memory_space=pltpu.SMEM)
VMEM_SPEC = pl.BlockSpec(memory_space=pltpu.VMEM)
HBM_SPEC = pl.BlockSpec(memory_space=pltpu.HBM)


def pick_kernel(groups, count, idx, *refs):
    ws, outs, sems = refs[:count], refs[count : (1 + groups) * count], refs[(1 + groups) * count]
    loads = []
    for j in range(groups):
        for n in range(count):
            for k in range(4):
                size = ws[n].shape[2] // 4
                piece = pl.ds(k * size, size)
                held = outs[j * count + n]
                loads.append(pltpu.make_async_copy(ws[n].at[0, idx[j], piece], held.at[piece], sems.at[len(loads)]))
    for load in loads:
        load.start()
    for load in loads:
        load.wait()


def pick(order, groups, ws, behind=()):
    n = len(ws)
    held = order.call(
        functools.partial(pick_kernel, len(groups), n),
        "pick_group",
        [pltpu.VMEM(w.shape[2:], w.dtype) for w in ws] * len(groups),
        [SMEM_SPEC] + [HBM_SPEC] * n,
        (jnp.stack(groups), *(in_hbm(w) for w in ws)),
        [pltpu.SemaphoreType.DMA((4 * n * len(groups),))],
        us=1.7 * n * len(groups),
        behind=behind,
    )
    return [held[j * n : (j + 1) * n] for j in range(len(groups))]


def normalize(x, gain_row):
    centred = x - jnp.mean(x, axis=-1, keepdims=True)
    spread = jnp.mean(centred * centred, axis=-1, keepdims=True)
    return (centred * lax.rsqrt(spread + eps) * gain_row).astype(jnp.bfloat16)


def up(normed, w):
    return jax.nn.gelu(jnp.dot(normed, w, preferred_element_type=jnp.float32), approximate=True).astype(jnp.bfloat16)


def prepare(idx, own, par, gain, normed):
    rows = own.shape[0]
    swapped = idx[1] == 1
    gain_row = jnp.where(idx[0] == 0, gain[0, 0:1, :], gain[0, 1:2, :]).astype(jnp.float32)
    x_own = own[...].astype(jnp.float32)
    x_par = par[...].astype(jnp.float32)
    normed[pl.ds(0, rows), :] = normalize(jnp.where(swapped, x_par, x_own), gain_row)
    normed[pl.ds(rows, rows), :] = normalize(jnp.where(swapped, x_own, x_par), gain_row)


def kept_rows(idx, own, par):
    return jnp.where(idx[1] == 1, par[...].astype(jnp.float32), own[...].astype(jnp.float32))


def window(ref, lo, rows):
    return ref.at[pl.ds(lo, rows)]


def block_kernel(own_lo, par_lo, idx, own, par, gain, w_in, w_out, r_in, r_out, give, keep, normed, total):
    rows = give.shape[0]
    own, par = window(own, own_lo, rows), window(par, par_lo, rows)
    prepare(idx, own, par, gain, normed)
    per = r_in.shape[1] // HB
    for b in range(2 * per):
        first, second = (w_in, w_out) if b < per else (r_in, r_out)
        piece = pl.ds((b % per) * HB, HB)
        part = jnp.dot(up(normed[...], first[:, piece]), second[piece, :], preferred_element_type=jnp.float32)
        if b == 0:
            total[...] = part
        elif b < 2 * per - 1:
            total[...] += part
        else:
            give[...] = (total[pl.ds(rows, rows), :] + part[rows:]).astype(jnp.bfloat16)
            keep[...] = kept_rows(idx, own, par) + (total[pl.ds(0, rows), :] + part[:rows])


def block(order, idx, own, par, gain, ws, own_lo=0, par_lo=0, behind=()):
    d = own.shape[1]
    return order.call(
        functools.partial(block_kernel, own_lo, par_lo),
        "block",
        [jax.ShapeDtypeStruct((ROWS, d), jnp.bfloat16), jax.ShapeDtypeStruct((ROWS, d), jnp.float32)],
        [SMEM_SPEC] + [VMEM_SPEC] * 7,
        (idx, own, par, gain, *(in_vmem(w) for w in ws)),
        [pltpu.VMEM((2 * ROWS, d), jnp.bfloat16), pltpu.VMEM((2 * ROWS, d), jnp.float32)],
        8 * MIB,
        us=4,
        behind=behind,
    )


def up_kernel(idx, own, par, gain, w_in, r_in, hidden, normed):
    for k in range(own.shape[0] // ROWS):
        prepare(idx, window(own, k * ROWS, ROWS), window(par, k * ROWS, ROWS), gain, window(normed, 2 * k * ROWS, 2 * ROWS))
    units = w_in.shape[1]
    for n, w in enumerate((w_in, r_in)):
        for lo in range(0, units, HB):
            hidden[:, pl.ds(n * units + lo, HB)] = up(normed[...], w[:, pl.ds(lo, HB)])


def up_rows(order, idx, own, par, gain, w_in, r_in):
    rows, d = own.shape
    return order.call(
        up_kernel,
        "up",
        [jax.ShapeDtypeStruct((2 * rows, 2 * w_in.shape[1]), jnp.bfloat16)],
        [SMEM_SPEC] + [VMEM_SPEC] * 5,
        (idx, own, par, gain, in_vmem(w_in), in_vmem(r_in)),
        [pltpu.VMEM((2 * rows, d), jnp.bfloat16)],
        8 * MIB,
        us=3,
    )[0]


def down_kernel(lo, idx, own, par, hidden, w_out, r_out, give, keep):
    rows = give.shape[0]
    units = w_out.shape[0]
    mine = window(hidden, 2 * lo, 2 * rows)
    total = jnp.dot(mine[:, pl.ds(0, units)], w_out[...], preferred_element_type=jnp.float32)
    total += jnp.dot(mine[:, pl.ds(units, units)], r_out[...], preferred_element_type=jnp.float32)
    give[...] = total[rows:].astype(jnp.bfloat16)
    keep[...] = kept_rows(idx, window(own, lo, rows), window(par, lo, rows)) + total[:rows]


def down(order, idx, own, par, hidden, w_out, r_out, lo, behind=()):
    d = own.shape[1]
    return order.call(
        functools.partial(down_kernel, lo),
        "down",
        [jax.ShapeDtypeStruct((ROWS, d), jnp.bfloat16), jax.ShapeDtypeStruct((ROWS, d), jnp.float32)],
        [SMEM_SPEC] + [VMEM_SPEC] * 5,
        (idx, own, par, hidden, in_vmem(w_out), in_vmem(r_out)),
        vmem=8 * MIB,
        us=2,
        behind=behind,
    )


def join_kernel(keep, got, out):
    out[...] = (keep[...] + got[...].astype(jnp.float32)).astype(jnp.bfloat16)


def join(order, keep, got, behind=()):
    shape = jax.ShapeDtypeStruct(got.shape, jnp.bfloat16)
    return order.call(join_kernel, "join", [shape], [VMEM_SPEC] * 2, (keep, got), us=0.5, behind=behind)[0]


def last_kernel(keep, got, *refs):
    *done, out = refs
    rows = keep.shape[0]
    for k, x in enumerate(done):
        out[0, pl.ds(k * rows, rows), :] = x[...]
    out[0, pl.ds(len(done) * rows, rows), :] = (keep[...] + got[...].astype(jnp.float32)).astype(jnp.bfloat16)


def pack_kernel(*refs):
    *xs, out = refs
    rows = xs[0].shape[0]
    for k, x in enumerate(xs):
        out[0, pl.ds(k * rows, rows), :] = x[...]


def whole(order, kernel, name, args, rows):
    shape = jax.ShapeDtypeStruct((1, rows, args[0].shape[1]), jnp.bfloat16)
    return order.call(kernel, name, [shape], [VMEM_SPEC] * len(args), args, vmem=8 * MIB, us=0.5)[0]


def body(act, group_of, gain, w_in, w_out):
    place = lax.axis_index("section")
    g1 = group_of[0]
    prior = route(group_of, to_next_section)[0]
    g2 = jnp.where(place == 0, 1, prior).astype(jnp.int32)
    swap = (place % Y != Y - 1).astype(jnp.int32)
    idx1, idx2 = jnp.stack([g1, swap]), jnp.stack([g2, jnp.ones((), jnp.int32)])
    order = Order()

    def across(x):
        return route(x, to_x_neighbour)

    def onward(x):
        return route(x, to_next_section)

    def mirror(*xs):
        return route(whole(order, pack_kernel, "pack", xs, len(xs) * ROWS), to_mirror)

    rows = act.shape[1]
    r_in, r_out = route(w_in, to_other_core), route(w_out, to_other_core)
    own = [act[0, : rows // 2], act[0, rows // 2 :]]
    par = [across(x) for x in own]

    ((w_in1, w_out1, r_in1),) = pick(order, (g1,), (w_in, w_out, r_in))
    hidden = up_rows(order, idx1, own[0], par[0], gain, w_in1, r_in1)
    ((r_out1,),) = pick(order, (g1,), (r_out,))
    w1 = (w_in1, w_out1, r_in1, r_out1)
    give, keep0 = down(order, idx1, own[0], par[0], hidden, w_out1, r_out1, 0)
    got0 = across(give)
    give, keep1 = down(order, idx1, own[0], par[0], hidden, w_out1, r_out1, ROWS, (par[1], g2.reshape(1)))
    got1 = across(give)
    give, keep2 = block(order, idx1, own[1], par[1], gain, w1, 0, 0)
    got2 = across(give)
    x0 = onward(join(order, keep0, got0))
    give, keep3 = block(order, idx1, own[1], par[1], gain, w1, ROWS, ROWS)
    got3 = across(give)
    x1 = onward(join(order, keep1, got1))
    ((w_in2, w_out2),) = pick(order, (g2,), (w_in, w_out))
    x2 = onward(join(order, keep2, got2))
    ((r_in2, r_out2),) = pick(order, (g2,), (r_in, r_out), (x0,))
    x3 = onward(join(order, keep3, got3, (x1,)))
    w2 = (w_in2, w_out2, r_in2, r_out2)

    y0, y1, y2, y3 = (across(x) for x in (x0, x1, x2, x3))
    give, keep0 = block(order, idx2, x0, y0, gain, w2)
    got0 = across(give)
    low = mirror(x0, x1)
    give, keep1 = block(order, idx2, x1, y1, gain, w2, behind=(x2,))
    got1 = across(give)
    high = mirror(x2, x3)
    give, keep2 = block(order, idx2, x2, y2, gain, w2, behind=(y3,))
    got2 = across(give)
    give, keep3 = block(order, idx2, x3, y3, gain, w2)
    got3 = across(give)
    done = [join(order, keep0, got0), join(order, keep1, got1, (low,)), join(order, keep2, got2)]
    stash = whole(order, pack_kernel, "pack", (low[0], high[0]), rows)
    return whole(order, last_kernel, "last", (keep3, got3, *done), rows), stash


def solution(mesh):
    placed = (
        P("section", "tensor", None),
        P("section"),
        P("section", None, None),
        P("section", None, None, "tensor"),
        P("section", None, "tensor", None),
    )
    return jax.shard_map(
        body,
        mesh=mesh,
        in_specs=placed,
        out_specs=(P("section", "tensor", None), P("section", "tensor", None)),
        check_vma=False,
    )
```

time: 469 us -> 107 us (0.23)
  waiting for transfers between devices: 390 us -> 25.7 us
  Pallas kernels: 0 us -> 47.6 us
  matrix products: 31 us -> 0 us
  other arithmetic: 15.2 us -> 0.15 us
  starting transfers between devices: 15.9 us -> 30.3 us
  between operations: 15.1 us -> 2.17 us
    ppermute x7 -> x23, waiting for transfers between devices: 216 us -> 25.7 us  [route(): return lax.ppermute(x, AXES, pairs)]
    psum x1 -> x0, waiting for transfers between devices: 92.9 us -> none  [body(): lax.psum(jnp.dot(hidden_one, first_out, preferred_element_type=jnp.float3...]
    pallas_call x0 -> x24, Pallas kernels: none -> 47.6 us  [call(): pl.pallas_call(with_token, out_shape=tuple(outs) + (jax.ShapeDtypeStruct(...]
    reduce_scatter x1 -> x0, waiting for transfers between devices: 41.9 us -> none  [contract(): lax.psum_scatter(jnp.dot(hidden, w_second, preferred_element_type=jnp.flo...]
    all_gather x1 -> x0, waiting for transfers between devices: 38 us -> none  [body(): whole_rows = lax.all_gather(shard_rows, 'tensor', axis=0, tiled=True)]
    dot_general x2 -> x0, matrix products: 31 us -> none  [the longest x1 15.5 us: contract(): jnp.dot(hidden, w_second, preferred_element_type=jnp.float32)]
    ppermute x7 -> x23, starting transfers between devices: 15.8 us -> 30.3 us  [route(): return lax.ppermute(x, AXES, pairs)]
    convert_element_type x2 -> x0, other arithmetic: 6.18 us -> none  [the longest x1 5.39 us: body(): (whole_rows.astype(jnp.float32) + branch).astype(jnp.bfloat16)]
  transfers between devices with their start and end apart: 10 -> 23, of which waited for: 10 -> 8; matrix products, arithmetic and copies ran while one was open for 0% -> 1% of each run, Pallas kernels for 0% -> 43%
where the time goes in v2:
time: 107 us
  Pallas kernels  47.6 us (44%)
  starting transfers between devices  30.3 us (28%)
  waiting for transfers between devices  25.7 us (24%)
  between operations  2.17 us (2%)
  local copies, waits for them, and re-layouts  1.27 us (1%)
    pallas_call x24, Pallas kernels, call(): pl.pallas_call(with_token, out_shape=tuple(outs) + (jax.ShapeDtypeStruct(...  47.6 us
    ppermute x23, starting transfers between devices, route(): return lax.ppermute(x, AXES, pairs)  30.3 us
    ppermute x23, waiting for transfers between devices, route(): return lax.ppermute(x, AXES, pairs)  25.7 us
  transfers between devices with their start and end apart: 23, of which 8 were waited for; matrix products, arithmetic and copies ran while one was open for 1% of the time, Pallas kernels for 43%

profile of v2, /device:TPU:0, one launch (start us, length us, event | category | flops | bytes accessed | tf_op | source)
XLA Modules:
  0.0 107.2 jit_solution(15941946959836668287)
XLA Ops:
  2.5 1.7 %collective-permute-start.4 = (bf16[128,2048]{1,0:T(8,128)(2,1)S(1)}, bf16[128,2048]{1,0:T(8,128)(2,1)S(1)}, u32[]{:S(2)}, u32[]{:S(2)}) collective-permute-start(bf16[128,2048]{1,0:T(8,128)(2,1)S(1)} %get-tuple-element.120.refs_1_), channel_id=1, source_target_pairs={{0,2},{1,3},{2,0},{3,1},{4,6},{5,7},{6,4},{7,5},{8,10},{9,11},{10,... | collective-permute-start | bytes 1572872 | tf_op jit(solution)/shard_map/ppermute | solution.py:25
  7.0 6.8 %collective-permute-done = s32[1]{0:T(128)} collective-permute-done((s32[1]{0:T(128)}, s32[1]{0:T(128)}, u32[]{:S(2)}, u32[]{:S(2)}) %collective-permute-start) | collective-permute-done | bytes 36 | tf_op jit(solution)/shard_map/ppermute | solution.py:25
  14.5 4.7 %pick_group.4 = (bf16[2048,1024]{1,0:T(8,128)(2,1)S(1)}, bf16[1024,2048]{1,0:T(8,128)(2,1)S(1)}, bf16[2048,1024]{1,0:T(8,128)(2,1)S(1)}, f32[8,128]{1,0:T(8,128)S(1)}) custom-call(s32[1]{0:T(128)S(6)} %copy.7.refs_0_, bf16[1,2,2048,1024]{3,2,1,0:T(8,128)(2,1)} %refs_1_.3, bf16[1,2,1024,2048]{3,2,1,0:T(8,128)(2,1)} %refs_2_.3, ...), custom_call_target="tpu_custom_call" | custom-call | flops 5864999936 | bytes 16384 | tf_op jit(solution)/shard_map/pick_group/pallas_call | solution.py:65
  19.2 4.0 %up.1 = (bf16[256,2048]{1,0:T(8,128)(2,1)S(1)}, f32[8,128]{1,0:T(8,128)S(1)}) custom-call(s32[2]{0:T(128)S(1)} %pad_add_fusion.1.refs_0_, bf16[128,2048]{1,0:T(8,128)(2,1)S(1)} %get-tuple-element.120.refs_1_, bf16[128,2048]{1,0:T(8,128)(2,1)S(1)} %collective-permute-done.4.refs_2_, bf16[1,2,2048]{2,1,0:T(2,128)(2,1)S(1)} %copy-done, ...), custom_call_target="tpu_custom_call" | custom-call | flops 3449999872 | bytes 16384 | tf_op jit(solution)/shard_map/up/pallas_call | solution.py:65
  23.2 3.0 %collective-permute-done.3.refs_1_.refs_2_ = bf16[1,2,1024,2048]{3,2,1,0:T(8,128)(2,1)} collective-permute-done((bf16[1,2,1024,2048]{3,2,1,0:T(8,128)(2,1)}, bf16[1,2,1024,2048]{3,2,1,0:T(8,128)(2,1)}, u32[]{:S(2)}, u32[]{:S(2)}) %collective-permute-start.3) | collective-permute-done | bytes 8388640 | tf_op jit(solution)/shard_map/ppermute | solution.py:25
  26.2 2.2 %pick_group.5 = (bf16[1024,2048]{1,0:T(8,128)(2,1)S(1)}, f32[8,128]{1,0:T(8,128)S(1)}) custom-call(s32[1]{0:T(128)S(6)} %copy.7.refs_0_, bf16[1,2,1024,2048]{3,2,1,0:T(8,128)(2,1)} %collective-permute-done.3.refs_1_.refs_2_, f32[8,128]{1,0:T(8,128)S(1)} %get-tuple-element.65.refs_2_), custom_call_target="tpu_custom_call" | custom-call | flops 1955000064 | bytes 16384 | tf_op jit(solution)/shard_map/pick_group/pallas_call | solution.py:65
  28.4 1.8 %down.2 = (bf16[64,2048]{1,0:T(8,128)(2,1)S(1)}, f32[64,2048]{1,0:T(8,128)S(1)}, f32[8,128]{1,0:T(8,128)S(1)}) custom-call(s32[2]{0:T(128)S(1)} %pad_add_fusion.1.refs_0_, bf16[128,2048]{1,0:T(8,128)(2,1)S(1)} %get-tuple-element.120.refs_1_, bf16[128,2048]{1,0:T(8,128)(2,1)S(1)} %collective-permute-done.4.refs_2_, ...), custom_call_target="tpu_custom_call" | custom-call | flops 2300000000 | bytes 16384 | tf_op jit(solution)/shard_map/down/pallas_call | solution.py:65
  30.3 1.6 %collective-permute-start.5 = (bf16[64,2048]{1,0:T(8,128)(2,1)S(1)}, bf16[64,2048]{1,0:T(8,128)(2,1)S(1)}, u32[]{:S(2)}, u32[]{:S(2)}) collective-permute-start(bf16[64,2048]{1,0:T(8,128)(2,1)S(1)} %get-tuple-element.70), channel_id=1, source_target_pairs={{0,2},{1,3},{2,0},{3,1},{4,6},{5,7},{6,4},{7,5},{8,10},{9,11},{10,... | collective-permute-start | bytes 786440 | tf_op jit(solution)/shard_map/ppermute | solution.py:25
  31.9 1.8 %down.3 = (bf16[64,2048]{1,0:T(8,128)(2,1)S(1)}, f32[64,2048]{1,0:T(8,128)S(1)}, f32[8,128]{1,0:T(8,128)S(1)}) custom-call(s32[2]{0:T(128)S(1)} %pad_add_fusion.1.refs_0_, bf16[128,2048]{1,0:T(8,128)(2,1)S(1)} %get-tuple-element.120.refs_1_, bf16[128,2048]{1,0:T(8,128)(2,1)S(1)} %collective-permute-done.4.refs_2_, ...), custom_call_target="tpu_custom_call" | custom-call | flops 2300000000 | bytes 16384 | tf_op jit(solution)/shard_map/down/pallas_call | solution.py:65
  34.3 3.9 %block.6 = (bf16[64,2048]{1,0:T(8,128)(2,1)S(1)}, f32[64,2048]{1,0:T(8,128)S(1)}, f32[8,128]{1,0:T(8,128)S(1)}) custom-call(s32[2]{0:T(128)S(1)} %pad_add_fusion.1.refs_0_, bf16[128,2048]{1,0:T(8,128)(2,1)S(1)} %get-tuple-element.121.refs_1_, bf16[128,2048]{1,0:T(8,128)(2,1)S(1)} %collective-permute-done.1.refs_7_.refs_2_, bf16[1,2,2048]{2,1,0:T(2,128)(2,1)S(1)} %copy-done, ...), custom_call_target="tpu_custom_call" | custom-call | flops 4600000000 | bytes 16384 | tf_op jit(solution)/shard_map/block/pallas_call | solution.py:65
  39.9 1.8 %collective-permute-start.9 = (bf16[64,2048]{1,0:T(8,128)(2,1)S(1)}, bf16[64,2048]{1,0:T(8,128)(2,1)S(1)}, u32[]{:S(2)}, u32[]{:S(2)}) collective-permute-start(bf16[64,2048]{1,0:T(8,128)(2,1)S(1)} %get-tuple-element.85), channel_id=1, source_target_pairs={{0,4},{1,5},{2,6},{3,7},{4,8},{5,9},{6,10},{7,11},{8,12},{9,13},{1... | collective-permute-start | bytes 786440 | tf_op jit(solution)/shard_map/ppermute | solution.py:25
  41.8 3.9 %block.7 = (bf16[64,2048]{1,0:T(8,128)(2,1)S(1)}, f32[64,2048]{1,0:T(8,128)S(1)}, f32[8,128]{1,0:T(8,128)S(1)}) custom-call(s32[2]{0:T(128)S(1)} %pad_add_fusion.1.refs_0_, bf16[128,2048]{1,0:T(8,128)(2,1)S(1)} %get-tuple-element.121.refs_1_, bf16[128,2048]{1,0:T(8,128)(2,1)S(1)} %collective-permute-done.1.refs_7_.refs_2_, bf16[1,2,2048]{2,1,0:T(2,128)(2,1)S(1)} %copy-done, ...), custom_call_target="tpu_custom_call" | custom-call | flops 4600000000 | bytes 16384 | tf_op jit(solution)/shard_map/block/pallas_call | solution.py:65
  48.6 3.5 %pick_group.6 = (bf16[2048,1024]{1,0:T(8,128)(2,1)S(1)}, bf16[1024,2048]{1,0:T(8,128)(2,1)S(1)}, f32[8,128]{1,0:T(8,128)S(1)}) custom-call(s32[1]{0:T(128)} %bitcast.1.refs_8_.refs_0_, bf16[1,2,2048,1024]{3,2,1,0:T(8,128)(2,1)} %refs_1_.3, bf16[1,2,1024,2048]{3,2,1,0:T(8,128)(2,1)} %refs_2_.3, f32[8,128]{1,0:T(8,128)S(1)} %get-tuple-element.82.refs_3_), custom_call_target="tpu_custom_call" | custom-call | flops 3910000128 | bytes 16384 | tf_op jit(solution)/shard_map/pick_group/pallas_call | solution.py:65
  55.4 3.5 %pick_group.7 = (bf16[2048,1024]{1,0:T(8,128)(2,1)S(1)}, bf16[1024,2048]{1,0:T(8,128)(2,1)S(1)}, f32[8,128]{1,0:T(8,128)S(1)}) custom-call(s32[1]{0:T(128)} %bitcast.1.refs_8_.refs_0_, bf16[1,2,2048,1024]{3,2,1,0:T(8,128)(2,1)} %collective-permute-done.2.refs_3_.refs_1_, bf16[1,2,1024,2048]{3,2,1,0:T(8,128)(2,1)} %collective-permute-done.3.refs_1_.refs_2_, ...), custom_call_target="tpu_custom_call" | custom-call | flops 3910000128 | bytes 16384 | tf_op jit(solution)/shard_map/pick_group/pallas_call | solution.py:65
  61.3 3.9 %collective-permute-done.13.refs_9_.refs_0_.refs_1_ = bf16[64,2048]{1,0:T(8,128)(2,1)S(1)} collective-permute-done((bf16[64,2048]{1,0:T(8,128)(2,1)S(1)}, bf16[64,2048]{1,0:T(8,128)(2,1)S(1)}, u32[]{:S(2)}, u32[]{:S(2)}) %collective-permute-start.13) | collective-permute-done | bytes 262176 | tf_op jit(solution)/shard_map/ppermute | solution.py:25
  65.8 3.9 %block.8 = (bf16[64,2048]{1,0:T(8,128)(2,1)S(1)}, f32[64,2048]{1,0:T(8,128)S(1)}, f32[8,128]{1,0:T(8,128)S(1)}) custom-call(s32[2]{0:T(128)S(1)} %pad_add_fusion.refs_0_, bf16[64,2048]{1,0:T(8,128)(2,1)S(1)} %collective-permute-done.9.refs_4_.refs_1_.refs_0_, bf16[64,2048]{1,0:T(8,128)(2,1)S(1)} %collective-permute-done.16.refs_2_, ...), custom_call_target="tpu_custom_call" | custom-call | flops 4600000000 | bytes 16384 | tf_op jit(solution)/shard_map/block/pallas_call | solution.py:65
  72.1 3.9 %block.9 = (bf16[64,2048]{1,0:T(8,128)(2,1)S(1)}, f32[64,2048]{1,0:T(8,128)S(1)}, f32[8,128]{1,0:T(8,128)S(1)}) custom-call(s32[2]{0:T(128)S(1)} %pad_add_fusion.refs_0_, bf16[64,2048]{1,0:T(8,128)(2,1)S(1)} %collective-permute-done.10.refs_3_.refs_1_, bf16[64,2048]{1,0:T(8,128)(2,1)S(1)} %collective-permute-done.15.refs_2_, ...), custom_call_target="tpu_custom_call" | custom-call | flops 4600000000 | bytes 16384 | tf_op jit(solution)/shard_map/block/pallas_call | solution.py:65
  76.0 2.1 %collective-permute-start.19 = (bf16[64,2048]{1,0:T(8,128)(2,1)S(1)}, bf16[64,2048]{1,0:T(8,128)(2,1)S(1)}, u32[]{:S(2)}, u32[]{:S(2)}) collective-permute-start(bf16[64,2048]{1,0:T(8,128)(2,1)S(1)} %get-tuple-element.107), channel_id=1, source_target_pairs={{0,2},{1,3},{2,0},{3,1},{4,6},{5,7},{6,4},{7,5},{8,10},{9,11},{10,... | collective-permute-start | bytes 786440 | tf_op jit(solution)/shard_map/ppermute | solution.py:25
  78.1 3.6 %collective-permute-start.20 = (bf16[1,128,2048]{2,1,0:T(8,128)(2,1)S(1)}, bf16[1,128,2048]{2,1,0:T(8,128)(2,1)S(1)}, u32[]{:S(2)}, u32[]{:S(2)}) collective-permute-start(bf16[1,128,2048]{2,1,0:T(8,128)(2,1)S(1)} %get-tuple-element.109), channel_id=1, source_target_pairs={{0,126},{1,127},{2,124},{3,125},{4,122},{5,123},{6,120},{7,121},{8... | collective-permute-start | bytes 1572872 | tf_op jit(solution)/shard_map/ppermute | solution.py:25
  81.7 4.0 %collective-permute-start.22 = (bf16[1,128,2048]{2,1,0:T(8,128)(2,1)S(1)}, bf16[1,128,2048]{2,1,0:T(8,128)(2,1)S(1)}, u32[]{:S(2)}, u32[]{:S(2)}) collective-permute-start(bf16[1,128,2048]{2,1,0:T(8,128)(2,1)S(1)} %get-tuple-element.115), channel_id=1, source_target_pairs={{0,126},{1,127},{2,124},{3,125},{4,122},{5,123},{6,120},{7,121},{8... | collective-permute-start | bytes 1572872 | tf_op jit(solution)/shard_map/ppermute | solution.py:25
  85.7 3.9 %block.10 = (bf16[64,2048]{1,0:T(8,128)(2,1)S(1)}, f32[64,2048]{1,0:T(8,128)S(1)}, f32[8,128]{1,0:T(8,128)S(1)}) custom-call(s32[2]{0:T(128)S(1)} %pad_add_fusion.refs_0_, bf16[64,2048]{1,0:T(8,128)(2,1)S(1)} %collective-permute-done.13.refs_9_.refs_0_.refs_1_, bf16[64,2048]{1,0:T(8,128)(2,1)S(1)} %collective-permute-done.14.refs_2_, ...), custom_call_target="tpu_custom_call" | custom-call | flops 4600000000 | bytes 16384 | tf_op jit(solution)/shard_map/block/pallas_call | solution.py:65
  90.3 3.9 %block.11 = (bf16[64,2048]{1,0:T(8,128)(2,1)S(1)}, f32[64,2048]{1,0:T(8,128)S(1)}, f32[8,128]{1,0:T(8,128)S(1)}) custom-call(s32[2]{0:T(128)S(1)} %pad_add_fusion.refs_0_, bf16[64,2048]{1,0:T(8,128)(2,1)S(1)} %collective-permute-done.11.refs_1_, bf16[64,2048]{1,0:T(8,128)(2,1)S(1)} %collective-permute-done.12.refs_9_.refs_2_, ...), custom_call_target="tpu_custom_call" | custom-call | flops 4600000000 | bytes 16384 | tf_op jit(solution)/shard_map/block/pallas_call | solution.py:65
  95.8 2.6 %collective-permute-done.20.refs_3_ = bf16[1,128,2048]{2,1,0:T(8,128)(2,1)S(1)} collective-permute-done((bf16[1,128,2048]{2,1,0:T(8,128)(2,1)S(1)}, bf16[1,128,2048]{2,1,0:T(8,128)(2,1)S(1)}, u32[]{:S(2)}, u32[]{:S(2)}) %collective-permute-start.20) | collective-permute-done | bytes 524320 | tf_op jit(solution)/shard_map/ppermute | solution.py:25
  98.5 6.6 %collective-permute-done.22 = bf16[1,128,2048]{2,1,0:T(8,128)(2,1)S(1)} collective-permute-done((bf16[1,128,2048]{2,1,0:T(8,128)(2,1)S(1)}, bf16[1,128,2048]{2,1,0:T(8,128)(2,1)S(1)}, u32[]{:S(2)}, u32[]{:S(2)}) %collective-permute-start.22) | collective-permute-done | bytes 524320 | tf_op jit(solution)/shard_map/ppermute | solution.py:25
  (52 shorter events, 22.4 us)
Async XLA Ops:
  0.6 13.9 %collective-permute-start.2 = (bf16[1,2,2048,1024]{3,2,1,0:T(8,128)(2,1)}, bf16[1,2,2048,1024]{3,2,1,0:T(8,128)(2,1)}, u32[]{:S(2)}, u32[]{:S(2)}) collective-permute-start(bf16[1,2,2048,1024]{3,2,1,0:T(8,128)(2,1)} %refs_1_.3), channel_id=1, source_target_pairs={{0,1},{1,0},{2,3},{3,2},{4,5},{5,4},{6,7},{7,6},{8,9},{9,8},{10,11... | collective-permute-start | bytes 25165832 | tf_op jit(solution)/shard_map/ppermute | solution.py:25
  0.7 25.5 %collective-permute-start.3 = (bf16[1,2,1024,2048]{3,2,1,0:T(8,128)(2,1)}, bf16[1,2,1024,2048]{3,2,1,0:T(8,128)(2,1)}, u32[]{:S(2)}, u32[]{:S(2)}) collective-permute-start(bf16[1,2,1024,2048]{3,2,1,0:T(8,128)(2,1)} %refs_2_.3), channel_id=1, source_target_pairs={{0,1},{1,0},{2,3},{3,2},{4,5},{5,4},{6,7},{7,6},{8,9},{9,8},{10,11... | collective-permute-start | bytes 25165832 | tf_op jit(solution)/shard_map/ppermute | solution.py:25
  2.5 16.7 %collective-permute-start.4 = (bf16[128,2048]{1,0:T(8,128)(2,1)S(1)}, bf16[128,2048]{1,0:T(8,128)(2,1)S(1)}, u32[]{:S(2)}, u32[]{:S(2)}) collective-permute-start(bf16[128,2048]{1,0:T(8,128)(2,1)S(1)} %get-tuple-element.120.refs_1_), channel_id=1, source_target_pairs={{0,2},{1,3},{2,0},{3,1},{4,6},{5,7},{6,4},{7,5},{8,10},{9,11},{10,... | collective-permute-start | bytes 1572872 | tf_op jit(solution)/shard_map/ppermute | solution.py:25
  4.1 9.6 %collective-permute-start = (s32[1]{0:T(128)}, s32[1]{0:T(128)}, u32[]{:S(2)}, u32[]{:S(2)}) collective-permute-start(s32[1]{0:T(128)} %param.6), channel_id=1, source_target_pairs={{0,4},{1,5},{2,6},{3,7},{4,8},{5,9},{6,10},{7,11},{8,12},{9,13},{1... | collective-permute-start | bytes 20 | tf_op jit(solution)/shard_map/ppermute | solution.py:25
  5.7 26.2 %collective-permute-start.1 = (bf16[128,2048]{1,0:T(8,128)(2,1)S(1)}, bf16[128,2048]{1,0:T(8,128)(2,1)S(1)}, u32[]{:S(2)}, u32[]{:S(2)}) collective-permute-start(bf16[128,2048]{1,0:T(8,128)(2,1)S(1)} %get-tuple-element.121.refs_1_), channel_id=1, source_target_pairs={{0,2},{1,3},{2,0},{3,1},{4,6},{5,7},{6,4},{7,5},{8,10},{9,11},{10,... | collective-permute-start | bytes 1572872 | tf_op jit(solution)/shard_map/ppermute | solution.py:25
  14.5 4.7 %copy-start = (bf16[1,2,2048]{2,1,0:T(2,128)(2,1)S(1)}, bf16[1,2,2048]{2,1,0:T(2,128)(2,1)}, u32[]{:S(2)}) copy-start(bf16[1,2,2048]{2,1,0:T(2,128)(2,1)} %refs_3_.13) | copy-start | bytes 24580
  30.3 9.6 %collective-permute-start.5 = (bf16[64,2048]{1,0:T(8,128)(2,1)S(1)}, bf16[64,2048]{1,0:T(8,128)(2,1)S(1)}, u32[]{:S(2)}, u32[]{:S(2)}) collective-permute-start(bf16[64,2048]{1,0:T(8,128)(2,1)S(1)} %get-tuple-element.70), channel_id=1, source_target_pairs={{0,2},{1,3},{2,0},{3,1},{4,6},{5,7},{6,4},{7,5},{8,10},{9,11},{10,... | collective-permute-start | bytes 786440 | tf_op jit(solution)/shard_map/ppermute | solution.py:25
  33.8 11.9 %collective-permute-start.8 = (bf16[64,2048]{1,0:T(8,128)(2,1)S(1)}, bf16[64,2048]{1,0:T(8,128)(2,1)S(1)}, u32[]{:S(2)}, u32[]{:S(2)}) collective-permute-start(bf16[64,2048]{1,0:T(8,128)(2,1)S(1)} %get-tuple-element.80), channel_id=1, source_target_pairs={{0,2},{1,3},{2,0},{3,1},{4,6},{5,7},{6,4},{7,5},{8,10},{9,11},{10,... | collective-permute-start | bytes 786440 | tf_op jit(solution)/shard_map/ppermute | solution.py:25
  38.2 13.8 %collective-permute-start.7 = (bf16[64,2048]{1,0:T(8,128)(2,1)S(1)}, bf16[64,2048]{1,0:T(8,128)(2,1)S(1)}, u32[]{:S(2)}, u32[]{:S(2)}) collective-permute-start(bf16[64,2048]{1,0:T(8,128)(2,1)S(1)} %get-tuple-element.78), channel_id=1, source_target_pairs={{0,2},{1,3},{2,0},{3,1},{4,6},{5,7},{6,4},{7,5},{8,10},{9,11},{10,... | collective-permute-start | bytes 786440 | tf_op jit(solution)/shard_map/ppermute | solution.py:25
  39.9 14.5 %collective-permute-start.9 = (bf16[64,2048]{1,0:T(8,128)(2,1)S(1)}, bf16[64,2048]{1,0:T(8,128)(2,1)S(1)}, u32[]{:S(2)}, u32[]{:S(2)}) collective-permute-start(bf16[64,2048]{1,0:T(8,128)(2,1)S(1)} %get-tuple-element.85), channel_id=1, source_target_pairs={{0,4},{1,5},{2,6},{3,7},{4,8},{5,9},{6,10},{7,11},{8,12},{9,13},{1... | collective-permute-start | bytes 786440 | tf_op jit(solution)/shard_map/ppermute | solution.py:25
  45.8 14.3 %collective-permute-start.10 = (bf16[64,2048]{1,0:T(8,128)(2,1)S(1)}, bf16[64,2048]{1,0:T(8,128)(2,1)S(1)}, u32[]{:S(2)}, u32[]{:S(2)}) collective-permute-start(bf16[64,2048]{1,0:T(8,128)(2,1)S(1)} %get-tuple-element.87), channel_id=1, source_target_pairs={{0,4},{1,5},{2,6},{3,7},{4,8},{5,9},{6,10},{7,11},{8,12},{9,13},{1... | collective-permute-start | bytes 786440 | tf_op jit(solution)/shard_map/ppermute | solution.py:25
  47.4 12.7 %collective-permute-start.6 = (bf16[64,2048]{1,0:T(8,128)(2,1)S(1)}, bf16[64,2048]{1,0:T(8,128)(2,1)S(1)}, u32[]{:S(2)}, u32[]{:S(2)}) collective-permute-start(bf16[64,2048]{1,0:T(8,128)(2,1)S(1)} %get-tuple-element.76), channel_id=1, source_target_pairs={{0,2},{1,3},{2,0},{3,1},{4,6},{5,7},{6,4},{7,5},{8,10},{9,11},{10,... | collective-permute-start | bytes 786440 | tf_op jit(solution)/shard_map/ppermute | solution.py:25
  52.1 13.1 %collective-permute-start.13 = (bf16[64,2048]{1,0:T(8,128)(2,1)S(1)}, bf16[64,2048]{1,0:T(8,128)(2,1)S(1)}, u32[]{:S(2)}, u32[]{:S(2)}) collective-permute-start(bf16[64,2048]{1,0:T(8,128)(2,1)S(1)} %get-tuple-element.93), channel_id=1, source_target_pairs={{0,4},{1,5},{2,6},{3,7},{4,8},{5,9},{6,10},{7,11},{8,12},{9,13},{1... | collective-permute-start | bytes 786440 | tf_op jit(solution)/shard_map/ppermute | solution.py:25
  54.5 11.3 %collective-permute-start.16 = (bf16[64,2048]{1,0:T(8,128)(2,1)S(1)}, bf16[64,2048]{1,0:T(8,128)(2,1)S(1)}, u32[]{:S(2)}, u32[]{:S(2)}) collective-permute-start(bf16[64,2048]{1,0:T(8,128)(2,1)S(1)} %collective-permute-done.9.refs_4_.refs_1_.refs_0_), channel_id=1, source_target_pairs={{0,2},{1,3},{2,0},{3,1},{4,6},{5,7},{6,4},{7,5},{8,10},{9,11},{10,... | collective-permute-start | bytes 786440 | tf_op jit(solution)/shard_map/ppermute | solution.py:25
  60.2 11.9 %collective-permute-start.11 = (bf16[64,2048]{1,0:T(8,128)(2,1)S(1)}, bf16[64,2048]{1,0:T(8,128)(2,1)S(1)}, u32[]{:S(2)}, u32[]{:S(2)}) collective-permute-start(bf16[64,2048]{1,0:T(8,128)(2,1)S(1)} %get-tuple-element.88), channel_id=1, source_target_pairs={{0,4},{1,5},{2,6},{3,7},{4,8},{5,9},{6,10},{7,11},{8,12},{9,13},{1... | collective-permute-start | bytes 786440 | tf_op jit(solution)/shard_map/ppermute | solution.py:25
  60.2 11.8 %collective-permute-start.15 = (bf16[64,2048]{1,0:T(8,128)(2,1)S(1)}, bf16[64,2048]{1,0:T(8,128)(2,1)S(1)}, u32[]{:S(2)}, u32[]{:S(2)}) collective-permute-start(bf16[64,2048]{1,0:T(8,128)(2,1)S(1)} %collective-permute-done.10.refs_3_.refs_1_), channel_id=1, source_target_pairs={{0,2},{1,3},{2,0},{3,1},{4,6},{5,7},{6,4},{7,5},{8,10},{9,11},{10,... | collective-permute-start | bytes 786440 | tf_op jit(solution)/shard_map/ppermute | solution.py:25
  65.2 16.5 %collective-permute-start.14 = (bf16[64,2048]{1,0:T(8,128)(2,1)S(1)}, bf16[64,2048]{1,0:T(8,128)(2,1)S(1)}, u32[]{:S(2)}, u32[]{:S(2)}) collective-permute-start(bf16[64,2048]{1,0:T(8,128)(2,1)S(1)} %collective-permute-done.13.refs_9_.refs_0_.refs_1_), channel_id=1, source_target_pairs={{0,2},{1,3},{2,0},{3,1},{4,6},{5,7},{6,4},{7,5},{8,10},{9,11},{10,... | collective-permute-start | bytes 786440 | tf_op jit(solution)/shard_map/ppermute | solution.py:25
  69.7 24.5 %collective-permute-start.18 = (bf16[64,2048]{1,0:T(8,128)(2,1)S(1)}, bf16[64,2048]{1,0:T(8,128)(2,1)S(1)}, u32[]{:S(2)}, u32[]{:S(2)}) collective-permute-start(bf16[64,2048]{1,0:T(8,128)(2,1)S(1)} %get-tuple-element.103), channel_id=1, source_target_pairs={{0,2},{1,3},{2,0},{3,1},{4,6},{5,7},{6,4},{7,5},{8,10},{9,11},{10,... | collective-permute-start | bytes 786440 | tf_op jit(solution)/shard_map/ppermute | solution.py:25
  72.0 13.7 %collective-permute-start.12 = (bf16[64,2048]{1,0:T(8,128)(2,1)S(1)}, bf16[64,2048]{1,0:T(8,128)(2,1)S(1)}, u32[]{:S(2)}, u32[]{:S(2)}) collective-permute-start(bf16[64,2048]{1,0:T(8,128)(2,1)S(1)} %collective-permute-done.11.refs_1_), channel_id=1, source_target_pairs={{0,2},{1,3},{2,0},{3,1},{4,6},{5,7},{6,4},{7,5},{8,10},{9,11},{10,... | collective-permute-start | bytes 786440 | tf_op jit(solution)/shard_map/ppermute | solution.py:25
  76.0 19.8 %collective-permute-start.19 = (bf16[64,2048]{1,0:T(8,128)(2,1)S(1)}, bf16[64,2048]{1,0:T(8,128)(2,1)S(1)}, u32[]{:S(2)}, u32[]{:S(2)}) collective-permute-start(bf16[64,2048]{1,0:T(8,128)(2,1)S(1)} %get-tuple-element.107), channel_id=1, source_target_pairs={{0,2},{1,3},{2,0},{3,1},{4,6},{5,7},{6,4},{7,5},{8,10},{9,11},{10,... | collective-permute-start | bytes 786440 | tf_op jit(solution)/shard_map/ppermute | solution.py:25
  78.1 20.3 %collective-permute-start.20 = (bf16[1,128,2048]{2,1,0:T(8,128)(2,1)S(1)}, bf16[1,128,2048]{2,1,0:T(8,128)(2,1)S(1)}, u32[]{:S(2)}, u32[]{:S(2)}) collective-permute-start(bf16[1,128,2048]{2,1,0:T(8,128)(2,1)S(1)} %get-tuple-element.109), channel_id=1, source_target_pairs={{0,126},{1,127},{2,124},{3,125},{4,122},{5,123},{6,120},{7,121},{8... | collective-permute-start | bytes 1572872 | tf_op jit(solution)/shard_map/ppermute | solution.py:25
  81.7 23.4 %collective-permute-start.22 = (bf16[1,128,2048]{2,1,0:T(8,128)(2,1)S(1)}, bf16[1,128,2048]{2,1,0:T(8,128)(2,1)S(1)}, u32[]{:S(2)}, u32[]{:S(2)}) collective-permute-start(bf16[1,128,2048]{2,1,0:T(8,128)(2,1)S(1)} %get-tuple-element.115), channel_id=1, source_target_pairs={{0,126},{1,127},{2,124},{3,125},{4,122},{5,123},{6,120},{7,121},{8... | collective-permute-start | bytes 1572872 | tf_op jit(solution)/shard_map/ppermute | solution.py:25
  89.6 8.8 %collective-permute-start.21 = (bf16[64,2048]{1,0:T(8,128)(2,1)S(1)}, bf16[64,2048]{1,0:T(8,128)(2,1)S(1)}, u32[]{:S(2)}, u32[]{:S(2)}) collective-permute-start(bf16[64,2048]{1,0:T(8,128)(2,1)S(1)} %get-tuple-element.112), channel_id=1, source_target_pairs={{0,2},{1,3},{2,0},{3,1},{4,6},{5,7},{6,4},{7,5},{8,10},{9,11},{10,... | collective-permute-start | bytes 786440 | tf_op jit(solution)/shard_map/ppermute | solution.py:25
  94.2 11.9 %collective-permute-start.17 = (bf16[64,2048]{1,0:T(8,128)(2,1)S(1)}, bf16[64,2048]{1,0:T(8,128)(2,1)S(1)}, u32[]{:S(2)}, u32[]{:S(2)}) collective-permute-start(bf16[64,2048]{1,0:T(8,128)(2,1)S(1)} %get-tuple-element.101), channel_id=1, source_target_pairs={{0,2},{1,3},{2,0},{3,1},{4,6},{5,7},{6,4},{7,5},{8,10},{9,11},{10,... | collective-permute-start | bytes 786440 | tf_op jit(solution)/shard_map/ppermute | solution.py:25

commit v3 on v2

--- a/solution.py
+++ b/solution.py
@@ -157,7 +157,7 @@
             keep[...] = kept_rows(idx, own, par) + (total[pl.ds(0, rows), :] + part[:rows])
 
 
-def block(order, idx, own, par, gain, ws, own_lo=0, par_lo=0, behind=()):
+def block(order, idx, own, par, gain, ws, own_lo=0, par_lo=0, behind=(), us=4):
     d = own.shape[1]
     return order.call(
         functools.partial(block_kernel, own_lo, par_lo),
@@ -167,7 +167,7 @@
         (idx, own, par, gain, *(in_vmem(w) for w in ws)),
         [pltpu.VMEM((2 * ROWS, d), jnp.bfloat16), pltpu.VMEM((2 * ROWS, d), jnp.float32)],
         8 * MIB,
-        us=4,
+        us=us,
         behind=behind,
     )
 
@@ -223,9 +223,17 @@
     out[...] = (keep[...] + got[...].astype(jnp.float32)).astype(jnp.bfloat16)
 
 
-def join(order, keep, got, behind=()):
+def join(order, keep, got, behind=(), us=0.5):
     shape = jax.ShapeDtypeStruct(got.shape, jnp.bfloat16)
-    return order.call(join_kernel, "join", [shape], [VMEM_SPEC] * 2, (keep, got), us=0.5, behind=behind)[0]
+    return order.call(join_kernel, "join", [shape], [VMEM_SPEC] * 2, (keep, got), us=us, behind=behind)[0]
+
+
+def wait_kernel(out):
+    out[...] = jnp.zeros(out.shape, out.dtype)
+
+
+def wait(order, *arrays):
+    order.call(wait_kernel, "wait", [jax.ShapeDtypeStruct((8, 128), jnp.float32)], [], (), us=0.5, behind=arrays)
 
 
 def last_kernel(keep, got, *refs):
@@ -292,17 +300,21 @@
     w2 = (w_in2, w_out2, r_in2, r_out2)
 
     y0, y1, y2, y3 = (across(x) for x in (x0, x1, x2, x3))
-    give, keep0 = block(order, idx2, x0, y0, gain, w2)
+    give, keep0 = block(order, idx2, x0, y0, gain, w2, us=1)
     got0 = across(give)
     low = mirror(x0, x1)
-    give, keep1 = block(order, idx2, x1, y1, gain, w2, behind=(x2,))
+    give, keep1 = block(order, idx2, x1, y1, gain, w2, behind=(x2,), us=1)
     got1 = across(give)
     high = mirror(x2, x3)
-    give, keep2 = block(order, idx2, x2, y2, gain, w2, behind=(y3,))
+    give, keep2 = block(order, idx2, x2, y2, gain, w2, us=1)
     got2 = across(give)
-    give, keep3 = block(order, idx2, x3, y3, gain, w2)
+    give, keep3 = block(order, idx2, x3, y3, gain, w2, us=1)
     got3 = across(give)
-    done = [join(order, keep0, got0), join(order, keep1, got1, (low,)), join(order, keep2, got2)]
+    done = [join(order, keep0, got0, us=3)]
+    wait(order, low)
+    done.append(join(order, keep1, got1, us=3))
+    wait(order, high)
+    done.append(join(order, keep2, got2, us=3))
     stash = whole(order, pack_kernel, "pack", (low[0], high[0]), rows)
     return whole(order, last_kernel, "last", (keep3, got3, *done), rows), stash
 

time: 107 us -> 103 us (0.963)
  waiting for transfers between devices: 25.7 us -> 19.7 us
  Pallas kernels: 47.6 us -> 48.7 us
    ppermute x23, waiting for transfers between devices: 25.7 us -> 19.7 us  [route(): return lax.ppermute(x, AXES, pairs)]
    pallas_call x24 -> x26, Pallas kernels: 47.6 us -> 48.7 us  [call(): pl.pallas_call(with_token, out_shape=tuple(outs) + (jax.ShapeDtypeStruct(...]
  transfers between devices with their start and end apart: 23 -> 23, of which waited for: 8 -> 6; matrix products, arithmetic and copies ran while one was open for 1% -> 1% of each run, Pallas kernels for 43% -> 47%
where the time goes in v3:
time: 103 us; the launch traced here: 102 us
  Pallas kernels  48.7 us (47%)
  starting transfers between devices  30.4 us (30%)
  waiting for transfers between devices  19.7 us (19%)
  between operations  2.19 us (2%)
  local copies, waits for them, and re-layouts  1.28 us (1%)
    pallas_call x26, Pallas kernels, call(): pl.pallas_call(with_token, out_shape=tuple(outs) + (jax.ShapeDtypeStruct(...  48.7 us
    ppermute x23, starting transfers between devices, route(): return lax.ppermute(x, AXES, pairs)  30.4 us
    ppermute x23, waiting for transfers between devices, route(): return lax.ppermute(x, AXES, pairs)  19.7 us
  transfers between devices with their start and end apart: 23, of which 6 were waited for; matrix products, arithmetic and copies ran while one was open for 1% of the time, Pallas kernels for 47%

profile of v3, /device:TPU:0, one launch (start us, length us, event | category | flops | bytes accessed | tf_op | source)
XLA Modules:
  0.0 102.5 jit_solution(12241299632889537977)
XLA Ops:
  2.5 1.7 %collective-permute-start.4 = (bf16[128,2048]{1,0:T(8,128)(2,1)S(1)}, bf16[128,2048]{1,0:T(8,128)(2,1)S(1)}, u32[]{:S(2)}, u32[]{:S(2)}) collective-permute-start(bf16[128,2048]{1,0:T(8,128)(2,1)S(1)} %get-tuple-element.124.refs_1_), channel_id=1, source_target_pairs={{0,2},{1,3},{2,0},{3,1},{4,6},{5,7},{6,4},{7,5},{8,10},{9,11},{10,... | collective-permute-start | bytes 1572872 | tf_op jit(solution)/shard_map/ppermute | solution.py:25
  7.0 6.9 %collective-permute-done = s32[1]{0:T(128)} collective-permute-done((s32[1]{0:T(128)}, s32[1]{0:T(128)}, u32[]{:S(2)}, u32[]{:S(2)}) %collective-permute-start) | collective-permute-done | bytes 36 | tf_op jit(solution)/shard_map/ppermute | solution.py:25
  14.6 4.7 %pick_group.4 = (bf16[2048,1024]{1,0:T(8,128)(2,1)S(1)}, bf16[1024,2048]{1,0:T(8,128)(2,1)S(1)}, bf16[2048,1024]{1,0:T(8,128)(2,1)S(1)}, f32[8,128]{1,0:T(8,128)S(1)}) custom-call(s32[1]{0:T(128)S(6)} %copy.7.refs_0_, bf16[1,2,2048,1024]{3,2,1,0:T(8,128)(2,1)} %refs_1_.3, bf16[1,2,1024,2048]{3,2,1,0:T(8,128)(2,1)} %refs_2_.3, ...), custom_call_target="tpu_custom_call" | custom-call | flops 5864999936 | bytes 16384 | tf_op jit(solution)/shard_map/pick_group/pallas_call | solution.py:65
  19.3 4.0 %up.1 = (bf16[256,2048]{1,0:T(8,128)(2,1)S(1)}, f32[8,128]{1,0:T(8,128)S(1)}) custom-call(s32[2]{0:T(128)S(1)} %pad_add_fusion.1.refs_0_, bf16[128,2048]{1,0:T(8,128)(2,1)S(1)} %get-tuple-element.124.refs_1_, bf16[128,2048]{1,0:T(8,128)(2,1)S(1)} %collective-permute-done.4.refs_2_, bf16[1,2,2048]{2,1,0:T(2,128)(2,1)S(1)} %copy-done, ...), custom_call_target="tpu_custom_call" | custom-call | flops 3449999872 | bytes 16384 | tf_op jit(solution)/shard_map/up/pallas_call | solution.py:65
  23.3 2.9 %collective-permute-done.3.refs_1_.refs_2_ = bf16[1,2,1024,2048]{3,2,1,0:T(8,128)(2,1)} collective-permute-done((bf16[1,2,1024,2048]{3,2,1,0:T(8,128)(2,1)}, bf16[1,2,1024,2048]{3,2,1,0:T(8,128)(2,1)}, u32[]{:S(2)}, u32[]{:S(2)}) %collective-permute-start.3) | collective-permute-done | bytes 8388640 | tf_op jit(solution)/shard_map/ppermute | solution.py:25
  26.2 2.2 %pick_group.5 = (bf16[1024,2048]{1,0:T(8,128)(2,1)S(1)}, f32[8,128]{1,0:T(8,128)S(1)}) custom-call(s32[1]{0:T(128)S(6)} %copy.7.refs_0_, bf16[1,2,1024,2048]{3,2,1,0:T(8,128)(2,1)} %collective-permute-done.3.refs_1_.refs_2_, f32[8,128]{1,0:T(8,128)S(1)} %get-tuple-element.67.refs_2_), custom_call_target="tpu_custom_call" | custom-call | flops 1955000064 | bytes 16384 | tf_op jit(solution)/shard_map/pick_group/pallas_call | solution.py:65
  28.4 1.8 %down.2 = (bf16[64,2048]{1,0:T(8,128)(2,1)S(1)}, f32[64,2048]{1,0:T(8,128)S(1)}, f32[8,128]{1,0:T(8,128)S(1)}) custom-call(s32[2]{0:T(128)S(1)} %pad_add_fusion.1.refs_0_, bf16[128,2048]{1,0:T(8,128)(2,1)S(1)} %get-tuple-element.124.refs_1_, bf16[128,2048]{1,0:T(8,128)(2,1)S(1)} %collective-permute-done.4.refs_2_, ...), custom_call_target="tpu_custom_call" | custom-call | flops 2300000000 | bytes 16384 | tf_op jit(solution)/shard_map/down/pallas_call | solution.py:65
  30.3 1.6 %collective-permute-start.5 = (bf16[64,2048]{1,0:T(8,128)(2,1)S(1)}, bf16[64,2048]{1,0:T(8,128)(2,1)S(1)}, u32[]{:S(2)}, u32[]{:S(2)}) collective-permute-start(bf16[64,2048]{1,0:T(8,128)(2,1)S(1)} %get-tuple-element.72), channel_id=1, source_target_pairs={{0,2},{1,3},{2,0},{3,1},{4,6},{5,7},{6,4},{7,5},{8,10},{9,11},{10,... | collective-permute-start | bytes 786440 | tf_op jit(solution)/shard_map/ppermute | solution.py:25
  31.9 1.8 %down.3 = (bf16[64,2048]{1,0:T(8,128)(2,1)S(1)}, f32[64,2048]{1,0:T(8,128)S(1)}, f32[8,128]{1,0:T(8,128)S(1)}) custom-call(s32[2]{0:T(128)S(1)} %pad_add_fusion.1.refs_0_, bf16[128,2048]{1,0:T(8,128)(2,1)S(1)} %get-tuple-element.124.refs_1_, bf16[128,2048]{1,0:T(8,128)(2,1)S(1)} %collective-permute-done.4.refs_2_, ...), custom_call_target="tpu_custom_call" | custom-call | flops 2300000000 | bytes 16384 | tf_op jit(solution)/shard_map/down/pallas_call | solution.py:65
  34.3 3.9 %block.6 = (bf16[64,2048]{1,0:T(8,128)(2,1)S(1)}, f32[64,2048]{1,0:T(8,128)S(1)}, f32[8,128]{1,0:T(8,128)S(1)}) custom-call(s32[2]{0:T(128)S(1)} %pad_add_fusion.1.refs_0_, bf16[128,2048]{1,0:T(8,128)(2,1)S(1)} %get-tuple-element.125.refs_1_, bf16[128,2048]{1,0:T(8,128)(2,1)S(1)} %collective-permute-done.1.refs_7_.refs_2_, bf16[1,2,2048]{2,1,0:T(2,128)(2,1)S(1)} %copy-done, ...), custom_call_target="tpu_custom_call" | custom-call | flops 4600000000 | bytes 16384 | tf_op jit(solution)/shard_map/block/pallas_call | solution.py:65
  38.2 1.6 %collective-permute-start.7 = (bf16[64,2048]{1,0:T(8,128)(2,1)S(1)}, bf16[64,2048]{1,0:T(8,128)(2,1)S(1)}, u32[]{:S(2)}, u32[]{:S(2)}) collective-permute-start(bf16[64,2048]{1,0:T(8,128)(2,1)S(1)} %get-tuple-element.80), channel_id=1, source_target_pairs={{0,2},{1,3},{2,0},{3,1},{4,6},{5,7},{6,4},{7,5},{8,10},{9,11},{10,... | collective-permute-start | bytes 786440 | tf_op jit(solution)/shard_map/ppermute | solution.py:25
  39.9 1.8 %collective-permute-start.9 = (bf16[64,2048]{1,0:T(8,128)(2,1)S(1)}, bf16[64,2048]{1,0:T(8,128)(2,1)S(1)}, u32[]{:S(2)}, u32[]{:S(2)}) collective-permute-start(bf16[64,2048]{1,0:T(8,128)(2,1)S(1)} %get-tuple-element.87), channel_id=1, source_target_pairs={{0,4},{1,5},{2,6},{3,7},{4,8},{5,9},{6,10},{7,11},{8,12},{9,13},{1... | collective-permute-start | bytes 786440 | tf_op jit(solution)/shard_map/ppermute | solution.py:25
  41.8 3.9 %block.7 = (bf16[64,2048]{1,0:T(8,128)(2,1)S(1)}, f32[64,2048]{1,0:T(8,128)S(1)}, f32[8,128]{1,0:T(8,128)S(1)}) custom-call(s32[2]{0:T(128)S(1)} %pad_add_fusion.1.refs_0_, bf16[128,2048]{1,0:T(8,128)(2,1)S(1)} %get-tuple-element.125.refs_1_, bf16[128,2048]{1,0:T(8,128)(2,1)S(1)} %collective-permute-done.1.refs_7_.refs_2_, bf16[1,2,2048]{2,1,0:T(2,128)(2,1)S(1)} %copy-done, ...), custom_call_target="tpu_custom_call" | custom-call | flops 4600000000 | bytes 16384 | tf_op jit(solution)/shard_map/block/pallas_call | solution.py:65
  48.6 3.5 %pick_group.6 = (bf16[2048,1024]{1,0:T(8,128)(2,1)S(1)}, bf16[1024,2048]{1,0:T(8,128)(2,1)S(1)}, f32[8,128]{1,0:T(8,128)S(1)}) custom-call(s32[1]{0:T(128)} %bitcast.1.refs_8_.refs_0_, bf16[1,2,2048,1024]{3,2,1,0:T(8,128)(2,1)} %refs_1_.3, bf16[1,2,1024,2048]{3,2,1,0:T(8,128)(2,1)} %refs_2_.3, f32[8,128]{1,0:T(8,128)S(1)} %get-tuple-element.84.refs_3_), custom_call_target="tpu_custom_call" | custom-call | flops 3910000128 | bytes 16384 | tf_op jit(solution)/shard_map/pick_group/pallas_call | solution.py:65
  55.5 3.5 %pick_group.7 = (bf16[2048,1024]{1,0:T(8,128)(2,1)S(1)}, bf16[1024,2048]{1,0:T(8,128)(2,1)S(1)}, f32[8,128]{1,0:T(8,128)S(1)}) custom-call(s32[1]{0:T(128)} %bitcast.1.refs_8_.refs_0_, bf16[1,2,2048,1024]{3,2,1,0:T(8,128)(2,1)} %collective-permute-done.2.refs_3_.refs_1_, bf16[1,2,1024,2048]{3,2,1,0:T(8,128)(2,1)} %collective-permute-done.3.refs_1_.refs_2_, ...), custom_call_target="tpu_custom_call" | custom-call | flops 3910000128 | bytes 16384 | tf_op jit(solution)/shard_map/pick_group/pallas_call | solution.py:65
  61.4 3.8 %collective-permute-done.13.refs_9_.refs_0_.refs_1_ = bf16[64,2048]{1,0:T(8,128)(2,1)S(1)} collective-permute-done((bf16[64,2048]{1,0:T(8,128)(2,1)S(1)}, bf16[64,2048]{1,0:T(8,128)(2,1)S(1)}, u32[]{:S(2)}, u32[]{:S(2)}) %collective-permute-start.13) | collective-permute-done | bytes 262176 | tf_op jit(solution)/shard_map/ppermute | solution.py:25
  65.8 3.9 %block.8 = (bf16[64,2048]{1,0:T(8,128)(2,1)S(1)}, f32[64,2048]{1,0:T(8,128)S(1)}, f32[8,128]{1,0:T(8,128)S(1)}) custom-call(s32[2]{0:T(128)S(1)} %pad_add_fusion.refs_0_, bf16[64,2048]{1,0:T(8,128)(2,1)S(1)} %collective-permute-done.9.refs_4_.refs_1_.refs_0_, bf16[64,2048]{1,0:T(8,128)(2,1)S(1)} %collective-permute-done.16.refs_2_, ...), custom_call_target="tpu_custom_call" | custom-call | flops 1150000000 | bytes 16384 | tf_op jit(solution)/shard_map/block/pallas_call | solution.py:65
  71.3 4.4 %collective-permute-start.20 = (bf16[1,128,2048]{2,1,0:T(8,128)(2,1)S(1)}, bf16[1,128,2048]{2,1,0:T(8,128)(2,1)S(1)}, u32[]{:S(2)}, u32[]{:S(2)}) collective-permute-start(bf16[1,128,2048]{2,1,0:T(8,128)(2,1)S(1)} %get-tuple-element.111), channel_id=1, source_target_pairs={{0,126},{1,127},{2,124},{3,125},{4,122},{5,123},{6,120},{7,121},{8... | collective-permute-start | bytes 1572872 | tf_op jit(solution)/shard_map/ppermute | solution.py:25
  76.3 3.9 %block.9 = (bf16[64,2048]{1,0:T(8,128)(2,1)S(1)}, f32[64,2048]{1,0:T(8,128)S(1)}, f32[8,128]{1,0:T(8,128)S(1)}) custom-call(s32[2]{0:T(128)S(1)} %pad_add_fusion.refs_0_, bf16[64,2048]{1,0:T(8,128)(2,1)S(1)} %collective-permute-done.10.refs_3_.refs_1_, bf16[64,2048]{1,0:T(8,128)(2,1)S(1)} %collective-permute-done.15.refs_2_, ...), custom_call_target="tpu_custom_call" | custom-call | flops 1150000000 | bytes 16384 | tf_op jit(solution)/shard_map/block/pallas_call | solution.py:65
  81.7 3.2 %collective-permute-start.22 = (bf16[1,128,2048]{2,1,0:T(8,128)(2,1)S(1)}, bf16[1,128,2048]{2,1,0:T(8,128)(2,1)S(1)}, u32[]{:S(2)}, u32[]{:S(2)}) collective-permute-start(bf16[1,128,2048]{2,1,0:T(8,128)(2,1)S(1)} %get-tuple-element.117), channel_id=1, source_target_pairs={{0,126},{1,127},{2,124},{3,125},{4,122},{5,123},{6,120},{7,121},{8... | collective-permute-start | bytes 1572872 | tf_op jit(solution)/shard_map/ppermute | solution.py:25
  84.9 3.9 %block.10 = (bf16[64,2048]{1,0:T(8,128)(2,1)S(1)}, f32[64,2048]{1,0:T(8,128)S(1)}, f32[8,128]{1,0:T(8,128)S(1)}) custom-call(s32[2]{0:T(128)S(1)} %pad_add_fusion.refs_0_, bf16[64,2048]{1,0:T(8,128)(2,1)S(1)} %collective-permute-done.13.refs_9_.refs_0_.refs_1_, bf16[64,2048]{1,0:T(8,128)(2,1)S(1)} %collective-permute-done.14.refs_2_, ...), custom_call_target="tpu_custom_call" | custom-call | flops 1150000000 | bytes 16384 | tf_op jit(solution)/shard_map/block/pallas_call | solution.py:65
  89.0 3.9 %block.11 = (bf16[64,2048]{1,0:T(8,128)(2,1)S(1)}, f32[64,2048]{1,0:T(8,128)S(1)}, f32[8,128]{1,0:T(8,128)S(1)}) custom-call(s32[2]{0:T(128)S(1)} %pad_add_fusion.refs_0_, bf16[64,2048]{1,0:T(8,128)(2,1)S(1)} %collective-permute-done.11.refs_1_, bf16[64,2048]{1,0:T(8,128)(2,1)S(1)} %collective-permute-done.12.refs_2_, bf16[1,2,2048]{2,1,0:T(2,128)(2,1)S(1)} %copy-done, ...), custom_call_target="tpu_custom_call" | custom-call | flops 1150000000 | bytes 16384 | tf_op jit(solution)/shard_map/block/pallas_call | solution.py:65
  92.9 2.1 %collective-permute-start.17 = (bf16[64,2048]{1,0:T(8,128)(2,1)S(1)}, bf16[64,2048]{1,0:T(8,128)(2,1)S(1)}, u32[]{:S(2)}, u32[]{:S(2)}) collective-permute-start(bf16[64,2048]{1,0:T(8,128)(2,1)S(1)} %get-tuple-element.103), channel_id=1, source_target_pairs={{0,2},{1,3},{2,0},{3,1},{4,6},{5,7},{6,4},{7,5},{8,10},{9,11},{10,... | collective-permute-start | bytes 786440 | tf_op jit(solution)/shard_map/ppermute | solution.py:25
  95.7 4.0 %collective-permute-done.22.refs_1_ = bf16[1,128,2048]{2,1,0:T(8,128)(2,1)S(1)} collective-permute-done((bf16[1,128,2048]{2,1,0:T(8,128)(2,1)S(1)}, bf16[1,128,2048]{2,1,0:T(8,128)(2,1)S(1)}, u32[]{:S(2)}, u32[]{:S(2)}) %collective-permute-start.22) | collective-permute-done | bytes 524320 | tf_op jit(solution)/shard_map/ppermute | solution.py:25
  (54 shorter events, 21.2 us)
Async XLA Ops:
  0.6 13.9 %collective-permute-start.2 = (bf16[1,2,2048,1024]{3,2,1,0:T(8,128)(2,1)}, bf16[1,2,2048,1024]{3,2,1,0:T(8,128)(2,1)}, u32[]{:S(2)}, u32[]{:S(2)}) collective-permute-start(bf16[1,2,2048,1024]{3,2,1,0:T(8,128)(2,1)} %refs_1_.3), channel_id=1, source_target_pairs={{0,1},{1,0},{2,3},{3,2},{4,5},{5,4},{6,7},{7,6},{8,9},{9,8},{10,11... | collective-permute-start | bytes 25165832 | tf_op jit(solution)/shard_map/ppermute | solution.py:25
  0.7 25.5 %collective-permute-start.3 = (bf16[1,2,1024,2048]{3,2,1,0:T(8,128)(2,1)}, bf16[1,2,1024,2048]{3,2,1,0:T(8,128)(2,1)}, u32[]{:S(2)}, u32[]{:S(2)}) collective-permute-start(bf16[1,2,1024,2048]{3,2,1,0:T(8,128)(2,1)} %refs_2_.3), channel_id=1, source_target_pairs={{0,1},{1,0},{2,3},{3,2},{4,5},{5,4},{6,7},{7,6},{8,9},{9,8},{10,11... | collective-permute-start | bytes 25165832 | tf_op jit(solution)/shard_map/ppermute | solution.py:25
  2.5 16.8 %collective-permute-start.4 = (bf16[128,2048]{1,0:T(8,128)(2,1)S(1)}, bf16[128,2048]{1,0:T(8,128)(2,1)S(1)}, u32[]{:S(2)}, u32[]{:S(2)}) collective-permute-start(bf16[128,2048]{1,0:T(8,128)(2,1)S(1)} %get-tuple-element.124.refs_1_), channel_id=1, source_target_pairs={{0,2},{1,3},{2,0},{3,1},{4,6},{5,7},{6,4},{7,5},{8,10},{9,11},{10,... | collective-permute-start | bytes 1572872 | tf_op jit(solution)/shard_map/ppermute | solution.py:25
  4.1 9.8 %collective-permute-start = (s32[1]{0:T(128)}, s32[1]{0:T(128)}, u32[]{:S(2)}, u32[]{:S(2)}) collective-permute-start(s32[1]{0:T(128)} %param.6), channel_id=1, source_target_pairs={{0,4},{1,5},{2,6},{3,7},{4,8},{5,9},{6,10},{7,11},{8,12},{9,13},{1... | collective-permute-start | bytes 20 | tf_op jit(solution)/shard_map/ppermute | solution.py:25
  5.7 26.2 %collective-permute-start.1 = (bf16[128,2048]{1,0:T(8,128)(2,1)S(1)}, bf16[128,2048]{1,0:T(8,128)(2,1)S(1)}, u32[]{:S(2)}, u32[]{:S(2)}) collective-permute-start(bf16[128,2048]{1,0:T(8,128)(2,1)S(1)} %get-tuple-element.125.refs_1_), channel_id=1, source_target_pairs={{0,2},{1,3},{2,0},{3,1},{4,6},{5,7},{6,4},{7,5},{8,10},{9,11},{10,... | collective-permute-start | bytes 1572872 | tf_op jit(solution)/shard_map/ppermute | solution.py:25
  14.6 4.7 %copy-start = (bf16[1,2,2048]{2,1,0:T(2,128)(2,1)S(1)}, bf16[1,2,2048]{2,1,0:T(2,128)(2,1)}, u32[]{:S(2)}) copy-start(bf16[1,2,2048]{2,1,0:T(2,128)(2,1)} %refs_3_.13) | copy-start | bytes 24580
  30.3 9.6 %collective-permute-start.5 = (bf16[64,2048]{1,0:T(8,128)(2,1)S(1)}, bf16[64,2048]{1,0:T(8,128)(2,1)S(1)}, u32[]{:S(2)}, u32[]{:S(2)}) collective-permute-start(bf16[64,2048]{1,0:T(8,128)(2,1)S(1)} %get-tuple-element.72), channel_id=1, source_target_pairs={{0,2},{1,3},{2,0},{3,1},{4,6},{5,7},{6,4},{7,5},{8,10},{9,11},{10,... | collective-permute-start | bytes 786440 | tf_op jit(solution)/shard_map/ppermute | solution.py:25
  33.8 11.9 %collective-permute-start.8 = (bf16[64,2048]{1,0:T(8,128)(2,1)S(1)}, bf16[64,2048]{1,0:T(8,128)(2,1)S(1)}, u32[]{:S(2)}, u32[]{:S(2)}) collective-permute-start(bf16[64,2048]{1,0:T(8,128)(2,1)S(1)} %get-tuple-element.82), channel_id=1, source_target_pairs={{0,2},{1,3},{2,0},{3,1},{4,6},{5,7},{6,4},{7,5},{8,10},{9,11},{10,... | collective-permute-start | bytes 786440 | tf_op jit(solution)/shard_map/ppermute | solution.py:25
  38.2 13.8 %collective-permute-start.7 = (bf16[64,2048]{1,0:T(8,128)(2,1)S(1)}, bf16[64,2048]{1,0:T(8,128)(2,1)S(1)}, u32[]{:S(2)}, u32[]{:S(2)}) collective-permute-start(bf16[64,2048]{1,0:T(8,128)(2,1)S(1)} %get-tuple-element.80), channel_id=1, source_target_pairs={{0,2},{1,3},{2,0},{3,1},{4,6},{5,7},{6,4},{7,5},{8,10},{9,11},{10,... | collective-permute-start | bytes 786440 | tf_op jit(solution)/shard_map/ppermute | solution.py:25
  39.9 14.6 %collective-permute-start.9 = (bf16[64,2048]{1,0:T(8,128)(2,1)S(1)}, bf16[64,2048]{1,0:T(8,128)(2,1)S(1)}, u32[]{:S(2)}, u32[]{:S(2)}) collective-permute-start(bf16[64,2048]{1,0:T(8,128)(2,1)S(1)} %get-tuple-element.87), channel_id=1, source_target_pairs={{0,4},{1,5},{2,6},{3,7},{4,8},{5,9},{6,10},{7,11},{8,12},{9,13},{1... | collective-permute-start | bytes 786440 | tf_op jit(solution)/shard_map/ppermute | solution.py:25
  45.8 14.3 %collective-permute-start.10 = (bf16[64,2048]{1,0:T(8,128)(2,1)S(1)}, bf16[64,2048]{1,0:T(8,128)(2,1)S(1)}, u32[]{:S(2)}, u32[]{:S(2)}) collective-permute-start(bf16[64,2048]{1,0:T(8,128)(2,1)S(1)} %get-tuple-element.89), channel_id=1, source_target_pairs={{0,4},{1,5},{2,6},{3,7},{4,8},{5,9},{6,10},{7,11},{8,12},{9,13},{1... | collective-permute-start | bytes 786440 | tf_op jit(solution)/shard_map/ppermute | solution.py:25
  47.4 12.7 %collective-permute-start.6 = (bf16[64,2048]{1,0:T(8,128)(2,1)S(1)}, bf16[64,2048]{1,0:T(8,128)(2,1)S(1)}, u32[]{:S(2)}, u32[]{:S(2)}) collective-permute-start(bf16[64,2048]{1,0:T(8,128)(2,1)S(1)} %get-tuple-element.78), channel_id=1, source_target_pairs={{0,2},{1,3},{2,0},{3,1},{4,6},{5,7},{6,4},{7,5},{8,10},{9,11},{10,... | collective-permute-start | bytes 786440 | tf_op jit(solution)/shard_map/ppermute | solution.py:25
  52.1 13.1 %collective-permute-start.13 = (bf16[64,2048]{1,0:T(8,128)(2,1)S(1)}, bf16[64,2048]{1,0:T(8,128)(2,1)S(1)}, u32[]{:S(2)}, u32[]{:S(2)}) collective-permute-start(bf16[64,2048]{1,0:T(8,128)(2,1)S(1)} %get-tuple-element.95), channel_id=1, source_target_pairs={{0,4},{1,5},{2,6},{3,7},{4,8},{5,9},{6,10},{7,11},{8,12},{9,13},{1... | collective-permute-start | bytes 786440 | tf_op jit(solution)/shard_map/ppermute | solution.py:25
  54.5 11.3 %collective-permute-start.16 = (bf16[64,2048]{1,0:T(8,128)(2,1)S(1)}, bf16[64,2048]{1,0:T(8,128)(2,1)S(1)}, u32[]{:S(2)}, u32[]{:S(2)}) collective-permute-start(bf16[64,2048]{1,0:T(8,128)(2,1)S(1)} %collective-permute-done.9.refs_4_.refs_1_.refs_0_), channel_id=1, source_target_pairs={{0,2},{1,3},{2,0},{3,1},{4,6},{5,7},{6,4},{7,5},{8,10},{9,11},{10,... | collective-permute-start | bytes 786440 | tf_op jit(solution)/shard_map/ppermute | solution.py:25
  60.1 15.5 %collective-permute-start.11 = (bf16[64,2048]{1,0:T(8,128)(2,1)S(1)}, bf16[64,2048]{1,0:T(8,128)(2,1)S(1)}, u32[]{:S(2)}, u32[]{:S(2)}) collective-permute-start(bf16[64,2048]{1,0:T(8,128)(2,1)S(1)} %get-tuple-element.90), channel_id=1, source_target_pairs={{0,4},{1,5},{2,6},{3,7},{4,8},{5,9},{6,10},{7,11},{8,12},{9,13},{1... | collective-permute-start | bytes 786440 | tf_op jit(solution)/shard_map/ppermute | solution.py:25
  60.2 16.0 %collective-permute-start.15 = (bf16[64,2048]{1,0:T(8,128)(2,1)S(1)}, bf16[64,2048]{1,0:T(8,128)(2,1)S(1)}, u32[]{:S(2)}, u32[]{:S(2)}) collective-permute-start(bf16[64,2048]{1,0:T(8,128)(2,1)S(1)} %collective-permute-done.10.refs_3_.refs_1_), channel_id=1, source_target_pairs={{0,2},{1,3},{2,0},{3,1},{4,6},{5,7},{6,4},{7,5},{8,10},{9,11},{10,... | collective-permute-start | bytes 786440 | tf_op jit(solution)/shard_map/ppermute | solution.py:25
  65.2 16.5 %collective-permute-start.14 = (bf16[64,2048]{1,0:T(8,128)(2,1)S(1)}, bf16[64,2048]{1,0:T(8,128)(2,1)S(1)}, u32[]{:S(2)}, u32[]{:S(2)}) collective-permute-start(bf16[64,2048]{1,0:T(8,128)(2,1)S(1)} %collective-permute-done.13.refs_9_.refs_0_.refs_1_), channel_id=1, source_target_pairs={{0,2},{1,3},{2,0},{3,1},{4,6},{5,7},{6,4},{7,5},{8,10},{9,11},{10,... | collective-permute-start | bytes 786440 | tf_op jit(solution)/shard_map/ppermute | solution.py:25
  69.7 23.2 %collective-permute-start.18 = (bf16[64,2048]{1,0:T(8,128)(2,1)S(1)}, bf16[64,2048]{1,0:T(8,128)(2,1)S(1)}, u32[]{:S(2)}, u32[]{:S(2)}) collective-permute-start(bf16[64,2048]{1,0:T(8,128)(2,1)S(1)} %get-tuple-element.105), channel_id=1, source_target_pairs={{0,2},{1,3},{2,0},{3,1},{4,6},{5,7},{6,4},{7,5},{8,10},{9,11},{10,... | collective-permute-start | bytes 786440 | tf_op jit(solution)/shard_map/ppermute | solution.py:25
  71.3 23.8 %collective-permute-start.20 = (bf16[1,128,2048]{2,1,0:T(8,128)(2,1)S(1)}, bf16[1,128,2048]{2,1,0:T(8,128)(2,1)S(1)}, u32[]{:S(2)}, u32[]{:S(2)}) collective-permute-start(bf16[1,128,2048]{2,1,0:T(8,128)(2,1)S(1)} %get-tuple-element.111), channel_id=1, source_target_pairs={{0,126},{1,127},{2,124},{3,125},{4,122},{5,123},{6,120},{7,121},{8... | collective-permute-start | bytes 1572872 | tf_op jit(solution)/shard_map/ppermute | solution.py:25
  75.7 13.2 %collective-permute-start.12 = (bf16[64,2048]{1,0:T(8,128)(2,1)S(1)}, bf16[64,2048]{1,0:T(8,128)(2,1)S(1)}, u32[]{:S(2)}, u32[]{:S(2)}) collective-permute-start(bf16[64,2048]{1,0:T(8,128)(2,1)S(1)} %collective-permute-done.11.refs_1_), channel_id=1, source_target_pairs={{0,2},{1,3},{2,0},{3,1},{4,6},{5,7},{6,4},{7,5},{8,10},{9,11},{10,... | collective-permute-start | bytes 786440 | tf_op jit(solution)/shard_map/ppermute | solution.py:25
  80.2 15.5 %collective-permute-start.19 = (bf16[64,2048]{1,0:T(8,128)(2,1)S(1)}, bf16[64,2048]{1,0:T(8,128)(2,1)S(1)}, u32[]{:S(2)}, u32[]{:S(2)}) collective-permute-start(bf16[64,2048]{1,0:T(8,128)(2,1)S(1)} %get-tuple-element.109), channel_id=1, source_target_pairs={{0,2},{1,3},{2,0},{3,1},{4,6},{5,7},{6,4},{7,5},{8,10},{9,11},{10,... | collective-permute-start | bytes 786440 | tf_op jit(solution)/shard_map/ppermute | solution.py:25
  81.7 18.0 %collective-permute-start.22 = (bf16[1,128,2048]{2,1,0:T(8,128)(2,1)S(1)}, bf16[1,128,2048]{2,1,0:T(8,128)(2,1)S(1)}, u32[]{:S(2)}, u32[]{:S(2)}) collective-permute-start(bf16[1,128,2048]{2,1,0:T(8,128)(2,1)S(1)} %get-tuple-element.117), channel_id=1, source_target_pairs={{0,126},{1,127},{2,124},{3,125},{4,122},{5,123},{6,120},{7,121},{8... | collective-permute-start | bytes 1572872 | tf_op jit(solution)/shard_map/ppermute | solution.py:25
  88.9 11.4 %collective-permute-start.21 = (bf16[64,2048]{1,0:T(8,128)(2,1)S(1)}, bf16[64,2048]{1,0:T(8,128)(2,1)S(1)}, u32[]{:S(2)}, u32[]{:S(2)}) collective-permute-start(bf16[64,2048]{1,0:T(8,128)(2,1)S(1)} %get-tuple-element.115), channel_id=1, source_target_pairs={{0,2},{1,3},{2,0},{3,1},{4,6},{5,7},{6,4},{7,5},{8,10},{9,11},{10,... | collective-permute-start | bytes 786440 | tf_op jit(solution)/shard_map/ppermute | solution.py:25
  92.9 8.5 %collective-permute-start.17 = (bf16[64,2048]{1,0:T(8,128)(2,1)S(1)}, bf16[64,2048]{1,0:T(8,128)(2,1)S(1)}, u32[]{:S(2)}, u32[]{:S(2)}) collective-permute-start(bf16[64,2048]{1,0:T(8,128)(2,1)S(1)} %get-tuple-element.103), channel_id=1, source_target_pairs={{0,2},{1,3},{2,0},{3,1},{4,6},{5,7},{6,4},{7,5},{8,10},{9,11},{10,... | collective-permute-start | bytes 786440 | tf_op jit(solution)/shard_map/ppermute | solution.py:25

commit v4 on v3

--- a/solution.py
+++ b/solution.py
@@ -53,7 +53,7 @@
     def __init__(self):
         self.token = jnp.zeros((8, 128), jnp.float32)
 
-    def call(self, kernel, name, outs, specs, args, scratch=(), vmem=4 * MIB, us=0.1, behind=()):
+    def call(self, kernel, name, outs, specs, args, scratch=(), vmem=4 * MIB, us=0.1, behind=(), out_specs=None, aliases=None):
         vmem_spec = pl.BlockSpec(memory_space=pltpu.VMEM)
 
         def with_token(*refs):
@@ -66,7 +66,8 @@
             with_token,
             out_shape=tuple(outs) + (jax.ShapeDtypeStruct((8, 128), jnp.float32),),
             in_specs=list(specs) + [pl.BlockSpec(memory_space=pl.ANY)] * (1 + len(behind)),
-            out_specs=(vmem_spec,) * (len(outs) + 1),
+            out_specs=tuple(out_specs or (vmem_spec,) * len(outs)) + (vmem_spec,),
+            input_output_aliases=aliases or {},
             scratch_shapes=list(scratch),
             compiler_params=pltpu.CompilerParams(vmem_limit_bytes=vmem),
             cost_estimate=pl.CostEstimate(flops=int(us * 1.15e9), bytes_accessed=2**14, transcendentals=0),
@@ -195,24 +196,61 @@
     )[0]
 
 
-def down_kernel(lo, idx, own, par, hidden, w_out, r_out, give, keep):
+def base_kernel(hidden, w_out, base):
+    units = w_out.shape[0]
+    base[...] = jnp.dot(hidden[:, pl.ds(0, units)], w_out[...], preferred_element_type=jnp.float32)
+
+
+def base_rows(order, hidden, w_out):
+    shape = jax.ShapeDtypeStruct((hidden.shape[0], w_out.shape[1]), jnp.float32)
+    return order.call(base_kernel, "base", [shape], [VMEM_SPEC] * 2, (hidden, in_vmem(w_out)), vmem=8 * MIB, us=1.8)[0]
+
+
+def finish(lo, idx, own, par, total, give, keep):
     rows = give.shape[0]
-    units = w_out.shape[0]
-    mine = window(hidden, 2 * lo, 2 * rows)
-    total = jnp.dot(mine[:, pl.ds(0, units)], w_out[...], preferred_element_type=jnp.float32)
-    total += jnp.dot(mine[:, pl.ds(units, units)], r_out[...], preferred_element_type=jnp.float32)
     give[...] = total[rows:].astype(jnp.bfloat16)
     keep[...] = kept_rows(idx, window(own, lo, rows), window(par, lo, rows)) + total[:rows]
 
 
-def down(order, idx, own, par, hidden, w_out, r_out, lo, behind=()):
+def down_kernel(lo, idx, own, par, hidden, base, r_out, give, keep):
+    units = r_out.shape[0]
+    mine = pl.ds(2 * lo, 2 * give.shape[0])
+    total = base[mine, :] + jnp.dot(hidden[mine, pl.ds(units, units)], r_out[...], preferred_element_type=jnp.float32)
+    finish(lo, idx, own, par, total, give, keep)
+
+
+def down_load_kernel(lo, idx, own, par, hidden, base, r_out, give, keep, held, sems):
+    units, parts = held.shape[0], sems.shape[0]
+    step = units // parts
+    loads = []
+    for k in range(parts):
+        piece = pl.ds(k * step, step)
+        loads.append(pltpu.make_async_copy(r_out.at[0, idx[0], piece], held.at[piece], sems.at[k]))
+        loads[-1].start()
+    mine = pl.ds(2 * lo, 2 * give.shape[0])
+    total = base[mine, :]
+    cut = parts // 2
+    for half in range(2):
+        for load in loads[half * cut : (half + 1) * cut]:
+            load.wait()
+        piece = pl.ds(half * cut * step, cut * step)
+        total += jnp.dot(
+            hidden[mine, pl.ds(units + half * cut * step, cut * step)], held[piece, :], preferred_element_type=jnp.float32
+        )
+    finish(lo, idx, own, par, total, give, keep)
+
+
+def down(order, idx, own, par, hidden, base, r_out, lo, behind=()):
     d = own.shape[1]
+    loading = r_out.ndim > 2
     return order.call(
-        functools.partial(down_kernel, lo),
+        functools.partial(down_load_kernel if loading else down_kernel, lo),
         "down",
-        [jax.ShapeDtypeStruct((ROWS, d), jnp.bfloat16), jax.ShapeDtypeStruct((ROWS, d), jnp.float32)],
-        [SMEM_SPEC] + [VMEM_SPEC] * 5,
-        (idx, own, par, hidden, in_vmem(w_out), in_vmem(r_out)),
+        [jax.ShapeDtypeStruct((ROWS, d), jnp.bfloat16), jax.ShapeDtypeStruct((ROWS, d), jnp.float32)]
+        + [pltpu.VMEM(r_out.shape[2:], r_out.dtype)] * loading,
+        [SMEM_SPEC] + [VMEM_SPEC] * 4 + [HBM_SPEC if loading else VMEM_SPEC],
+        (idx, own, par, hidden, base, in_hbm(r_out) if loading else in_vmem(r_out)),
+        [pltpu.SemaphoreType.DMA((8,))] * loading,
         vmem=8 * MIB,
         us=2,
         behind=behind,
@@ -281,11 +319,11 @@
 
     ((w_in1, w_out1, r_in1),) = pick(order, (g1,), (w_in, w_out, r_in))
     hidden = up_rows(order, idx1, own[0], par[0], gain, w_in1, r_in1)
-    ((r_out1,),) = pick(order, (g1,), (r_out,))
+    base = base_rows(order, hidden, w_out1)
+    give, keep0, r_out1 = down(order, idx1, own[0], par[0], hidden, base, r_out, 0)
     w1 = (w_in1, w_out1, r_in1, r_out1)
-    give, keep0 = down(order, idx1, own[0], par[0], hidden, w_out1, r_out1, 0)
     got0 = across(give)
-    give, keep1 = down(order, idx1, own[0], par[0], hidden, w_out1, r_out1, ROWS, (par[1], g2.reshape(1)))
+    give, keep1 = down(order, idx1, own[0], par[0], hidden, base, r_out1, ROWS, (par[1], g2.reshape(1)))
     got1 = across(give)
     give, keep2 = block(order, idx1, own[1], par[1], gain, w1, 0, 0)
     got2 = across(give)

time: 103 us -> 101 us (0.981)
  waiting for transfers between devices: 19.7 us -> 17.8 us
    ppermute x23, waiting for transfers between devices: 19.7 us -> 17.8 us  [route(): return lax.ppermute(x, AXES, pairs)]
where the time goes in v4:
time: 101 us
  Pallas kernels  48.7 us (48%)
  starting transfers between devices  30.7 us (30%)
  waiting for transfers between devices  17.8 us (18%)
  between operations  2.18 us (2%)
  local copies, waits for them, and re-layouts  1.28 us (1%)
    pallas_call x26, Pallas kernels, call(): pl.pallas_call(with_token, out_shape=tuple(outs) + (jax.ShapeDtypeStruct(...  48.7 us
    ppermute x23, starting transfers between devices, route(): return lax.ppermute(x, AXES, pairs)  30.7 us
    ppermute x23, waiting for transfers between devices, route(): return lax.ppermute(x, AXES, pairs)  17.8 us
  transfers between devices with their start and end apart: 23, of which 6 were waited for; matrix products, arithmetic and copies ran while one was open for 1% of the time, Pallas kernels for 47%

profile of v4, /device:TPU:0, one launch (start us, length us, event | category | flops | bytes accessed | tf_op | source)
XLA Modules:
  0.0 100.8 jit_solution(7964380174624181063)
XLA Ops:
  2.5 1.7 %collective-permute-start.3 = (bf16[128,2048]{1,0:T(8,128)(2,1)S(1)}, bf16[128,2048]{1,0:T(8,128)(2,1)S(1)}, u32[]{:S(2)}, u32[]{:S(2)}) collective-permute-start(bf16[128,2048]{1,0:T(8,128)(2,1)S(1)} %get-tuple-element.126.refs_1_), channel_id=1, source_target_pairs={{0,2},{1,3},{2,0},{3,1},{4,6},{5,7},{6,4},{7,5},{8,10},{9,11},{10,... | collective-permute-start | bytes 1572872 | tf_op jit(solution)/shard_map/ppermute | solution.py:25
  4.1 1.6 %collective-permute-start = (s32[1]{0:T(128)}, s32[1]{0:T(128)}, u32[]{:S(2)}, u32[]{:S(2)}) collective-permute-start(s32[1]{0:T(128)} %param.6), channel_id=1, source_target_pairs={{0,4},{1,5},{2,6},{3,7},{4,8},{5,9},{6,10},{7,11},{8,12},{9,13},{1... | collective-permute-start | bytes 20 | tf_op jit(solution)/shard_map/ppermute | solution.py:25
  7.0 6.9 %collective-permute-done = s32[1]{0:T(128)} collective-permute-done((s32[1]{0:T(128)}, s32[1]{0:T(128)}, u32[]{:S(2)}, u32[]{:S(2)}) %collective-permute-start) | collective-permute-done | bytes 36 | tf_op jit(solution)/shard_map/ppermute | solution.py:25
  14.6 4.7 %pick_group.3 = (bf16[2048,1024]{1,0:T(8,128)(2,1)S(1)}, bf16[1024,2048]{1,0:T(8,128)(2,1)S(1)}, bf16[2048,1024]{1,0:T(8,128)(2,1)S(1)}, f32[8,128]{1,0:T(8,128)S(1)}) custom-call(s32[1]{0:T(128)S(6)} %copy.7.refs_0_, bf16[1,2,2048,1024]{3,2,1,0:T(8,128)(2,1)} %refs_1_.3, bf16[1,2,1024,2048]{3,2,1,0:T(8,128)(2,1)} %refs_2_.3, ...), custom_call_target="tpu_custom_call" | custom-call | flops 5864999936 | bytes 16384 | tf_op jit(solution)/shard_map/pick_group/pallas_call | solution.py:65
  19.3 4.0 %up.1 = (bf16[256,2048]{1,0:T(8,128)(2,1)S(1)}, f32[8,128]{1,0:T(8,128)S(1)}) custom-call(s32[2]{0:T(128)S(1)} %pad_add_fusion.1.refs_0_, bf16[128,2048]{1,0:T(8,128)(2,1)S(1)} %get-tuple-element.126.refs_1_, bf16[128,2048]{1,0:T(8,128)(2,1)S(1)} %collective-permute-done.3.refs_2_, bf16[1,2,2048]{2,1,0:T(2,128)(2,1)S(1)} %copy-done, ...), custom_call_target="tpu_custom_call" | custom-call | flops 3449999872 | bytes 16384 | tf_op jit(solution)/shard_map/up/pallas_call | solution.py:65
  24.6 1.6 %collective-permute-done.4.refs_5_.refs_2_ = bf16[1,2,1024,2048]{3,2,1,0:T(8,128)(2,1)} collective-permute-done((bf16[1,2,1024,2048]{3,2,1,0:T(8,128)(2,1)}, bf16[1,2,1024,2048]{3,2,1,0:T(8,128)(2,1)}, u32[]{:S(2)}, u32[]{:S(2)}) %collective-permute-start.4) | collective-permute-done | bytes 8388640 | tf_op jit(solution)/shard_map/ppermute | solution.py:25
  26.2 3.2 %down.2 = (bf16[64,2048]{1,0:T(8,128)(2,1)S(1)}, f32[64,2048]{1,0:T(8,128)S(1)}, bf16[1024,2048]{1,0:T(8,128)(2,1)S(1)}, f32[8,128]{1,0:T(8,128)S(1)}) custom-call(s32[2]{0:T(128)S(1)} %pad_add_fusion.1.refs_0_, bf16[128,2048]{1,0:T(8,128)(2,1)S(1)} %get-tuple-element.126.refs_1_, bf16[128,2048]{1,0:T(8,128)(2,1)S(1)} %collective-permute-done.3.refs_2_, ...), custom_call_target="tpu_custom_call" | custom-call | flops 2300000000 | bytes 16384 | tf_op jit(solution)/shard_map/down/pallas_call | solution.py:65
  29.5 1.7 %collective-permute-start.5 = (bf16[64,2048]{1,0:T(8,128)(2,1)S(1)}, bf16[64,2048]{1,0:T(8,128)(2,1)S(1)}, u32[]{:S(2)}, u32[]{:S(2)}) collective-permute-start(bf16[64,2048]{1,0:T(8,128)(2,1)S(1)} %get-tuple-element.74), channel_id=1, source_target_pairs={{0,2},{1,3},{2,0},{3,1},{4,6},{5,7},{6,4},{7,5},{8,10},{9,11},{10,... | collective-permute-start | bytes 786440 | tf_op jit(solution)/shard_map/ppermute | solution.py:25
  33.0 3.9 %block.6 = (bf16[64,2048]{1,0:T(8,128)(2,1)S(1)}, f32[64,2048]{1,0:T(8,128)S(1)}, f32[8,128]{1,0:T(8,128)S(1)}) custom-call(s32[2]{0:T(128)S(1)} %pad_add_fusion.1.refs_0_, bf16[128,2048]{1,0:T(8,128)(2,1)S(1)} %get-tuple-element.127.refs_1_, bf16[128,2048]{1,0:T(8,128)(2,1)S(1)} %collective-permute-done.1.refs_7_.refs_2_, bf16[1,2,2048]{2,1,0:T(2,128)(2,1)S(1)} %copy-done, ...), custom_call_target="tpu_custom_call" | custom-call | flops 4600000000 | bytes 16384 | tf_op jit(solution)/shard_map/block/pallas_call | solution.py:65
  36.9 1.6 %collective-permute-start.7 = (bf16[64,2048]{1,0:T(8,128)(2,1)S(1)}, bf16[64,2048]{1,0:T(8,128)(2,1)S(1)}, u32[]{:S(2)}, u32[]{:S(2)}) collective-permute-start(bf16[64,2048]{1,0:T(8,128)(2,1)S(1)} %get-tuple-element.82), channel_id=1, source_target_pairs={{0,2},{1,3},{2,0},{3,1},{4,6},{5,7},{6,4},{7,5},{8,10},{9,11},{10,... | collective-permute-start | bytes 786440 | tf_op jit(solution)/shard_map/ppermute | solution.py:25
  38.7 1.9 %collective-permute-start.9 = (bf16[64,2048]{1,0:T(8,128)(2,1)S(1)}, bf16[64,2048]{1,0:T(8,128)(2,1)S(1)}, u32[]{:S(2)}, u32[]{:S(2)}) collective-permute-start(bf16[64,2048]{1,0:T(8,128)(2,1)S(1)} %get-tuple-element.89), channel_id=1, source_target_pairs={{0,4},{1,5},{2,6},{3,7},{4,8},{5,9},{6,10},{7,11},{8,12},{9,13},{1... | collective-permute-start | bytes 786440 | tf_op jit(solution)/shard_map/ppermute | solution.py:25
  40.7 3.9 %block.7 = (bf16[64,2048]{1,0:T(8,128)(2,1)S(1)}, f32[64,2048]{1,0:T(8,128)S(1)}, f32[8,128]{1,0:T(8,128)S(1)}) custom-call(s32[2]{0:T(128)S(1)} %pad_add_fusion.1.refs_0_, bf16[128,2048]{1,0:T(8,128)(2,1)S(1)} %get-tuple-element.127.refs_1_, bf16[128,2048]{1,0:T(8,128)(2,1)S(1)} %collective-permute-done.1.refs_7_.refs_2_, bf16[1,2,2048]{2,1,0:T(2,128)(2,1)S(1)} %copy-done, ...), custom_call_target="tpu_custom_call" | custom-call | flops 4600000000 | bytes 16384 | tf_op jit(solution)/shard_map/block/pallas_call | solution.py:65
  44.7 1.6 %collective-permute-start.10 = (bf16[64,2048]{1,0:T(8,128)(2,1)S(1)}, bf16[64,2048]{1,0:T(8,128)(2,1)S(1)}, u32[]{:S(2)}, u32[]{:S(2)}) collective-permute-start(bf16[64,2048]{1,0:T(8,128)(2,1)S(1)} %get-tuple-element.91), channel_id=1, source_target_pairs={{0,4},{1,5},{2,6},{3,7},{4,8},{5,9},{6,10},{7,11},{8,12},{9,13},{1... | collective-permute-start | bytes 786440 | tf_op jit(solution)/shard_map/ppermute | solution.py:25
  47.8 3.5 %pick_group.4 = (bf16[2048,1024]{1,0:T(8,128)(2,1)S(1)}, bf16[1024,2048]{1,0:T(8,128)(2,1)S(1)}, f32[8,128]{1,0:T(8,128)S(1)}) custom-call(s32[1]{0:T(128)} %bitcast.1.refs_8_.refs_0_, bf16[1,2,2048,1024]{3,2,1,0:T(8,128)(2,1)} %refs_1_.3, bf16[1,2,1024,2048]{3,2,1,0:T(8,128)(2,1)} %refs_2_.3, f32[8,128]{1,0:T(8,128)S(1)} %get-tuple-element.86.refs_3_), custom_call_target="tpu_custom_call" | custom-call | flops 3910000128 | bytes 16384 | tf_op jit(solution)/shard_map/pick_group/pallas_call | solution.py:65
  53.6 3.5 %pick_group.5 = (bf16[2048,1024]{1,0:T(8,128)(2,1)S(1)}, bf16[1024,2048]{1,0:T(8,128)(2,1)S(1)}, f32[8,128]{1,0:T(8,128)S(1)}) custom-call(s32[1]{0:T(128)} %bitcast.1.refs_8_.refs_0_, bf16[1,2,2048,1024]{3,2,1,0:T(8,128)(2,1)} %collective-permute-done.2.refs_3_.refs_1_, bf16[1,2,1024,2048]{3,2,1,0:T(8,128)(2,1)} %collective-permute-done.4.refs_5_.refs_2_, ...), custom_call_target="tpu_custom_call" | custom-call | flops 3910000128 | bytes 16384 | tf_op jit(solution)/shard_map/pick_group/pallas_call | solution.py:65
  59.8 4.1 %collective-permute-done.13.refs_9_.refs_0_.refs_1_ = bf16[64,2048]{1,0:T(8,128)(2,1)S(1)} collective-permute-done((bf16[64,2048]{1,0:T(8,128)(2,1)S(1)}, bf16[64,2048]{1,0:T(8,128)(2,1)S(1)}, u32[]{:S(2)}, u32[]{:S(2)}) %collective-permute-start.13) | collective-permute-done | bytes 262176 | tf_op jit(solution)/shard_map/ppermute | solution.py:25
  64.8 3.9 %block.8 = (bf16[64,2048]{1,0:T(8,128)(2,1)S(1)}, f32[64,2048]{1,0:T(8,128)S(1)}, f32[8,128]{1,0:T(8,128)S(1)}) custom-call(s32[2]{0:T(128)S(1)} %pad_add_fusion.refs_0_, bf16[64,2048]{1,0:T(8,128)(2,1)S(1)} %collective-permute-done.9.refs_4_.refs_1_.refs_0_, bf16[64,2048]{1,0:T(8,128)(2,1)S(1)} %collective-permute-done.16.refs_2_, ...), custom_call_target="tpu_custom_call" | custom-call | flops 1150000000 | bytes 16384 | tf_op jit(solution)/shard_map/block/pallas_call | solution.py:65
  70.0 4.8 %collective-permute-start.20 = (bf16[1,128,2048]{2,1,0:T(8,128)(2,1)S(1)}, bf16[1,128,2048]{2,1,0:T(8,128)(2,1)S(1)}, u32[]{:S(2)}, u32[]{:S(2)}) collective-permute-start(bf16[1,128,2048]{2,1,0:T(8,128)(2,1)S(1)} %get-tuple-element.113), channel_id=1, source_target_pairs={{0,126},{1,127},{2,124},{3,125},{4,122},{5,123},{6,120},{7,121},{8... | collective-permute-start | bytes 1572872 | tf_op jit(solution)/shard_map/ppermute | solution.py:25
  75.5 3.9 %block.9 = (bf16[64,2048]{1,0:T(8,128)(2,1)S(1)}, f32[64,2048]{1,0:T(8,128)S(1)}, f32[8,128]{1,0:T(8,128)S(1)}) custom-call(s32[2]{0:T(128)S(1)} %pad_add_fusion.refs_0_, bf16[64,2048]{1,0:T(8,128)(2,1)S(1)} %collective-permute-done.10.refs_3_.refs_1_, bf16[64,2048]{1,0:T(8,128)(2,1)S(1)} %collective-permute-done.15.refs_2_, ...), custom_call_target="tpu_custom_call" | custom-call | flops 1150000000 | bytes 16384 | tf_op jit(solution)/shard_map/block/pallas_call | solution.py:65
  80.9 2.8 %collective-permute-start.22 = (bf16[1,128,2048]{2,1,0:T(8,128)(2,1)S(1)}, bf16[1,128,2048]{2,1,0:T(8,128)(2,1)S(1)}, u32[]{:S(2)}, u32[]{:S(2)}) collective-permute-start(bf16[1,128,2048]{2,1,0:T(8,128)(2,1)S(1)} %get-tuple-element.119), channel_id=1, source_target_pairs={{0,126},{1,127},{2,124},{3,125},{4,122},{5,123},{6,120},{7,121},{8... | collective-permute-start | bytes 1572872 | tf_op jit(solution)/shard_map/ppermute | solution.py:25
  83.7 3.9 %block.10 = (bf16[64,2048]{1,0:T(8,128)(2,1)S(1)}, f32[64,2048]{1,0:T(8,128)S(1)}, f32[8,128]{1,0:T(8,128)S(1)}) custom-call(s32[2]{0:T(128)S(1)} %pad_add_fusion.refs_0_, bf16[64,2048]{1,0:T(8,128)(2,1)S(1)} %collective-permute-done.13.refs_9_.refs_0_.refs_1_, bf16[64,2048]{1,0:T(8,128)(2,1)S(1)} %collective-permute-done.14.refs_2_, ...), custom_call_target="tpu_custom_call" | custom-call | flops 1150000000 | bytes 16384 | tf_op jit(solution)/shard_map/block/pallas_call | solution.py:65
  87.7 3.9 %block.11 = (bf16[64,2048]{1,0:T(8,128)(2,1)S(1)}, f32[64,2048]{1,0:T(8,128)S(1)}, f32[8,128]{1,0:T(8,128)S(1)}) custom-call(s32[2]{0:T(128)S(1)} %pad_add_fusion.refs_0_, bf16[64,2048]{1,0:T(8,128)(2,1)S(1)} %collective-permute-done.11.refs_1_, bf16[64,2048]{1,0:T(8,128)(2,1)S(1)} %collective-permute-done.12.refs_2_, bf16[1,2,2048]{2,1,0:T(2,128)(2,1)S(1)} %copy-done, ...), custom_call_target="tpu_custom_call" | custom-call | flops 1150000000 | bytes 16384 | tf_op jit(solution)/shard_map/block/pallas_call | solution.py:65
  91.7 2.1 %collective-permute-start.17 = (bf16[64,2048]{1,0:T(8,128)(2,1)S(1)}, bf16[64,2048]{1,0:T(8,128)(2,1)S(1)}, u32[]{:S(2)}, u32[]{:S(2)}) collective-permute-start(bf16[64,2048]{1,0:T(8,128)(2,1)S(1)} %get-tuple-element.105), channel_id=1, source_target_pairs={{0,2},{1,3},{2,0},{3,1},{4,6},{5,7},{6,4},{7,5},{8,10},{9,11},{10,... | collective-permute-start | bytes 786440 | tf_op jit(solution)/shard_map/ppermute | solution.py:25
  94.5 3.5 %collective-permute-done.22.refs_1_ = bf16[1,128,2048]{2,1,0:T(8,128)(2,1)S(1)} collective-permute-done((bf16[1,128,2048]{2,1,0:T(8,128)(2,1)S(1)}, bf16[1,128,2048]{2,1,0:T(8,128)(2,1)S(1)}, u32[]{:S(2)}, u32[]{:S(2)}) %collective-permute-start.22) | collective-permute-done | bytes 524320 | tf_op jit(solution)/shard_map/ppermute | solution.py:25
  (54 shorter events, 20.2 us)
Async XLA Ops:
  0.6 13.9 %collective-permute-start.2 = (bf16[1,2,2048,1024]{3,2,1,0:T(8,128)(2,1)}, bf16[1,2,2048,1024]{3,2,1,0:T(8,128)(2,1)}, u32[]{:S(2)}, u32[]{:S(2)}) collective-permute-start(bf16[1,2,2048,1024]{3,2,1,0:T(8,128)(2,1)} %refs_1_.3), channel_id=1, source_target_pairs={{0,1},{1,0},{2,3},{3,2},{4,5},{5,4},{6,7},{7,6},{8,9},{9,8},{10,11... | collective-permute-start | bytes 25165832 | tf_op jit(solution)/shard_map/ppermute | solution.py:25
  0.7 25.5 %collective-permute-start.4 = (bf16[1,2,1024,2048]{3,2,1,0:T(8,128)(2,1)}, bf16[1,2,1024,2048]{3,2,1,0:T(8,128)(2,1)}, u32[]{:S(2)}, u32[]{:S(2)}) collective-permute-start(bf16[1,2,1024,2048]{3,2,1,0:T(8,128)(2,1)} %refs_2_.3), channel_id=1, source_target_pairs={{0,1},{1,0},{2,3},{3,2},{4,5},{5,4},{6,7},{7,6},{8,9},{9,8},{10,11... | collective-permute-start | bytes 25165832 | tf_op jit(solution)/shard_map/ppermute | solution.py:25
  2.5 16.8 %collective-permute-start.3 = (bf16[128,2048]{1,0:T(8,128)(2,1)S(1)}, bf16[128,2048]{1,0:T(8,128)(2,1)S(1)}, u32[]{:S(2)}, u32[]{:S(2)}) collective-permute-start(bf16[128,2048]{1,0:T(8,128)(2,1)S(1)} %get-tuple-element.126.refs_1_), channel_id=1, source_target_pairs={{0,2},{1,3},{2,0},{3,1},{4,6},{5,7},{6,4},{7,5},{8,10},{9,11},{10,... | collective-permute-start | bytes 1572872 | tf_op jit(solution)/shard_map/ppermute | solution.py:25
  4.1 9.8 %collective-permute-start = (s32[1]{0:T(128)}, s32[1]{0:T(128)}, u32[]{:S(2)}, u32[]{:S(2)}) collective-permute-start(s32[1]{0:T(128)} %param.6), channel_id=1, source_target_pairs={{0,4},{1,5},{2,6},{3,7},{4,8},{5,9},{6,10},{7,11},{8,12},{9,13},{1... | collective-permute-start | bytes 20 | tf_op jit(solution)/shard_map/ppermute | solution.py:25
  5.7 25.4 %collective-permute-start.1 = (bf16[128,2048]{1,0:T(8,128)(2,1)S(1)}, bf16[128,2048]{1,0:T(8,128)(2,1)S(1)}, u32[]{:S(2)}, u32[]{:S(2)}) collective-permute-start(bf16[128,2048]{1,0:T(8,128)(2,1)S(1)} %get-tuple-element.127.refs_1_), channel_id=1, source_target_pairs={{0,2},{1,3},{2,0},{3,1},{4,6},{5,7},{6,4},{7,5},{8,10},{9,11},{10,... | collective-permute-start | bytes 1572872 | tf_op jit(solution)/shard_map/ppermute | solution.py:25
  14.6 4.7 %copy-start = (bf16[1,2,2048]{2,1,0:T(2,128)(2,1)S(1)}, bf16[1,2,2048]{2,1,0:T(2,128)(2,1)}, u32[]{:S(2)}) copy-start(bf16[1,2,2048]{2,1,0:T(2,128)(2,1)} %refs_3_.13) | copy-start | bytes 24580
  29.5 9.2 %collective-permute-start.5 = (bf16[64,2048]{1,0:T(8,128)(2,1)S(1)}, bf16[64,2048]{1,0:T(8,128)(2,1)S(1)}, u32[]{:S(2)}, u32[]{:S(2)}) collective-permute-start(bf16[64,2048]{1,0:T(8,128)(2,1)S(1)} %get-tuple-element.74), channel_id=1, source_target_pairs={{0,2},{1,3},{2,0},{3,1},{4,6},{5,7},{6,4},{7,5},{8,10},{9,11},{10,... | collective-permute-start | bytes 786440 | tf_op jit(solution)/shard_map/ppermute | solution.py:25
  32.4 12.2 %collective-permute-start.8 = (bf16[64,2048]{1,0:T(8,128)(2,1)S(1)}, bf16[64,2048]{1,0:T(8,128)(2,1)S(1)}, u32[]{:S(2)}, u32[]{:S(2)}) collective-permute-start(bf16[64,2048]{1,0:T(8,128)(2,1)S(1)} %get-tuple-element.84), channel_id=1, source_target_pairs={{0,2},{1,3},{2,0},{3,1},{4,6},{5,7},{6,4},{7,5},{8,10},{9,11},{10,... | collective-permute-start | bytes 786440 | tf_op jit(solution)/shard_map/ppermute | solution.py:25
  36.9 14.4 %collective-permute-start.7 = (bf16[64,2048]{1,0:T(8,128)(2,1)S(1)}, bf16[64,2048]{1,0:T(8,128)(2,1)S(1)}, u32[]{:S(2)}, u32[]{:S(2)}) collective-permute-start(bf16[64,2048]{1,0:T(8,128)(2,1)S(1)} %get-tuple-element.82), channel_id=1, source_target_pairs={{0,2},{1,3},{2,0},{3,1},{4,6},{5,7},{6,4},{7,5},{8,10},{9,11},{10,... | collective-permute-start | bytes 786440 | tf_op jit(solution)/shard_map/ppermute | solution.py:25
  38.7 14.1 %collective-permute-start.9 = (bf16[64,2048]{1,0:T(8,128)(2,1)S(1)}, bf16[64,2048]{1,0:T(8,128)(2,1)S(1)}, u32[]{:S(2)}, u32[]{:S(2)}) collective-permute-start(bf16[64,2048]{1,0:T(8,128)(2,1)S(1)} %get-tuple-element.89), channel_id=1, source_target_pairs={{0,4},{1,5},{2,6},{3,7},{4,8},{5,9},{6,10},{7,11},{8,12},{9,13},{1... | collective-permute-start | bytes 786440 | tf_op jit(solution)/shard_map/ppermute | solution.py:25
  44.7 13.8 %collective-permute-start.10 = (bf16[64,2048]{1,0:T(8,128)(2,1)S(1)}, bf16[64,2048]{1,0:T(8,128)(2,1)S(1)}, u32[]{:S(2)}, u32[]{:S(2)}) collective-permute-start(bf16[64,2048]{1,0:T(8,128)(2,1)S(1)} %get-tuple-element.91), channel_id=1, source_target_pairs={{0,4},{1,5},{2,6},{3,7},{4,8},{5,9},{6,10},{7,11},{8,12},{9,13},{1... | collective-permute-start | bytes 786440 | tf_op jit(solution)/shard_map/ppermute | solution.py:25
  46.3 12.1 %collective-permute-start.6 = (bf16[64,2048]{1,0:T(8,128)(2,1)S(1)}, bf16[64,2048]{1,0:T(8,128)(2,1)S(1)}, u32[]{:S(2)}, u32[]{:S(2)}) collective-permute-start(bf16[64,2048]{1,0:T(8,128)(2,1)S(1)} %get-tuple-element.80), channel_id=1, source_target_pairs={{0,2},{1,3},{2,0},{3,1},{4,6},{5,7},{6,4},{7,5},{8,10},{9,11},{10,... | collective-permute-start | bytes 786440 | tf_op jit(solution)/shard_map/ppermute | solution.py:25
  51.3 12.6 %collective-permute-start.13 = (bf16[64,2048]{1,0:T(8,128)(2,1)S(1)}, bf16[64,2048]{1,0:T(8,128)(2,1)S(1)}, u32[]{:S(2)}, u32[]{:S(2)}) collective-permute-start(bf16[64,2048]{1,0:T(8,128)(2,1)S(1)} %get-tuple-element.97), channel_id=1, source_target_pairs={{0,4},{1,5},{2,6},{3,7},{4,8},{5,9},{6,10},{7,11},{8,12},{9,13},{1... | collective-permute-start | bytes 786440 | tf_op jit(solution)/shard_map/ppermute | solution.py:25
  52.8 11.9 %collective-permute-start.16 = (bf16[64,2048]{1,0:T(8,128)(2,1)S(1)}, bf16[64,2048]{1,0:T(8,128)(2,1)S(1)}, u32[]{:S(2)}, u32[]{:S(2)}) collective-permute-start(bf16[64,2048]{1,0:T(8,128)(2,1)S(1)} %collective-permute-done.9.refs_4_.refs_1_.refs_0_), channel_id=1, source_target_pairs={{0,2},{1,3},{2,0},{3,1},{4,6},{5,7},{6,4},{7,5},{8,10},{9,11},{10,... | collective-permute-start | bytes 786440 | tf_op jit(solution)/shard_map/ppermute | solution.py:25
  58.5 16.4 %collective-permute-start.11 = (bf16[64,2048]{1,0:T(8,128)(2,1)S(1)}, bf16[64,2048]{1,0:T(8,128)(2,1)S(1)}, u32[]{:S(2)}, u32[]{:S(2)}) collective-permute-start(bf16[64,2048]{1,0:T(8,128)(2,1)S(1)} %get-tuple-element.92), channel_id=1, source_target_pairs={{0,4},{1,5},{2,6},{3,7},{4,8},{5,9},{6,10},{7,11},{8,12},{9,13},{1... | collective-permute-start | bytes 786440 | tf_op jit(solution)/shard_map/ppermute | solution.py:25
  59.3 16.2 %collective-permute-start.15 = (bf16[64,2048]{1,0:T(8,128)(2,1)S(1)}, bf16[64,2048]{1,0:T(8,128)(2,1)S(1)}, u32[]{:S(2)}, u32[]{:S(2)}) collective-permute-start(bf16[64,2048]{1,0:T(8,128)(2,1)S(1)} %collective-permute-done.10.refs_3_.refs_1_), channel_id=1, source_target_pairs={{0,2},{1,3},{2,0},{3,1},{4,6},{5,7},{6,4},{7,5},{8,10},{9,11},{10,... | collective-permute-start | bytes 786440 | tf_op jit(solution)/shard_map/ppermute | solution.py:25
  63.9 17.0 %collective-permute-start.14 = (bf16[64,2048]{1,0:T(8,128)(2,1)S(1)}, bf16[64,2048]{1,0:T(8,128)(2,1)S(1)}, u32[]{:S(2)}, u32[]{:S(2)}) collective-permute-start(bf16[64,2048]{1,0:T(8,128)(2,1)S(1)} %collective-permute-done.13.refs_9_.refs_0_.refs_1_), channel_id=1, source_target_pairs={{0,2},{1,3},{2,0},{3,1},{4,6},{5,7},{6,4},{7,5},{8,10},{9,11},{10,... | collective-permute-start | bytes 786440 | tf_op jit(solution)/shard_map/ppermute | solution.py:25
  68.7 23.0 %collective-permute-start.18 = (bf16[64,2048]{1,0:T(8,128)(2,1)S(1)}, bf16[64,2048]{1,0:T(8,128)(2,1)S(1)}, u32[]{:S(2)}, u32[]{:S(2)}) collective-permute-start(bf16[64,2048]{1,0:T(8,128)(2,1)S(1)} %get-tuple-element.107), channel_id=1, source_target_pairs={{0,2},{1,3},{2,0},{3,1},{4,6},{5,7},{6,4},{7,5},{8,10},{9,11},{10,... | collective-permute-start | bytes 786440 | tf_op jit(solution)/shard_map/ppermute | solution.py:25
  70.0 23.8 %collective-permute-start.20 = (bf16[1,128,2048]{2,1,0:T(8,128)(2,1)S(1)}, bf16[1,128,2048]{2,1,0:T(8,128)(2,1)S(1)}, u32[]{:S(2)}, u32[]{:S(2)}) collective-permute-start(bf16[1,128,2048]{2,1,0:T(8,128)(2,1)S(1)} %get-tuple-element.113), channel_id=1, source_target_pairs={{0,126},{1,127},{2,124},{3,125},{4,122},{5,123},{6,120},{7,121},{8... | collective-permute-start | bytes 1572872 | tf_op jit(solution)/shard_map/ppermute | solution.py:25
  74.9 12.8 %collective-permute-start.12 = (bf16[64,2048]{1,0:T(8,128)(2,1)S(1)}, bf16[64,2048]{1,0:T(8,128)(2,1)S(1)}, u32[]{:S(2)}, u32[]{:S(2)}) collective-permute-start(bf16[64,2048]{1,0:T(8,128)(2,1)S(1)} %collective-permute-done.11.refs_1_), channel_id=1, source_target_pairs={{0,2},{1,3},{2,0},{3,1},{4,6},{5,7},{6,4},{7,5},{8,10},{9,11},{10,... | collective-permute-start | bytes 786440 | tf_op jit(solution)/shard_map/ppermute | solution.py:25
  79.4 15.0 %collective-permute-start.19 = (bf16[64,2048]{1,0:T(8,128)(2,1)S(1)}, bf16[64,2048]{1,0:T(8,128)(2,1)S(1)}, u32[]{:S(2)}, u32[]{:S(2)}) collective-permute-start(bf16[64,2048]{1,0:T(8,128)(2,1)S(1)} %get-tuple-element.111), channel_id=1, source_target_pairs={{0,2},{1,3},{2,0},{3,1},{4,6},{5,7},{6,4},{7,5},{8,10},{9,11},{10,... | collective-permute-start | bytes 786440 | tf_op jit(solution)/shard_map/ppermute | solution.py:25
  80.9 17.1 %collective-permute-start.22 = (bf16[1,128,2048]{2,1,0:T(8,128)(2,1)S(1)}, bf16[1,128,2048]{2,1,0:T(8,128)(2,1)S(1)}, u32[]{:S(2)}, u32[]{:S(2)}) collective-permute-start(bf16[1,128,2048]{2,1,0:T(8,128)(2,1)S(1)} %get-tuple-element.119), channel_id=1, source_target_pairs={{0,126},{1,127},{2,124},{3,125},{4,122},{5,123},{6,120},{7,121},{8... | collective-permute-start | bytes 1572872 | tf_op jit(solution)/shard_map/ppermute | solution.py:25
  87.6 11.0 %collective-permute-start.21 = (bf16[64,2048]{1,0:T(8,128)(2,1)S(1)}, bf16[64,2048]{1,0:T(8,128)(2,1)S(1)}, u32[]{:S(2)}, u32[]{:S(2)}) collective-permute-start(bf16[64,2048]{1,0:T(8,128)(2,1)S(1)} %get-tuple-element.117), channel_id=1, source_target_pairs={{0,2},{1,3},{2,0},{3,1},{4,6},{5,7},{6,4},{7,5},{8,10},{9,11},{10,... | collective-permute-start | bytes 786440 | tf_op jit(solution)/shard_map/ppermute | solution.py:25
  91.7 8.0 %collective-permute-start.17 = (bf16[64,2048]{1,0:T(8,128)(2,1)S(1)}, bf16[64,2048]{1,0:T(8,128)(2,1)S(1)}, u32[]{:S(2)}, u32[]{:S(2)}) collective-permute-start(bf16[64,2048]{1,0:T(8,128)(2,1)S(1)} %get-tuple-element.105), channel_id=1, source_target_pairs={{0,2},{1,3},{2,0},{3,1},{4,6},{5,7},{6,4},{7,5},{8,10},{9,11},{10,... | collective-permute-start | bytes 786440 | tf_op jit(solution)/shard_map/ppermute | solution.py:25

commit v5 on v3

--- a/solution.py
+++ b/solution.py
@@ -53,7 +53,7 @@
     def __init__(self):
         self.token = jnp.zeros((8, 128), jnp.float32)
 
-    def call(self, kernel, name, outs, specs, args, scratch=(), vmem=4 * MIB, us=0.1, behind=()):
+    def call(self, kernel, name, outs, specs, args, scratch=(), vmem=4 * MIB, us=0.1, behind=(), out_specs=None):
         vmem_spec = pl.BlockSpec(memory_space=pltpu.VMEM)
 
         def with_token(*refs):
@@ -66,7 +66,7 @@
             with_token,
             out_shape=tuple(outs) + (jax.ShapeDtypeStruct((8, 128), jnp.float32),),
             in_specs=list(specs) + [pl.BlockSpec(memory_space=pl.ANY)] * (1 + len(behind)),
-            out_specs=(vmem_spec,) * (len(outs) + 1),
+            out_specs=tuple(out_specs or (vmem_spec,) * len(outs)) + (vmem_spec,),
             scratch_shapes=list(scratch),
             compiler_params=pltpu.CompilerParams(vmem_limit_bytes=vmem),
             cost_estimate=pl.CostEstimate(flops=int(us * 1.15e9), bytes_accessed=2**14, transcendentals=0),
@@ -89,26 +89,82 @@
                 size = ws[n].shape[2] // 4
                 piece = pl.ds(k * size, size)
                 held = outs[j * count + n]
-                loads.append(pltpu.make_async_copy(ws[n].at[0, idx[j], piece], held.at[piece], sems.at[len(loads)]))
+                loads.append(pltpu.make_async_copy(ws[n].at[0, idx[j * count + n], piece], held.at[piece], sems.at[len(loads)]))
     for load in loads:
         load.start()
     for load in loads:
         load.wait()
 
 
-def pick(order, groups, ws, behind=()):
+def pick(order, groups, ws, behind=(), us=None):
     n = len(ws)
     held = order.call(
         functools.partial(pick_kernel, len(groups), n),
         "pick_group",
         [pltpu.VMEM(w.shape[2:], w.dtype) for w in ws] * len(groups),
         [SMEM_SPEC] + [HBM_SPEC] * n,
-        (jnp.stack(groups), *(in_hbm(w) for w in ws)),
+        (jnp.stack([g[i] if isinstance(g, tuple) else g for g in groups for i in range(n)]), *(in_hbm(w) for w in ws)),
         [pltpu.SemaphoreType.DMA((4 * n * len(groups),))],
-        us=1.7 * n * len(groups),
+        us=us or 1.7 * n * len(groups),
         behind=behind,
     )
     return [held[j * n : (j + 1) * n] for j in range(len(groups))]
+
+
+def copy_kernel(idx, w, sent, held, in_sems, out_sems):
+    parts = in_sems.shape[0]
+    pieces = [pl.ds(k * (held.shape[0] // parts), held.shape[0] // parts) for k in range(parts)]
+    loads = [pltpu.make_async_copy(w.at[0, idx[0], p], held.at[p], in_sems.at[k]) for k, p in enumerate(pieces)]
+    saves = [pltpu.make_async_copy(held.at[p], sent.at[0, 0, p], out_sems.at[k]) for k, p in enumerate(pieces)]
+    for load in loads:
+        load.start()
+    for load, save in zip(loads, saves):
+        load.wait()
+        save.start()
+    for save in saves:
+        save.wait()
+
+
+def copy_group(order, group, w, us):
+    shape = w.shape[2:]
+    return order.call(
+        copy_kernel,
+        "copy_group",
+        [pltpu.HBM((1, 1) + shape, w.dtype)],
+        [SMEM_SPEC, HBM_SPEC],
+        (group.reshape(1), in_hbm(w)),
+        [pltpu.VMEM(shape, w.dtype), pltpu.SemaphoreType.DMA((8,)), pltpu.SemaphoreType.DMA((8,))],
+        vmem=6 * MIB,
+        us=us,
+        out_specs=[HBM_SPEC],
+    )[0]
+
+
+def load_kernel(idx, first, second, held, sems):
+    parts = sems.shape[0]
+    pieces = [pl.ds(k * (held.shape[0] // parts), held.shape[0] // parts) for k in range(parts)]
+
+    def run(w):
+        loads = [pltpu.make_async_copy(w.at[0, 0, p], held.at[p], sems.at[k]) for k, p in enumerate(pieces)]
+        for load in loads:
+            load.start()
+        for load in loads:
+            load.wait()
+
+    pl.when(idx[0] == 0)(lambda: run(first))
+    pl.when(idx[0] != 0)(lambda: run(second))
+
+
+def load(order, which, first, second):
+    return order.call(
+        load_kernel,
+        "load",
+        [pltpu.VMEM(first.shape[2:], first.dtype)],
+        [SMEM_SPEC, HBM_SPEC, HBM_SPEC],
+        (which.reshape(1), in_hbm(first), in_hbm(second)),
+        [pltpu.SemaphoreType.DMA((8,))],
+        us=1.7,
+    )[0]
 
 
 def normalize(x, gain_row):
@@ -191,7 +247,7 @@
         (idx, own, par, gain, in_vmem(w_in), in_vmem(r_in)),
         [pltpu.VMEM((2 * rows, d), jnp.bfloat16)],
         8 * MIB,
-        us=3,
+        us=50,
     )[0]
 
 
@@ -275,13 +331,15 @@
         return route(whole(order, pack_kernel, "pack", xs, len(xs) * ROWS), to_mirror)
 
     rows = act.shape[1]
-    r_in, r_out = route(w_in, to_other_core), route(w_out, to_other_core)
+    r_in = route(w_in, to_other_core)
     own = [act[0, : rows // 2], act[0, rows // 2 :]]
     par = [across(x) for x in own]
 
-    ((w_in1, w_out1, r_in1),) = pick(order, (g1,), (w_in, w_out, r_in))
+    r_first = route(copy_group(order, g1, w_out, 0.05), to_other_core)
+    r_second = route(copy_group(order, 1 - g1, w_out, 0.05), to_other_core)
+    ((w_in1, w_out1, r_in1),) = pick(order, (g1,), (w_in, w_out, r_in), us=0.1)
     hidden = up_rows(order, idx1, own[0], par[0], gain, w_in1, r_in1)
-    ((r_out1,),) = pick(order, (g1,), (r_out,))
+    ((r_out1,),) = pick(order, (jnp.zeros_like(g1),), (r_first,))
     w1 = (w_in1, w_out1, r_in1, r_out1)
     give, keep0 = down(order, idx1, own[0], par[0], hidden, w_out1, r_out1, 0)
     got0 = across(give)
@@ -295,7 +353,8 @@
     x1 = onward(join(order, keep1, got1))
     ((w_in2, w_out2),) = pick(order, (g2,), (w_in, w_out))
     x2 = onward(join(order, keep2, got2))
-    ((r_in2, r_out2),) = pick(order, (g2,), (r_in, r_out), (x0,))
+    ((r_in2,),) = pick(order, (g2,), (r_in,), (x0,))
+    r_out2 = load(order, g2 - g1, r_first, r_second)
     x3 = onward(join(order, keep3, got3, (x1,)))
     w2 = (w_in2, w_out2, r_in2, r_out2)
 

time: 103 us -> 101 us (0.981)
  waiting for transfers between devices: 19.7 us -> 6.83 us
  Pallas kernels: 48.7 us -> 58 us
  starting transfers between devices: 30.4 us -> 31.6 us
    ppermute x23 -> x24, waiting for transfers between devices: 19.7 us -> 6.83 us  [route(): return lax.ppermute(x, AXES, pairs)]
    pallas_call x26 -> x29, Pallas kernels: 48.7 us -> 58 us  [call(): pl.pallas_call(with_token, out_shape=tuple(outs) + (jax.ShapeDtypeStruct(...]
    ppermute x23 -> x24, starting transfers between devices: 30.4 us -> 31.6 us  [route(): return lax.ppermute(x, AXES, pairs)]
  transfers between devices with their start and end apart: 23 -> 24, of which waited for: 6 -> 3; matrix products, arithmetic and copies ran while one was open for 1% -> 1% of each run, Pallas kernels for 47% -> 57%
where the time goes in v5:
time: 101 us; the launch traced here: 100 us
  Pallas kernels  58 us (57%)
  starting transfers between devices  31.6 us (31%)
  waiting for transfers between devices  6.83 us (7%)
  between operations  2.31 us (2%)
  local copies, waits for them, and re-layouts  1.28 us (1%)
    pallas_call x29, Pallas kernels, call(): pl.pallas_call(with_token, out_shape=tuple(outs) + (jax.ShapeDtypeStruct(...  58 us
    ppermute x24, starting transfers between devices, route(): return lax.ppermute(x, AXES, pairs)  31.6 us
    ppermute x24, waiting for transfers between devices, route(): return lax.ppermute(x, AXES, pairs)  6.83 us
  transfers between devices with their start and end apart: 24, of which 3 were waited for; matrix products, arithmetic and copies ran while one was open for 1% of the time, Pallas kernels for 57%

profile of v5, /device:TPU:0, one launch (start us, length us, event | category | flops | bytes accessed | tf_op | source)
XLA Modules:
  0.0 100.2 jit_solution(13264272566972170987)
XLA Ops:
  5.9 3.6 %copy_group.2 = (bf16[1,1,1024,2048]{3,2,1,0:T(8,128)(2,1)}, f32[8,128]{1,0:T(8,128)S(1)}) custom-call(s32[1]{0:T(128)} %copy.7.refs_0_, bf16[1,2,1024,2048]{3,2,1,0:T(8,128)(2,1)} %refs_2_.3, f32[8,128]{1,0:T(8,128)S(1)} %broadcast_in_dim.3.refs_2_), custom_call_target="tpu_custom_call" | custom-call | flops 57500000 | bytes 16384 | tf_op jit(solution)/shard_map/copy_group/pallas_call | solution.py:65
  10.2 3.6 %copy_group.3 = (bf16[1,1,1024,2048]{3,2,1,0:T(8,128)(2,1)}, f32[8,128]{1,0:T(8,128)S(1)}) custom-call(s32[1]{0:T(128)} %bitcast.5.refs_0_, bf16[1,2,1024,2048]{3,2,1,0:T(8,128)(2,1)} %refs_2_.3, f32[8,128]{1,0:T(8,128)S(1)} %get-tuple-element.68.refs_2_), custom_call_target="tpu_custom_call" | custom-call | flops 57500000 | bytes 16384 | tf_op jit(solution)/shard_map/copy_group/pallas_call | solution.py:65
  14.9 5.2 %pick_group.4 = (bf16[2048,1024]{1,0:T(8,128)(2,1)S(1)}, bf16[1024,2048]{1,0:T(8,128)(2,1)S(1)}, bf16[2048,1024]{1,0:T(8,128)(2,1)S(1)}, f32[8,128]{1,0:T(8,128)S(1)}) custom-call(s32[3]{0:T(128)S(1)} %stack.29.refs_0_, bf16[1,2,2048,1024]{3,2,1,0:T(8,128)(2,1)} %refs_1_.7, bf16[1,2,1024,2048]{3,2,1,0:T(8,128)(2,1)} %refs_2_.3, ...), custom_call_target="tpu_custom_call" | custom-call | flops 115000000 | bytes 16384 | tf_op jit(solution)/shard_map/pick_group/pallas_call | solution.py:65
  20.1 4.0 %up.1 = (bf16[256,2048]{1,0:T(8,128)(2,1)S(1)}, f32[8,128]{1,0:T(8,128)S(1)}) custom-call(s32[2]{0:T(128)S(1)} %pad_add_fusion.1.refs_0_, bf16[128,2048]{1,0:T(8,128)(2,1)S(1)} %get-tuple-element.134.refs_1_, bf16[128,2048]{1,0:T(8,128)(2,1)S(1)} %collective-permute-done.4.refs_2_, bf16[1,2,2048]{2,1,0:T(2,128)(2,1)S(1)} %copy-done, ...), custom_call_target="tpu_custom_call" | custom-call | flops 57500000256 | bytes 16384 | tf_op jit(solution)/shard_map/up/pallas_call | solution.py:65
  24.2 2.2 %pick_group.5 = (bf16[1024,2048]{1,0:T(8,128)(2,1)S(1)}, f32[8,128]{1,0:T(8,128)S(1)}) custom-call(s32[1]{0:T(128)} %constant.28.clone.1.refs_0_, bf16[1,1,1024,2048]{3,2,1,0:T(8,128)(2,1)} %collective-permute-done.3.refs_1_, f32[8,128]{1,0:T(8,128)S(1)} %get-tuple-element.75.refs_2_), custom_call_target="tpu_custom_call" | custom-call | flops 1955000064 | bytes 16384 | tf_op jit(solution)/shard_map/pick_group/pallas_call | solution.py:65
  26.4 1.8 %down.2 = (bf16[64,2048]{1,0:T(8,128)(2,1)S(1)}, f32[64,2048]{1,0:T(8,128)S(1)}, f32[8,128]{1,0:T(8,128)S(1)}) custom-call(s32[2]{0:T(128)S(1)} %pad_add_fusion.1.refs_0_, bf16[128,2048]{1,0:T(8,128)(2,1)S(1)} %get-tuple-element.134.refs_1_, bf16[128,2048]{1,0:T(8,128)(2,1)S(1)} %collective-permute-done.4.refs_2_, ...), custom_call_target="tpu_custom_call" | custom-call | flops 2300000000 | bytes 16384 | tf_op jit(solution)/shard_map/down/pallas_call | solution.py:65
  29.8 1.8 %down.3 = (bf16[64,2048]{1,0:T(8,128)(2,1)S(1)}, f32[64,2048]{1,0:T(8,128)S(1)}, f32[8,128]{1,0:T(8,128)S(1)}) custom-call(s32[2]{0:T(128)S(1)} %pad_add_fusion.1.refs_0_, bf16[128,2048]{1,0:T(8,128)(2,1)S(1)} %get-tuple-element.134.refs_1_, bf16[128,2048]{1,0:T(8,128)(2,1)S(1)} %collective-permute-done.4.refs_2_, ...), custom_call_target="tpu_custom_call" | custom-call | flops 2300000000 | bytes 16384 | tf_op jit(solution)/shard_map/down/pallas_call | solution.py:65
  32.3 3.9 %block.6 = (bf16[64,2048]{1,0:T(8,128)(2,1)S(1)}, f32[64,2048]{1,0:T(8,128)S(1)}, f32[8,128]{1,0:T(8,128)S(1)}) custom-call(s32[2]{0:T(128)S(1)} %pad_add_fusion.1.refs_0_, bf16[128,2048]{1,0:T(8,128)(2,1)S(1)} %get-tuple-element.135.refs_1_, bf16[128,2048]{1,0:T(8,128)(2,1)S(1)} %collective-permute-done.1.refs_7_.refs_2_, bf16[1,2,2048]{2,1,0:T(2,128)(2,1)S(1)} %copy-done, ...), custom_call_target="tpu_custom_call" | custom-call | flops 4600000000 | bytes 16384 | tf_op jit(solution)/shard_map/block/pallas_call | solution.py:65
  37.8 1.8 %collective-permute-start.10 = (bf16[64,2048]{1,0:T(8,128)(2,1)S(1)}, bf16[64,2048]{1,0:T(8,128)(2,1)S(1)}, u32[]{:S(2)}, u32[]{:S(2)}) collective-permute-start(bf16[64,2048]{1,0:T(8,128)(2,1)S(1)} %get-tuple-element.96), channel_id=1, source_target_pairs={{0,4},{1,5},{2,6},{3,7},{4,8},{5,9},{6,10},{7,11},{8,12},{9,13},{1... | collective-permute-start | bytes 786440 | tf_op jit(solution)/shard_map/ppermute | solution.py:25
  39.6 3.9 %block.7 = (bf16[64,2048]{1,0:T(8,128)(2,1)S(1)}, f32[64,2048]{1,0:T(8,128)S(1)}, f32[8,128]{1,0:T(8,128)S(1)}) custom-call(s32[2]{0:T(128)S(1)} %pad_add_fusion.1.refs_0_, bf16[128,2048]{1,0:T(8,128)(2,1)S(1)} %get-tuple-element.135.refs_1_, bf16[128,2048]{1,0:T(8,128)(2,1)S(1)} %collective-permute-done.1.refs_7_.refs_2_, bf16[1,2,2048]{2,1,0:T(2,128)(2,1)S(1)} %copy-done, ...), custom_call_target="tpu_custom_call" | custom-call | flops 4600000000 | bytes 16384 | tf_op jit(solution)/shard_map/block/pallas_call | solution.py:65
  46.3 4.0 %pick_group.6 = (bf16[2048,1024]{1,0:T(8,128)(2,1)S(1)}, bf16[1024,2048]{1,0:T(8,128)(2,1)S(1)}, f32[8,128]{1,0:T(8,128)S(1)}) custom-call(s32[2]{0:T(128)S(1)} %pad_add_fusion.2.refs_0_, bf16[1,2,2048,1024]{3,2,1,0:T(8,128)(2,1)} %refs_1_.7, bf16[1,2,1024,2048]{3,2,1,0:T(8,128)(2,1)} %refs_2_.3, f32[8,128]{1,0:T(8,128)S(1)} %get-tuple-element.93.refs_3_), custom_call_target="tpu_custom_call" | custom-call | flops 3910000128 | bytes 16384 | tf_op jit(solution)/shard_map/pick_group/pallas_call | solution.py:65
  50.4 1.7 %collective-permute-start.14 = (bf16[64,2048]{1,0:T(8,128)(2,1)S(1)}, bf16[64,2048]{1,0:T(8,128)(2,1)S(1)}, u32[]{:S(2)}, u32[]{:S(2)}) collective-permute-start(bf16[64,2048]{1,0:T(8,128)(2,1)S(1)} %get-tuple-element.105), channel_id=1, source_target_pairs={{0,4},{1,5},{2,6},{3,7},{4,8},{5,9},{6,10},{7,11},{8,12},{9,13},{1... | collective-permute-start | bytes 786440 | tf_op jit(solution)/shard_map/ppermute | solution.py:25
  53.0 2.2 %pick_group.7 = (bf16[2048,1024]{1,0:T(8,128)(2,1)S(1)}, f32[8,128]{1,0:T(8,128)S(1)}) custom-call(s32[1]{0:T(128)} %bitcast.1.refs_8_.refs_0_, bf16[1,2,2048,1024]{3,2,1,0:T(8,128)(2,1)} %collective-permute-done.2.refs_3_.refs_1_, f32[8,128]{1,0:T(8,128)S(1)} %get-tuple-element.95.refs_2_, bf16[64,2048]{1,0:T(8,128)(2,1)S(1)} %collective-permute-done.10.refs_3_.refs_1_.refs_0_), custom_call_target="tpu_custom_call" | custom-call | flops 1955000064 | bytes 16384 | tf_op jit(solution)/shard_map/pick_group/pallas_call | solution.py:65
  55.2 2.2 %load.1 = (bf16[1024,2048]{1,0:T(8,128)(2,1)S(1)}, f32[8,128]{1,0:T(8,128)S(1)}) custom-call(s32[1]{0:T(128)} %bitcast.7.refs_0_, bf16[1,1,1024,2048]{3,2,1,0:T(8,128)(2,1)} %collective-permute-done.3.refs_1_, bf16[1,1,1024,2048]{3,2,1,0:T(8,128)(2,1)} %collective-permute-done.7.refs_2_, f32[8,128]{1,0:T(8,128)S(1)} %get-tuple-element.97.refs_3_), custom_call_target="tpu_custom_call" | custom-call | flops 1955000064 | bytes 16384 | tf_op jit(solution)/shard_map/load/pallas_call | solution.py:65
  57.5 2.0 %collective-permute-start.12 = (bf16[64,2048]{1,0:T(8,128)(2,1)S(1)}, bf16[64,2048]{1,0:T(8,128)(2,1)S(1)}, u32[]{:S(2)}, u32[]{:S(2)}) collective-permute-start(bf16[64,2048]{1,0:T(8,128)(2,1)S(1)} %get-tuple-element.100), channel_id=1, source_target_pairs={{0,4},{1,5},{2,6},{3,7},{4,8},{5,9},{6,10},{7,11},{8,12},{9,13},{1... | collective-permute-start | bytes 786440 | tf_op jit(solution)/shard_map/ppermute | solution.py:25
  60.2 2.3 %collective-permute-done.14.refs_9_.refs_0_.refs_1_ = bf16[64,2048]{1,0:T(8,128)(2,1)S(1)} collective-permute-done((bf16[64,2048]{1,0:T(8,128)(2,1)S(1)}, bf16[64,2048]{1,0:T(8,128)(2,1)S(1)}, u32[]{:S(2)}, u32[]{:S(2)}) %collective-permute-start.14) | collective-permute-done | bytes 262176 | tf_op jit(solution)/shard_map/ppermute | solution.py:25
  63.1 3.9 %block.8 = (bf16[64,2048]{1,0:T(8,128)(2,1)S(1)}, f32[64,2048]{1,0:T(8,128)S(1)}, f32[8,128]{1,0:T(8,128)S(1)}) custom-call(s32[2]{0:T(128)S(1)} %pad_add_fusion.refs_0_, bf16[64,2048]{1,0:T(8,128)(2,1)S(1)} %collective-permute-done.10.refs_3_.refs_1_.refs_0_, bf16[64,2048]{1,0:T(8,128)(2,1)S(1)} %collective-permute-done.17.refs_2_, ...), custom_call_target="tpu_custom_call" | custom-call | flops 1150000000 | bytes 16384 | tf_op jit(solution)/shard_map/block/pallas_call | solution.py:65
  68.6 4.4 %collective-permute-start.21 = (bf16[1,128,2048]{2,1,0:T(8,128)(2,1)S(1)}, bf16[1,128,2048]{2,1,0:T(8,128)(2,1)S(1)}, u32[]{:S(2)}, u32[]{:S(2)}) collective-permute-start(bf16[1,128,2048]{2,1,0:T(8,128)(2,1)S(1)} %get-tuple-element.121), channel_id=1, source_target_pairs={{0,126},{1,127},{2,124},{3,125},{4,122},{5,123},{6,120},{7,121},{8... | collective-permute-start | bytes 1572872 | tf_op jit(solution)/shard_map/ppermute | solution.py:25
  73.6 3.9 %block.9 = (bf16[64,2048]{1,0:T(8,128)(2,1)S(1)}, f32[64,2048]{1,0:T(8,128)S(1)}, f32[8,128]{1,0:T(8,128)S(1)}) custom-call(s32[2]{0:T(128)S(1)} %pad_add_fusion.refs_0_, bf16[64,2048]{1,0:T(8,128)(2,1)S(1)} %collective-permute-done.11.refs_3_.refs_1_, bf16[64,2048]{1,0:T(8,128)(2,1)S(1)} %collective-permute-done.16.refs_2_, ...), custom_call_target="tpu_custom_call" | custom-call | flops 1150000000 | bytes 16384 | tf_op jit(solution)/shard_map/block/pallas_call | solution.py:65
  79.0 3.2 %collective-permute-start.23 = (bf16[1,128,2048]{2,1,0:T(8,128)(2,1)S(1)}, bf16[1,128,2048]{2,1,0:T(8,128)(2,1)S(1)}, u32[]{:S(2)}, u32[]{:S(2)}) collective-permute-start(bf16[1,128,2048]{2,1,0:T(8,128)(2,1)S(1)} %get-tuple-element.127), channel_id=1, source_target_pairs={{0,126},{1,127},{2,124},{3,125},{4,122},{5,123},{6,120},{7,121},{8... | collective-permute-start | bytes 1572872 | tf_op jit(solution)/shard_map/ppermute | solution.py:25
  82.2 3.9 %block.10 = (bf16[64,2048]{1,0:T(8,128)(2,1)S(1)}, f32[64,2048]{1,0:T(8,128)S(1)}, f32[8,128]{1,0:T(8,128)S(1)}) custom-call(s32[2]{0:T(128)S(1)} %pad_add_fusion.refs_0_, bf16[64,2048]{1,0:T(8,128)(2,1)S(1)} %collective-permute-done.14.refs_9_.refs_0_.refs_1_, bf16[64,2048]{1,0:T(8,128)(2,1)S(1)} %collective-permute-done.15.refs_2_, ...), custom_call_target="tpu_custom_call" | custom-call | flops 1150000000 | bytes 16384 | tf_op jit(solution)/shard_map/block/pallas_call | solution.py:65
  86.3 3.9 %block.11 = (bf16[64,2048]{1,0:T(8,128)(2,1)S(1)}, f32[64,2048]{1,0:T(8,128)S(1)}, f32[8,128]{1,0:T(8,128)S(1)}) custom-call(s32[2]{0:T(128)S(1)} %pad_add_fusion.refs_0_, bf16[64,2048]{1,0:T(8,128)(2,1)S(1)} %collective-permute-done.12.refs_1_, bf16[64,2048]{1,0:T(8,128)(2,1)S(1)} %collective-permute-done.13.refs_2_, bf16[1,2,2048]{2,1,0:T(2,128)(2,1)S(1)} %copy-done, ...), custom_call_target="tpu_custom_call" | custom-call | flops 1150000000 | bytes 16384 | tf_op jit(solution)/shard_map/block/pallas_call | solution.py:65
  90.2 2.1 %collective-permute-start.18 = (bf16[64,2048]{1,0:T(8,128)(2,1)S(1)}, bf16[64,2048]{1,0:T(8,128)(2,1)S(1)}, u32[]{:S(2)}, u32[]{:S(2)}) collective-permute-start(bf16[64,2048]{1,0:T(8,128)(2,1)S(1)} %get-tuple-element.113), channel_id=1, source_target_pairs={{0,2},{1,3},{2,0},{3,1},{4,6},{5,7},{6,4},{7,5},{8,10},{9,11},{10,... | collective-permute-start | bytes 786440 | tf_op jit(solution)/shard_map/ppermute | solution.py:25
  93.0 3.1 %collective-permute-done.23.refs_1_ = bf16[1,128,2048]{2,1,0:T(8,128)(2,1)S(1)} collective-permute-done((bf16[1,128,2048]{2,1,0:T(8,128)(2,1)S(1)}, bf16[1,128,2048]{2,1,0:T(8,128)(2,1)S(1)}, u32[]{:S(2)}, u32[]{:S(2)}) %collective-permute-start.23) | collective-permute-done | bytes 524320 | tf_op jit(solution)/shard_map/ppermute | solution.py:25
  (61 shorter events, 23.1 us)
Async XLA Ops:
  0.6 14.2 %collective-permute-start.2 = (bf16[1,2,2048,1024]{3,2,1,0:T(8,128)(2,1)}, bf16[1,2,2048,1024]{3,2,1,0:T(8,128)(2,1)}, u32[]{:S(2)}, u32[]{:S(2)}) collective-permute-start(bf16[1,2,2048,1024]{3,2,1,0:T(8,128)(2,1)} %refs_1_.7), channel_id=1, source_target_pairs={{0,1},{1,0},{2,3},{3,2},{4,5},{5,4},{6,7},{7,6},{8,9},{9,8},{10,11... | collective-permute-start | bytes 25165832 | tf_op jit(solution)/shard_map/ppermute | solution.py:25
  2.0 18.1 %collective-permute-start.4 = (bf16[128,2048]{1,0:T(8,128)(2,1)S(1)}, bf16[128,2048]{1,0:T(8,128)(2,1)S(1)}, u32[]{:S(2)}, u32[]{:S(2)}) collective-permute-start(bf16[128,2048]{1,0:T(8,128)(2,1)S(1)} %get-tuple-element.134.refs_1_), channel_id=1, source_target_pairs={{0,2},{1,3},{2,0},{3,1},{4,6},{5,7},{6,4},{7,5},{8,10},{9,11},{10,... | collective-permute-start | bytes 1572872 | tf_op jit(solution)/shard_map/ppermute | solution.py:25
  3.7 10.3 %collective-permute-start = (s32[1]{0:T(128)}, s32[1]{0:T(128)}, u32[]{:S(2)}, u32[]{:S(2)}) collective-permute-start(s32[1]{0:T(128)} %param.6), channel_id=1, source_target_pairs={{0,4},{1,5},{2,6},{3,7},{4,8},{5,9},{6,10},{7,11},{8,12},{9,13},{1... | collective-permute-start | bytes 20 | tf_op jit(solution)/shard_map/ppermute | solution.py:25
  9.5 14.6 %collective-permute-start.3 = (bf16[1,1,1024,2048]{3,2,1,0:T(8,128)(2,1)}, bf16[1,1,1024,2048]{3,2,1,0:T(8,128)(2,1)}, u32[]{:S(2)}, u32[]{:S(2)}) collective-permute-start(bf16[1,1,1024,2048]{3,2,1,0:T(8,128)(2,1)} %get-tuple-element.73), channel_id=1, source_target_pairs={{0,1},{1,0},{2,3},{3,2},{4,5},{5,4},{6,7},{7,6},{8,9},{9,8},{10,11... | collective-permute-start | bytes 12582920 | tf_op jit(solution)/shard_map/ppermute | solution.py:25
  9.6 20.2 %collective-permute-start.1 = (bf16[128,2048]{1,0:T(8,128)(2,1)S(1)}, bf16[128,2048]{1,0:T(8,128)(2,1)S(1)}, u32[]{:S(2)}, u32[]{:S(2)}) collective-permute-start(bf16[128,2048]{1,0:T(8,128)(2,1)S(1)} %get-tuple-element.135.refs_1_), channel_id=1, source_target_pairs={{0,2},{1,3},{2,0},{3,1},{4,6},{5,7},{6,4},{7,5},{8,10},{9,11},{10,... | collective-permute-start | bytes 1572872 | tf_op jit(solution)/shard_map/ppermute | solution.py:25
  13.9 41.3 %collective-permute-start.7 = (bf16[1,1,1024,2048]{3,2,1,0:T(8,128)(2,1)}, bf16[1,1,1024,2048]{3,2,1,0:T(8,128)(2,1)}, u32[]{:S(2)}, u32[]{:S(2)}) collective-permute-start(bf16[1,1,1024,2048]{3,2,1,0:T(8,128)(2,1)} %get-tuple-element.87), channel_id=1, source_target_pairs={{0,1},{1,0},{2,3},{3,2},{4,5},{5,4},{6,7},{7,6},{8,9},{9,8},{10,11... | collective-permute-start | bytes 12582920 | tf_op jit(solution)/shard_map/ppermute | solution.py:25
  28.2 9.5 %collective-permute-start.5 = (bf16[64,2048]{1,0:T(8,128)(2,1)S(1)}, bf16[64,2048]{1,0:T(8,128)(2,1)S(1)}, u32[]{:S(2)}, u32[]{:S(2)}) collective-permute-start(bf16[64,2048]{1,0:T(8,128)(2,1)S(1)} %get-tuple-element.80), channel_id=1, source_target_pairs={{0,2},{1,3},{2,0},{3,1},{4,6},{5,7},{6,4},{7,5},{8,10},{9,11},{10,... | collective-permute-start | bytes 786440 | tf_op jit(solution)/shard_map/ppermute | solution.py:25
  31.6 11.9 %collective-permute-start.9 = (bf16[64,2048]{1,0:T(8,128)(2,1)S(1)}, bf16[64,2048]{1,0:T(8,128)(2,1)S(1)}, u32[]{:S(2)}, u32[]{:S(2)}) collective-permute-start(bf16[64,2048]{1,0:T(8,128)(2,1)S(1)} %get-tuple-element.91), channel_id=1, source_target_pairs={{0,2},{1,3},{2,0},{3,1},{4,6},{5,7},{6,4},{7,5},{8,10},{9,11},{10,... | collective-permute-start | bytes 786440 | tf_op jit(solution)/shard_map/ppermute | solution.py:25
  36.2 14.1 %collective-permute-start.8 = (bf16[64,2048]{1,0:T(8,128)(2,1)S(1)}, bf16[64,2048]{1,0:T(8,128)(2,1)S(1)}, u32[]{:S(2)}, u32[]{:S(2)}) collective-permute-start(bf16[64,2048]{1,0:T(8,128)(2,1)S(1)} %get-tuple-element.89), channel_id=1, source_target_pairs={{0,2},{1,3},{2,0},{3,1},{4,6},{5,7},{6,4},{7,5},{8,10},{9,11},{10,... | collective-permute-start | bytes 786440 | tf_op jit(solution)/shard_map/ppermute | solution.py:25
  37.8 14.3 %collective-permute-start.10 = (bf16[64,2048]{1,0:T(8,128)(2,1)S(1)}, bf16[64,2048]{1,0:T(8,128)(2,1)S(1)}, u32[]{:S(2)}, u32[]{:S(2)}) collective-permute-start(bf16[64,2048]{1,0:T(8,128)(2,1)S(1)} %get-tuple-element.96), channel_id=1, source_target_pairs={{0,4},{1,5},{2,6},{3,7},{4,8},{5,9},{6,10},{7,11},{8,12},{9,13},{1... | collective-permute-start | bytes 786440 | tf_op jit(solution)/shard_map/ppermute | solution.py:25
  43.6 13.8 %collective-permute-start.11 = (bf16[64,2048]{1,0:T(8,128)(2,1)S(1)}, bf16[64,2048]{1,0:T(8,128)(2,1)S(1)}, u32[]{:S(2)}, u32[]{:S(2)}) collective-permute-start(bf16[64,2048]{1,0:T(8,128)(2,1)S(1)} %get-tuple-element.99), channel_id=1, source_target_pairs={{0,4},{1,5},{2,6},{3,7},{4,8},{5,9},{6,10},{7,11},{8,12},{9,13},{1... | collective-permute-start | bytes 786440 | tf_op jit(solution)/shard_map/ppermute | solution.py:25
  45.0 12.4 %collective-permute-start.6 = (bf16[64,2048]{1,0:T(8,128)(2,1)S(1)}, bf16[64,2048]{1,0:T(8,128)(2,1)S(1)}, u32[]{:S(2)}, u32[]{:S(2)}) collective-permute-start(bf16[64,2048]{1,0:T(8,128)(2,1)S(1)} %get-tuple-element.86), channel_id=1, source_target_pairs={{0,2},{1,3},{2,0},{3,1},{4,6},{5,7},{6,4},{7,5},{8,10},{9,11},{10,... | collective-permute-start | bytes 786440 | tf_op jit(solution)/shard_map/ppermute | solution.py:25
  50.4 12.2 %collective-permute-start.14 = (bf16[64,2048]{1,0:T(8,128)(2,1)S(1)}, bf16[64,2048]{1,0:T(8,128)(2,1)S(1)}, u32[]{:S(2)}, u32[]{:S(2)}) collective-permute-start(bf16[64,2048]{1,0:T(8,128)(2,1)S(1)} %get-tuple-element.105), channel_id=1, source_target_pairs={{0,4},{1,5},{2,6},{3,7},{4,8},{5,9},{6,10},{7,11},{8,12},{9,13},{1... | collective-permute-start | bytes 786440 | tf_op jit(solution)/shard_map/ppermute | solution.py:25
  52.1 11.0 %collective-permute-start.17 = (bf16[64,2048]{1,0:T(8,128)(2,1)S(1)}, bf16[64,2048]{1,0:T(8,128)(2,1)S(1)}, u32[]{:S(2)}, u32[]{:S(2)}) collective-permute-start(bf16[64,2048]{1,0:T(8,128)(2,1)S(1)} %collective-permute-done.10.refs_3_.refs_1_.refs_0_), channel_id=1, source_target_pairs={{0,2},{1,3},{2,0},{3,1},{4,6},{5,7},{6,4},{7,5},{8,10},{9,11},{10,... | collective-permute-start | bytes 786440 | tf_op jit(solution)/shard_map/ppermute | solution.py:25
  57.5 15.5 %collective-permute-start.12 = (bf16[64,2048]{1,0:T(8,128)(2,1)S(1)}, bf16[64,2048]{1,0:T(8,128)(2,1)S(1)}, u32[]{:S(2)}, u32[]{:S(2)}) collective-permute-start(bf16[64,2048]{1,0:T(8,128)(2,1)S(1)} %get-tuple-element.100), channel_id=1, source_target_pairs={{0,4},{1,5},{2,6},{3,7},{4,8},{5,9},{6,10},{7,11},{8,12},{9,13},{1... | collective-permute-start | bytes 786440 | tf_op jit(solution)/shard_map/ppermute | solution.py:25
  59.5 14.1 %collective-permute-start.16 = (bf16[64,2048]{1,0:T(8,128)(2,1)S(1)}, bf16[64,2048]{1,0:T(8,128)(2,1)S(1)}, u32[]{:S(2)}, u32[]{:S(2)}) collective-permute-start(bf16[64,2048]{1,0:T(8,128)(2,1)S(1)} %collective-permute-done.11.refs_3_.refs_1_), channel_id=1, source_target_pairs={{0,2},{1,3},{2,0},{3,1},{4,6},{5,7},{6,4},{7,5},{8,10},{9,11},{10,... | collective-permute-start | bytes 786440 | tf_op jit(solution)/shard_map/ppermute | solution.py:25
  62.5 16.5 %collective-permute-start.15 = (bf16[64,2048]{1,0:T(8,128)(2,1)S(1)}, bf16[64,2048]{1,0:T(8,128)(2,1)S(1)}, u32[]{:S(2)}, u32[]{:S(2)}) collective-permute-start(bf16[64,2048]{1,0:T(8,128)(2,1)S(1)} %collective-permute-done.14.refs_9_.refs_0_.refs_1_), channel_id=1, source_target_pairs={{0,2},{1,3},{2,0},{3,1},{4,6},{5,7},{6,4},{7,5},{8,10},{9,11},{10,... | collective-permute-start | bytes 786440 | tf_op jit(solution)/shard_map/ppermute | solution.py:25
  67.0 23.2 %collective-permute-start.19 = (bf16[64,2048]{1,0:T(8,128)(2,1)S(1)}, bf16[64,2048]{1,0:T(8,128)(2,1)S(1)}, u32[]{:S(2)}, u32[]{:S(2)}) collective-permute-start(bf16[64,2048]{1,0:T(8,128)(2,1)S(1)} %get-tuple-element.115), channel_id=1, source_target_pairs={{0,2},{1,3},{2,0},{3,1},{4,6},{5,7},{6,4},{7,5},{8,10},{9,11},{10,... | collective-permute-start | bytes 786440 | tf_op jit(solution)/shard_map/ppermute | solution.py:25
  68.6 23.8 %collective-permute-start.21 = (bf16[1,128,2048]{2,1,0:T(8,128)(2,1)S(1)}, bf16[1,128,2048]{2,1,0:T(8,128)(2,1)S(1)}, u32[]{:S(2)}, u32[]{:S(2)}) collective-permute-start(bf16[1,128,2048]{2,1,0:T(8,128)(2,1)S(1)} %get-tuple-element.121), channel_id=1, source_target_pairs={{0,126},{1,127},{2,124},{3,125},{4,122},{5,123},{6,120},{7,121},{8... | collective-permute-start | bytes 1572872 | tf_op jit(solution)/shard_map/ppermute | solution.py:25
  73.0 13.2 %collective-permute-start.13 = (bf16[64,2048]{1,0:T(8,128)(2,1)S(1)}, bf16[64,2048]{1,0:T(8,128)(2,1)S(1)}, u32[]{:S(2)}, u32[]{:S(2)}) collective-permute-start(bf16[64,2048]{1,0:T(8,128)(2,1)S(1)} %collective-permute-done.12.refs_1_), channel_id=1, source_target_pairs={{0,2},{1,3},{2,0},{3,1},{4,6},{5,7},{6,4},{7,5},{8,10},{9,11},{10,... | collective-permute-start | bytes 786440 | tf_op jit(solution)/shard_map/ppermute | solution.py:25
  77.5 15.5 %collective-permute-start.20 = (bf16[64,2048]{1,0:T(8,128)(2,1)S(1)}, bf16[64,2048]{1,0:T(8,128)(2,1)S(1)}, u32[]{:S(2)}, u32[]{:S(2)}) collective-permute-start(bf16[64,2048]{1,0:T(8,128)(2,1)S(1)} %get-tuple-element.119), channel_id=1, source_target_pairs={{0,2},{1,3},{2,0},{3,1},{4,6},{5,7},{6,4},{7,5},{8,10},{9,11},{10,... | collective-permute-start | bytes 786440 | tf_op jit(solution)/shard_map/ppermute | solution.py:25
  79.0 17.1 %collective-permute-start.23 = (bf16[1,128,2048]{2,1,0:T(8,128)(2,1)S(1)}, bf16[1,128,2048]{2,1,0:T(8,128)(2,1)S(1)}, u32[]{:S(2)}, u32[]{:S(2)}) collective-permute-start(bf16[1,128,2048]{2,1,0:T(8,128)(2,1)S(1)} %get-tuple-element.127), channel_id=1, source_target_pairs={{0,126},{1,127},{2,124},{3,125},{4,122},{5,123},{6,120},{7,121},{8... | collective-permute-start | bytes 1572872 | tf_op jit(solution)/shard_map/ppermute | solution.py:25
  86.2 10.5 %collective-permute-start.22 = (bf16[64,2048]{1,0:T(8,128)(2,1)S(1)}, bf16[64,2048]{1,0:T(8,128)(2,1)S(1)}, u32[]{:S(2)}, u32[]{:S(2)}) collective-permute-start(bf16[64,2048]{1,0:T(8,128)(2,1)S(1)} %get-tuple-element.125), channel_id=1, source_target_pairs={{0,2},{1,3},{2,0},{3,1},{4,6},{5,7},{6,4},{7,5},{8,10},{9,11},{10,... | collective-permute-start | bytes 786440 | tf_op jit(solution)/shard_map/ppermute | solution.py:25
  90.2 8.9 %collective-permute-start.18 = (bf16[64,2048]{1,0:T(8,128)(2,1)S(1)}, bf16[64,2048]{1,0:T(8,128)(2,1)S(1)}, u32[]{:S(2)}, u32[]{:S(2)}) collective-permute-start(bf16[64,2048]{1,0:T(8,128)(2,1)S(1)} %get-tuple-element.113), channel_id=1, source_target_pairs={{0,2},{1,3},{2,0},{3,1},{4,6},{5,7},{6,4},{7,5},{8,10},{9,11},{10,... | collective-permute-start | bytes 786440 | tf_op jit(solution)/shard_map/ppermute | solution.py:25
  (1 other events, 5.3 us)

commit v6 on v5

--- a/solution.py
+++ b/solution.py
@@ -10,7 +10,7 @@
 eps = 1e-05
 AXES = ("section", "tensor")
 Y = 4
-HB = 512
+HB = 1024
 MIB = 2**20
 ROWS = 64
 
@@ -140,31 +140,41 @@
     )[0]
 
 
-def load_kernel(idx, first, second, held, sems):
-    parts = sems.shape[0]
-    pieces = [pl.ds(k * (held.shape[0] // parts), held.shape[0] // parts) for k in range(parts)]
-
-    def run(w):
-        loads = [pltpu.make_async_copy(w.at[0, 0, p], held.at[p], sems.at[k]) for k, p in enumerate(pieces)]
-        for load in loads:
+def load_kernel(idx, w, first, second, held_w, held, sems):
+    parts = sems.shape[0] // 2
+
+    def pieces(ref):
+        size = ref.shape[0] // parts
+        return [pl.ds(k * size, size) for k in range(parts)]
+
+    loads = [pltpu.make_async_copy(w.at[0, idx[0], p], held_w.at[p], sems.at[k]) for k, p in enumerate(pieces(held_w))]
+    for load in loads:
+        load.start()
+
+    def run(ref):
+        more = [pltpu.make_async_copy(ref.at[0, 0, p], held.at[p], sems.at[parts + k]) for k, p in enumerate(pieces(held))]
+        for load in more:
             load.start()
-        for load in loads:
+        for load in more:
             load.wait()
 
-    pl.when(idx[0] == 0)(lambda: run(first))
-    pl.when(idx[0] != 0)(lambda: run(second))
-
-
-def load(order, which, first, second):
+    pl.when(idx[1] == 0)(lambda: run(first))
+    pl.when(idx[1] != 0)(lambda: run(second))
+    for load in loads:
+        load.wait()
+
+
+def load(order, group, which, w, first, second, behind=()):
     return order.call(
         load_kernel,
         "load",
-        [pltpu.VMEM(first.shape[2:], first.dtype)],
-        [SMEM_SPEC, HBM_SPEC, HBM_SPEC],
-        (which.reshape(1), in_hbm(first), in_hbm(second)),
+        [pltpu.VMEM(w.shape[2:], w.dtype), pltpu.VMEM(first.shape[2:], first.dtype)],
+        [SMEM_SPEC, HBM_SPEC, HBM_SPEC, HBM_SPEC],
+        (jnp.stack([group, which]), in_hbm(w), in_hbm(first), in_hbm(second)),
         [pltpu.SemaphoreType.DMA((8,))],
-        us=1.7,
-    )[0]
+        us=3.4,
+        behind=behind,
+    )
 
 
 def normalize(x, gain_row):
@@ -261,6 +271,44 @@
     keep[...] = kept_rows(idx, window(own, lo, rows), window(par, lo, rows)) + total[:rows]
 
 
+def down_load_kernel(lo, idx, own, par, hidden, w_out, r_out, give, keep, held, sems):
+    rows = give.shape[0]
+    units, parts = w_out.shape[0], sems.shape[0]
+    step = units // parts
+    loads = []
+    for k in range(parts):
+        piece = pl.ds(k * step, step)
+        loads.append(pltpu.make_async_copy(r_out.at[0, 0, piece], held.at[piece], sems.at[k]))
+        loads[-1].start()
+    mine = pl.ds(2 * lo, 2 * rows)
+    total = jnp.dot(hidden[mine, pl.ds(0, units)], w_out[...], preferred_element_type=jnp.float32)
+    cut = parts // 2
+    for half in range(2):
+        for load in loads[half * cut : (half + 1) * cut]:
+            load.wait()
+        first, size = half * cut * step, cut * step
+        total += jnp.dot(
+            hidden[mine, pl.ds(units + first, size)], held[pl.ds(first, size), :], preferred_element_type=jnp.float32
+        )
+    give[...] = total[rows:].astype(jnp.bfloat16)
+    keep[...] = kept_rows(idx, window(own, lo, rows), window(par, lo, rows)) + total[:rows]
+
+
+def down_load(order, idx, own, par, hidden, w_out, r_out, lo):
+    d = own.shape[1]
+    return order.call(
+        functools.partial(down_load_kernel, lo),
+        "down_load",
+        [jax.ShapeDtypeStruct((ROWS, d), jnp.bfloat16), jax.ShapeDtypeStruct((ROWS, d), jnp.float32)]
+        + [pltpu.VMEM(r_out.shape[2:], r_out.dtype)],
+        [SMEM_SPEC] + [VMEM_SPEC] * 4 + [HBM_SPEC],
+        (idx, own, par, hidden, in_vmem(w_out), in_hbm(r_out)),
+        [pltpu.SemaphoreType.DMA((8,))],
+        vmem=8 * MIB,
+        us=2,
+    )
+
+
 def down(order, idx, own, par, hidden, w_out, r_out, lo, behind=()):
     d = own.shape[1]
     return order.call(
@@ -339,9 +387,8 @@
     r_second = route(copy_group(order, 1 - g1, w_out, 0.05), to_other_core)
     ((w_in1, w_out1, r_in1),) = pick(order, (g1,), (w_in, w_out, r_in), us=0.1)
     hidden = up_rows(order, idx1, own[0], par[0], gain, w_in1, r_in1)
-    ((r_out1,),) = pick(order, (jnp.zeros_like(g1),), (r_first,))
+    give, keep0, r_out1 = down_load(order, idx1, own[0], par[0], hidden, w_out1, r_first, 0)
     w1 = (w_in1, w_out1, r_in1, r_out1)
-    give, keep0 = down(order, idx1, own[0], par[0], hidden, w_out1, r_out1, 0)
     got0 = across(give)
     give, keep1 = down(order, idx1, own[0], par[0], hidden, w_out1, r_out1, ROWS, (par[1], g2.reshape(1)))
     got1 = across(give)
@@ -353,8 +400,7 @@
     x1 = onward(join(order, keep1, got1))
     ((w_in2, w_out2),) = pick(order, (g2,), (w_in, w_out))
     x2 = onward(join(order, keep2, got2))
-    ((r_in2,),) = pick(order, (g2,), (r_in,), (x0,))
-    r_out2 = load(order, g2 - g1, r_first, r_second)
+    r_in2, r_out2 = load(order, g2, g2 - g1, r_in, r_first, r_second, (x0,))
     x3 = onward(join(order, keep3, got3, (x1,)))
     w2 = (w_in2, w_out2, r_in2, r_out2)
 

time: 101 us -> 99.8 us (0.988)
  Pallas kernels: 58 us -> 55.2 us
  waiting for transfers between devices: 6.83 us -> 8.32 us
    pallas_call x29 -> x27, Pallas kernels: 58 us -> 55.2 us  [call(): pl.pallas_call(with_token, out_shape=tuple(outs) + (jax.ShapeDtypeStruct(...]
    ppermute x24, waiting for transfers between devices: 6.83 us -> 8.32 us  [route(): return lax.ppermute(x, AXES, pairs)]
  transfers between devices with their start and end apart: 24 -> 24, of which waited for: 3 -> 5; matrix products, arithmetic and copies ran while one was open for 1% -> 2% of each run, Pallas kernels for 57% -> 55%
where the time goes in v6:
time: 99.8 us; the launch traced here: 99.3 us
  Pallas kernels  55.2 us (55%)
  starting transfers between devices  32 us (32%)
  waiting for transfers between devices  8.32 us (8%)
  between operations  2.14 us (2%)
  local copies, waits for them, and re-layouts  1.28 us (1%)
    pallas_call x27, Pallas kernels, call(): pl.pallas_call(with_token, out_shape=tuple(outs) + (jax.ShapeDtypeStruct(...  55.2 us
    ppermute x24, starting transfers between devices, route(): return lax.ppermute(x, AXES, pairs)  32 us
    ppermute x24, waiting for transfers between devices, route(): return lax.ppermute(x, AXES, pairs)  8.32 us
  transfers between devices with their start and end apart: 24, of which 5 were waited for; matrix products, arithmetic and copies ran while one was open for 2% of the time, Pallas kernels for 55%

profile of v6, /device:TPU:0, one launch (start us, length us, event | category | flops | bytes accessed | tf_op | source)
XLA Modules:
  0.0 99.3 jit_solution(12546059062145574622)
XLA Ops:
  2.0 1.7 %collective-permute-start.3 = (bf16[128,2048]{1,0:T(8,128)(2,1)S(1)}, bf16[128,2048]{1,0:T(8,128)(2,1)S(1)}, u32[]{:S(2)}, u32[]{:S(2)}) collective-permute-start(bf16[128,2048]{1,0:T(8,128)(2,1)S(1)} %get-tuple-element.130.refs_1_), channel_id=1, source_target_pairs={{0,2},{1,3},{2,0},{3,1},{4,6},{5,7},{6,4},{7,5},{8,10},{9,11},{10,... | collective-permute-start | bytes 1572872 | tf_op jit(solution)/shard_map/ppermute | solution.py:25
  5.9 3.6 %copy_group.2 = (bf16[1,1,1024,2048]{3,2,1,0:T(8,128)(2,1)}, f32[8,128]{1,0:T(8,128)S(1)}) custom-call(s32[1]{0:T(128)} %copy.7.refs_0_, bf16[1,2,1024,2048]{3,2,1,0:T(8,128)(2,1)} %refs_2_.3, f32[8,128]{1,0:T(8,128)S(1)} %broadcast_in_dim.3.refs_2_), custom_call_target="tpu_custom_call" | custom-call | flops 57500000 | bytes 16384 | tf_op jit(solution)/shard_map/copy_group/pallas_call | solution.py:65
  10.2 3.6 %copy_group.3 = (bf16[1,1,1024,2048]{3,2,1,0:T(8,128)(2,1)}, f32[8,128]{1,0:T(8,128)S(1)}) custom-call(s32[1]{0:T(128)} %bitcast.5.refs_0_, bf16[1,2,1024,2048]{3,2,1,0:T(8,128)(2,1)} %refs_2_.3, f32[8,128]{1,0:T(8,128)S(1)} %get-tuple-element.66.refs_2_), custom_call_target="tpu_custom_call" | custom-call | flops 57500000 | bytes 16384 | tf_op jit(solution)/shard_map/copy_group/pallas_call | solution.py:65
  14.9 5.2 %pick_group.2 = (bf16[2048,1024]{1,0:T(8,128)(2,1)S(1)}, bf16[1024,2048]{1,0:T(8,128)(2,1)S(1)}, bf16[2048,1024]{1,0:T(8,128)(2,1)S(1)}, f32[8,128]{1,0:T(8,128)S(1)}) custom-call(s32[3]{0:T(128)S(1)} %stack.35.refs_0_, bf16[1,2,2048,1024]{3,2,1,0:T(8,128)(2,1)} %refs_1_.7, bf16[1,2,1024,2048]{3,2,1,0:T(8,128)(2,1)} %refs_2_.3, ...), custom_call_target="tpu_custom_call" | custom-call | flops 115000000 | bytes 16384 | tf_op jit(solution)/shard_map/pick_group/pallas_call | solution.py:65
  20.1 3.9 %up.1 = (bf16[256,2048]{1,0:T(8,128)(2,1)S(1)}, f32[8,128]{1,0:T(8,128)S(1)}) custom-call(s32[2]{0:T(128)S(1)} %pad_add_fusion.1.refs_0_, bf16[128,2048]{1,0:T(8,128)(2,1)S(1)} %get-tuple-element.130.refs_1_, bf16[128,2048]{1,0:T(8,128)(2,1)S(1)} %collective-permute-done.3.refs_2_, bf16[1,2,2048]{2,1,0:T(2,128)(2,1)S(1)} %copy-done, ...), custom_call_target="tpu_custom_call" | custom-call | flops 57500000256 | bytes 16384 | tf_op jit(solution)/shard_map/up/pallas_call | solution.py:65
  24.1 3.5 %down_load.1 = (bf16[64,2048]{1,0:T(8,128)(2,1)S(1)}, f32[64,2048]{1,0:T(8,128)S(1)}, bf16[1024,2048]{1,0:T(8,128)(2,1)S(1)}, f32[8,128]{1,0:T(8,128)S(1)}) custom-call(s32[2]{0:T(128)S(1)} %pad_add_fusion.1.refs_0_, bf16[128,2048]{1,0:T(8,128)(2,1)S(1)} %get-tuple-element.130.refs_1_, bf16[128,2048]{1,0:T(8,128)(2,1)S(1)} %collective-permute-done.3.refs_2_, ...), custom_call_target="tpu_custom_call" | custom-call | flops 2300000000 | bytes 16384 | tf_op jit(solution)/shard_map/down_load/pallas_call | solution.py:65
  29.2 1.8 %down.1 = (bf16[64,2048]{1,0:T(8,128)(2,1)S(1)}, f32[64,2048]{1,0:T(8,128)S(1)}, f32[8,128]{1,0:T(8,128)S(1)}) custom-call(s32[2]{0:T(128)S(1)} %pad_add_fusion.1.refs_0_, bf16[128,2048]{1,0:T(8,128)(2,1)S(1)} %get-tuple-element.130.refs_1_, bf16[128,2048]{1,0:T(8,128)(2,1)S(1)} %collective-permute-done.3.refs_2_, ...), custom_call_target="tpu_custom_call" | custom-call | flops 2300000000 | bytes 16384 | tf_op jit(solution)/shard_map/down/pallas_call | solution.py:65
  31.6 3.6 %block.6 = (bf16[64,2048]{1,0:T(8,128)(2,1)S(1)}, f32[64,2048]{1,0:T(8,128)S(1)}, f32[8,128]{1,0:T(8,128)S(1)}) custom-call(s32[2]{0:T(128)S(1)} %pad_add_fusion.1.refs_0_, bf16[128,2048]{1,0:T(8,128)(2,1)S(1)} %get-tuple-element.131.refs_1_, bf16[128,2048]{1,0:T(8,128)(2,1)S(1)} %collective-permute-done.1.refs_7_.refs_2_, bf16[1,2,2048]{2,1,0:T(2,128)(2,1)S(1)} %copy-done, ...), custom_call_target="tpu_custom_call" | custom-call | flops 4600000000 | bytes 16384 | tf_op jit(solution)/shard_map/block/pallas_call | solution.py:65
  36.9 1.8 %collective-permute-start.10 = (bf16[64,2048]{1,0:T(8,128)(2,1)S(1)}, bf16[64,2048]{1,0:T(8,128)(2,1)S(1)}, u32[]{:S(2)}, u32[]{:S(2)}) collective-permute-start(bf16[64,2048]{1,0:T(8,128)(2,1)S(1)} %get-tuple-element.93), channel_id=1, source_target_pairs={{0,4},{1,5},{2,6},{3,7},{4,8},{5,9},{6,10},{7,11},{8,12},{9,13},{1... | collective-permute-start | bytes 786440 | tf_op jit(solution)/shard_map/ppermute | solution.py:25
  38.7 3.6 %block.7 = (bf16[64,2048]{1,0:T(8,128)(2,1)S(1)}, f32[64,2048]{1,0:T(8,128)S(1)}, f32[8,128]{1,0:T(8,128)S(1)}) custom-call(s32[2]{0:T(128)S(1)} %pad_add_fusion.1.refs_0_, bf16[128,2048]{1,0:T(8,128)(2,1)S(1)} %get-tuple-element.131.refs_1_, bf16[128,2048]{1,0:T(8,128)(2,1)S(1)} %collective-permute-done.1.refs_7_.refs_2_, bf16[1,2,2048]{2,1,0:T(2,128)(2,1)S(1)} %copy-done, ...), custom_call_target="tpu_custom_call" | custom-call | flops 4600000000 | bytes 16384 | tf_op jit(solution)/shard_map/block/pallas_call | solution.py:65
  42.5 1.6 %collective-permute-start.11 = (bf16[64,2048]{1,0:T(8,128)(2,1)S(1)}, bf16[64,2048]{1,0:T(8,128)(2,1)S(1)}, u32[]{:S(2)}, u32[]{:S(2)}) collective-permute-start(bf16[64,2048]{1,0:T(8,128)(2,1)S(1)} %get-tuple-element.95), channel_id=1, source_target_pairs={{0,4},{1,5},{2,6},{3,7},{4,8},{5,9},{6,10},{7,11},{8,12},{9,13},{1... | collective-permute-start | bytes 786440 | tf_op jit(solution)/shard_map/ppermute | solution.py:25
  45.6 4.0 %pick_group.3 = (bf16[2048,1024]{1,0:T(8,128)(2,1)S(1)}, bf16[1024,2048]{1,0:T(8,128)(2,1)S(1)}, f32[8,128]{1,0:T(8,128)S(1)}) custom-call(s32[2]{0:T(128)S(1)} %pad_add_fusion.3.refs_0_, bf16[1,2,2048,1024]{3,2,1,0:T(8,128)(2,1)} %refs_1_.7, bf16[1,2,1024,2048]{3,2,1,0:T(8,128)(2,1)} %refs_2_.3, f32[8,128]{1,0:T(8,128)S(1)} %get-tuple-element.90.refs_3_), custom_call_target="tpu_custom_call" | custom-call | flops 3910000128 | bytes 16384 | tf_op jit(solution)/shard_map/pick_group/pallas_call | solution.py:65
  51.8 4.0 %load.1 = (bf16[2048,1024]{1,0:T(8,128)(2,1)S(1)}, bf16[1024,2048]{1,0:T(8,128)(2,1)S(1)}, f32[8,128]{1,0:T(8,128)S(1)}) custom-call(s32[2]{0:T(128)S(1)} %pad_add_fusion.2.refs_0_, bf16[1,2,2048,1024]{3,2,1,0:T(8,128)(2,1)} %collective-permute-done.2.refs_3_.refs_1_, bf16[1,1,1024,2048]{3,2,1,0:T(8,128)(2,1)} %collective-permute-done.4.refs_5_.refs_2_, ...), custom_call_target="tpu_custom_call" | custom-call | flops 3910000128 | bytes 16384 | tf_op jit(solution)/shard_map/load/pallas_call | solution.py:65
  56.1 2.0 %collective-permute-start.12 = (bf16[64,2048]{1,0:T(8,128)(2,1)S(1)}, bf16[64,2048]{1,0:T(8,128)(2,1)S(1)}, u32[]{:S(2)}, u32[]{:S(2)}) collective-permute-start(bf16[64,2048]{1,0:T(8,128)(2,1)S(1)} %get-tuple-element.96), channel_id=1, source_target_pairs={{0,4},{1,5},{2,6},{3,7},{4,8},{5,9},{6,10},{7,11},{8,12},{9,13},{1... | collective-permute-start | bytes 786440 | tf_op jit(solution)/shard_map/ppermute | solution.py:25
  59.1 2.7 %collective-permute-done.14.refs_9_.refs_0_.refs_1_ = bf16[64,2048]{1,0:T(8,128)(2,1)S(1)} collective-permute-done((bf16[64,2048]{1,0:T(8,128)(2,1)S(1)}, bf16[64,2048]{1,0:T(8,128)(2,1)S(1)}, u32[]{:S(2)}, u32[]{:S(2)}) %collective-permute-start.14) | collective-permute-done | bytes 262176 | tf_op jit(solution)/shard_map/ppermute | solution.py:25
  62.3 3.6 %block.8 = (bf16[64,2048]{1,0:T(8,128)(2,1)S(1)}, f32[64,2048]{1,0:T(8,128)S(1)}, f32[8,128]{1,0:T(8,128)S(1)}) custom-call(s32[2]{0:T(128)S(1)} %pad_add_fusion.refs_0_, bf16[64,2048]{1,0:T(8,128)(2,1)S(1)} %collective-permute-done.10.refs_5_.refs_1_.refs_0_, bf16[64,2048]{1,0:T(8,128)(2,1)S(1)} %collective-permute-done.17.refs_2_, ...), custom_call_target="tpu_custom_call" | custom-call | flops 1150000000 | bytes 16384 | tf_op jit(solution)/shard_map/block/pallas_call | solution.py:65
  65.9 1.7 %collective-permute-start.19 = (bf16[64,2048]{1,0:T(8,128)(2,1)S(1)}, bf16[64,2048]{1,0:T(8,128)(2,1)S(1)}, u32[]{:S(2)}, u32[]{:S(2)}) collective-permute-start(bf16[64,2048]{1,0:T(8,128)(2,1)S(1)} %get-tuple-element.111), channel_id=1, source_target_pairs={{0,2},{1,3},{2,0},{3,1},{4,6},{5,7},{6,4},{7,5},{8,10},{9,11},{10,... | collective-permute-start | bytes 786440 | tf_op jit(solution)/shard_map/ppermute | solution.py:25
  67.6 4.4 %collective-permute-start.21 = (bf16[1,128,2048]{2,1,0:T(8,128)(2,1)S(1)}, bf16[1,128,2048]{2,1,0:T(8,128)(2,1)S(1)}, u32[]{:S(2)}, u32[]{:S(2)}) collective-permute-start(bf16[1,128,2048]{2,1,0:T(8,128)(2,1)S(1)} %get-tuple-element.117), channel_id=1, source_target_pairs={{0,126},{1,127},{2,124},{3,125},{4,122},{5,123},{6,120},{7,121},{8... | collective-permute-start | bytes 1572872 | tf_op jit(solution)/shard_map/ppermute | solution.py:25
  72.7 3.6 %block.9 = (bf16[64,2048]{1,0:T(8,128)(2,1)S(1)}, f32[64,2048]{1,0:T(8,128)S(1)}, f32[8,128]{1,0:T(8,128)S(1)}) custom-call(s32[2]{0:T(128)S(1)} %pad_add_fusion.refs_0_, bf16[64,2048]{1,0:T(8,128)(2,1)S(1)} %collective-permute-done.11.refs_3_.refs_1_, bf16[64,2048]{1,0:T(8,128)(2,1)S(1)} %collective-permute-done.16.refs_2_, ...), custom_call_target="tpu_custom_call" | custom-call | flops 1150000000 | bytes 16384 | tf_op jit(solution)/shard_map/block/pallas_call | solution.py:65
  77.9 3.2 %collective-permute-start.23 = (bf16[1,128,2048]{2,1,0:T(8,128)(2,1)S(1)}, bf16[1,128,2048]{2,1,0:T(8,128)(2,1)S(1)}, u32[]{:S(2)}, u32[]{:S(2)}) collective-permute-start(bf16[1,128,2048]{2,1,0:T(8,128)(2,1)S(1)} %get-tuple-element.123), channel_id=1, source_target_pairs={{0,126},{1,127},{2,124},{3,125},{4,122},{5,123},{6,120},{7,121},{8... | collective-permute-start | bytes 1572872 | tf_op jit(solution)/shard_map/ppermute | solution.py:25
  81.0 3.6 %block.10 = (bf16[64,2048]{1,0:T(8,128)(2,1)S(1)}, f32[64,2048]{1,0:T(8,128)S(1)}, f32[8,128]{1,0:T(8,128)S(1)}) custom-call(s32[2]{0:T(128)S(1)} %pad_add_fusion.refs_0_, bf16[64,2048]{1,0:T(8,128)(2,1)S(1)} %collective-permute-done.14.refs_9_.refs_0_.refs_1_, bf16[64,2048]{1,0:T(8,128)(2,1)S(1)} %collective-permute-done.15.refs_2_, ...), custom_call_target="tpu_custom_call" | custom-call | flops 1150000000 | bytes 16384 | tf_op jit(solution)/shard_map/block/pallas_call | solution.py:65
  85.1 3.6 %block.11 = (bf16[64,2048]{1,0:T(8,128)(2,1)S(1)}, f32[64,2048]{1,0:T(8,128)S(1)}, f32[8,128]{1,0:T(8,128)S(1)}) custom-call(s32[2]{0:T(128)S(1)} %pad_add_fusion.refs_0_, bf16[64,2048]{1,0:T(8,128)(2,1)S(1)} %collective-permute-done.12.refs_1_, bf16[64,2048]{1,0:T(8,128)(2,1)S(1)} %collective-permute-done.13.refs_2_, bf16[1,2,2048]{2,1,0:T(2,128)(2,1)S(1)} %copy-done, ...), custom_call_target="tpu_custom_call" | custom-call | flops 1150000000 | bytes 16384 | tf_op jit(solution)/shard_map/block/pallas_call | solution.py:65
  88.8 1.7 %collective-permute-start.18 = (bf16[64,2048]{1,0:T(8,128)(2,1)S(1)}, bf16[64,2048]{1,0:T(8,128)(2,1)S(1)}, u32[]{:S(2)}, u32[]{:S(2)}) collective-permute-start(bf16[64,2048]{1,0:T(8,128)(2,1)S(1)} %get-tuple-element.109), channel_id=1, source_target_pairs={{0,2},{1,3},{2,0},{3,1},{4,6},{5,7},{6,4},{7,5},{8,10},{9,11},{10,... | collective-permute-start | bytes 786440 | tf_op jit(solution)/shard_map/ppermute | solution.py:25
  91.2 3.9 %collective-permute-done.23.refs_1_ = bf16[1,128,2048]{2,1,0:T(8,128)(2,1)S(1)} collective-permute-done((bf16[1,128,2048]{2,1,0:T(8,128)(2,1)S(1)}, bf16[1,128,2048]{2,1,0:T(8,128)(2,1)S(1)}, u32[]{:S(2)}, u32[]{:S(2)}) %collective-permute-start.23) | collective-permute-done | bytes 524320 | tf_op jit(solution)/shard_map/ppermute | solution.py:25
  (60 shorter events, 20.8 us)
Async XLA Ops:
  0.6 14.2 %collective-permute-start.2 = (bf16[1,2,2048,1024]{3,2,1,0:T(8,128)(2,1)}, bf16[1,2,2048,1024]{3,2,1,0:T(8,128)(2,1)}, u32[]{:S(2)}, u32[]{:S(2)}) collective-permute-start(bf16[1,2,2048,1024]{3,2,1,0:T(8,128)(2,1)} %refs_1_.7), channel_id=1, source_target_pairs={{0,1},{1,0},{2,3},{3,2},{4,5},{5,4},{6,7},{7,6},{8,9},{9,8},{10,11... | collective-permute-start | bytes 25165832 | tf_op jit(solution)/shard_map/ppermute | solution.py:25
  2.0 18.1 %collective-permute-start.3 = (bf16[128,2048]{1,0:T(8,128)(2,1)S(1)}, bf16[128,2048]{1,0:T(8,128)(2,1)S(1)}, u32[]{:S(2)}, u32[]{:S(2)}) collective-permute-start(bf16[128,2048]{1,0:T(8,128)(2,1)S(1)} %get-tuple-element.130.refs_1_), channel_id=1, source_target_pairs={{0,2},{1,3},{2,0},{3,1},{4,6},{5,7},{6,4},{7,5},{8,10},{9,11},{10,... | collective-permute-start | bytes 1572872 | tf_op jit(solution)/shard_map/ppermute | solution.py:25
  3.7 10.3 %collective-permute-start = (s32[1]{0:T(128)}, s32[1]{0:T(128)}, u32[]{:S(2)}, u32[]{:S(2)}) collective-permute-start(s32[1]{0:T(128)} %param.6), channel_id=1, source_target_pairs={{0,4},{1,5},{2,6},{3,7},{4,8},{5,9},{6,10},{7,11},{8,12},{9,13},{1... | collective-permute-start | bytes 20 | tf_op jit(solution)/shard_map/ppermute | solution.py:25
  9.5 14.6 %collective-permute-start.4 = (bf16[1,1,1024,2048]{3,2,1,0:T(8,128)(2,1)}, bf16[1,1,1024,2048]{3,2,1,0:T(8,128)(2,1)}, u32[]{:S(2)}, u32[]{:S(2)}) collective-permute-start(bf16[1,1,1024,2048]{3,2,1,0:T(8,128)(2,1)} %get-tuple-element.73), channel_id=1, source_target_pairs={{0,1},{1,0},{2,3},{3,2},{4,5},{5,4},{6,7},{7,6},{8,9},{9,8},{10,11... | collective-permute-start | bytes 12582920 | tf_op jit(solution)/shard_map/ppermute | solution.py:25
  9.6 19.6 %collective-permute-start.1 = (bf16[128,2048]{1,0:T(8,128)(2,1)S(1)}, bf16[128,2048]{1,0:T(8,128)(2,1)S(1)}, u32[]{:S(2)}, u32[]{:S(2)}) collective-permute-start(bf16[128,2048]{1,0:T(8,128)(2,1)S(1)} %get-tuple-element.131.refs_1_), channel_id=1, source_target_pairs={{0,2},{1,3},{2,0},{3,1},{4,6},{5,7},{6,4},{7,5},{8,10},{9,11},{10,... | collective-permute-start | bytes 1572872 | tf_op jit(solution)/shard_map/ppermute | solution.py:25
  14.0 37.8 %collective-permute-start.7 = (bf16[1,1,1024,2048]{3,2,1,0:T(8,128)(2,1)}, bf16[1,1,1024,2048]{3,2,1,0:T(8,128)(2,1)}, u32[]{:S(2)}, u32[]{:S(2)}) collective-permute-start(bf16[1,1,1024,2048]{3,2,1,0:T(8,128)(2,1)} %get-tuple-element.84), channel_id=1, source_target_pairs={{0,1},{1,0},{2,3},{3,2},{4,5},{5,4},{6,7},{7,6},{8,9},{9,8},{10,11... | collective-permute-start | bytes 12582920 | tf_op jit(solution)/shard_map/ppermute | solution.py:25
  27.6 9.2 %collective-permute-start.5 = (bf16[64,2048]{1,0:T(8,128)(2,1)S(1)}, bf16[64,2048]{1,0:T(8,128)(2,1)S(1)}, u32[]{:S(2)}, u32[]{:S(2)}) collective-permute-start(bf16[64,2048]{1,0:T(8,128)(2,1)S(1)} %get-tuple-element.77), channel_id=1, source_target_pairs={{0,2},{1,3},{2,0},{3,1},{4,6},{5,7},{6,4},{7,5},{8,10},{9,11},{10,... | collective-permute-start | bytes 786440 | tf_op jit(solution)/shard_map/ppermute | solution.py:25
  31.0 11.4 %collective-permute-start.9 = (bf16[64,2048]{1,0:T(8,128)(2,1)S(1)}, bf16[64,2048]{1,0:T(8,128)(2,1)S(1)}, u32[]{:S(2)}, u32[]{:S(2)}) collective-permute-start(bf16[64,2048]{1,0:T(8,128)(2,1)S(1)} %get-tuple-element.88), channel_id=1, source_target_pairs={{0,2},{1,3},{2,0},{3,1},{4,6},{5,7},{6,4},{7,5},{8,10},{9,11},{10,... | collective-permute-start | bytes 786440 | tf_op jit(solution)/shard_map/ppermute | solution.py:25
  35.2 14.4 %collective-permute-start.8 = (bf16[64,2048]{1,0:T(8,128)(2,1)S(1)}, bf16[64,2048]{1,0:T(8,128)(2,1)S(1)}, u32[]{:S(2)}, u32[]{:S(2)}) collective-permute-start(bf16[64,2048]{1,0:T(8,128)(2,1)S(1)} %get-tuple-element.86), channel_id=1, source_target_pairs={{0,2},{1,3},{2,0},{3,1},{4,6},{5,7},{6,4},{7,5},{8,10},{9,11},{10,... | collective-permute-start | bytes 786440 | tf_op jit(solution)/shard_map/ppermute | solution.py:25
  36.9 14.3 %collective-permute-start.10 = (bf16[64,2048]{1,0:T(8,128)(2,1)S(1)}, bf16[64,2048]{1,0:T(8,128)(2,1)S(1)}, u32[]{:S(2)}, u32[]{:S(2)}) collective-permute-start(bf16[64,2048]{1,0:T(8,128)(2,1)S(1)} %get-tuple-element.93), channel_id=1, source_target_pairs={{0,4},{1,5},{2,6},{3,7},{4,8},{5,9},{6,10},{7,11},{8,12},{9,13},{1... | collective-permute-start | bytes 786440 | tf_op jit(solution)/shard_map/ppermute | solution.py:25
  42.5 13.5 %collective-permute-start.11 = (bf16[64,2048]{1,0:T(8,128)(2,1)S(1)}, bf16[64,2048]{1,0:T(8,128)(2,1)S(1)}, u32[]{:S(2)}, u32[]{:S(2)}) collective-permute-start(bf16[64,2048]{1,0:T(8,128)(2,1)S(1)} %get-tuple-element.95), channel_id=1, source_target_pairs={{0,4},{1,5},{2,6},{3,7},{4,8},{5,9},{6,10},{7,11},{8,12},{9,13},{1... | collective-permute-start | bytes 786440 | tf_op jit(solution)/shard_map/ppermute | solution.py:25
  44.1 11.9 %collective-permute-start.6 = (bf16[64,2048]{1,0:T(8,128)(2,1)S(1)}, bf16[64,2048]{1,0:T(8,128)(2,1)S(1)}, u32[]{:S(2)}, u32[]{:S(2)}) collective-permute-start(bf16[64,2048]{1,0:T(8,128)(2,1)S(1)} %get-tuple-element.83), channel_id=1, source_target_pairs={{0,2},{1,3},{2,0},{3,1},{4,6},{5,7},{6,4},{7,5},{8,10},{9,11},{10,... | collective-permute-start | bytes 786440 | tf_op jit(solution)/shard_map/ppermute | solution.py:25
  49.7 12.1 %collective-permute-start.14 = (bf16[64,2048]{1,0:T(8,128)(2,1)S(1)}, bf16[64,2048]{1,0:T(8,128)(2,1)S(1)}, u32[]{:S(2)}, u32[]{:S(2)}) collective-permute-start(bf16[64,2048]{1,0:T(8,128)(2,1)S(1)} %get-tuple-element.101), channel_id=1, source_target_pairs={{0,4},{1,5},{2,6},{3,7},{4,8},{5,9},{6,10},{7,11},{8,12},{9,13},{1... | collective-permute-start | bytes 786440 | tf_op jit(solution)/shard_map/ppermute | solution.py:25
  51.2 11.1 %collective-permute-start.17 = (bf16[64,2048]{1,0:T(8,128)(2,1)S(1)}, bf16[64,2048]{1,0:T(8,128)(2,1)S(1)}, u32[]{:S(2)}, u32[]{:S(2)}) collective-permute-start(bf16[64,2048]{1,0:T(8,128)(2,1)S(1)} %collective-permute-done.10.refs_5_.refs_1_.refs_0_), channel_id=1, source_target_pairs={{0,2},{1,3},{2,0},{3,1},{4,6},{5,7},{6,4},{7,5},{8,10},{9,11},{10,... | collective-permute-start | bytes 786440 | tf_op jit(solution)/shard_map/ppermute | solution.py:25
  56.1 16.0 %collective-permute-start.12 = (bf16[64,2048]{1,0:T(8,128)(2,1)S(1)}, bf16[64,2048]{1,0:T(8,128)(2,1)S(1)}, u32[]{:S(2)}, u32[]{:S(2)}) collective-permute-start(bf16[64,2048]{1,0:T(8,128)(2,1)S(1)} %get-tuple-element.96), channel_id=1, source_target_pairs={{0,4},{1,5},{2,6},{3,7},{4,8},{5,9},{6,10},{7,11},{8,12},{9,13},{1... | collective-permute-start | bytes 786440 | tf_op jit(solution)/shard_map/ppermute | solution.py:25
  58.1 14.6 %collective-permute-start.16 = (bf16[64,2048]{1,0:T(8,128)(2,1)S(1)}, bf16[64,2048]{1,0:T(8,128)(2,1)S(1)}, u32[]{:S(2)}, u32[]{:S(2)}) collective-permute-start(bf16[64,2048]{1,0:T(8,128)(2,1)S(1)} %collective-permute-done.11.refs_3_.refs_1_), channel_id=1, source_target_pairs={{0,2},{1,3},{2,0},{3,1},{4,6},{5,7},{6,4},{7,5},{8,10},{9,11},{10,... | collective-permute-start | bytes 786440 | tf_op jit(solution)/shard_map/ppermute | solution.py:25
  61.8 16.0 %collective-permute-start.15 = (bf16[64,2048]{1,0:T(8,128)(2,1)S(1)}, bf16[64,2048]{1,0:T(8,128)(2,1)S(1)}, u32[]{:S(2)}, u32[]{:S(2)}) collective-permute-start(bf16[64,2048]{1,0:T(8,128)(2,1)S(1)} %collective-permute-done.14.refs_9_.refs_0_.refs_1_), channel_id=1, source_target_pairs={{0,2},{1,3},{2,0},{3,1},{4,6},{5,7},{6,4},{7,5},{8,10},{9,11},{10,... | collective-permute-start | bytes 786440 | tf_op jit(solution)/shard_map/ppermute | solution.py:25
  65.9 22.9 %collective-permute-start.19 = (bf16[64,2048]{1,0:T(8,128)(2,1)S(1)}, bf16[64,2048]{1,0:T(8,128)(2,1)S(1)}, u32[]{:S(2)}, u32[]{:S(2)}) collective-permute-start(bf16[64,2048]{1,0:T(8,128)(2,1)S(1)} %get-tuple-element.111), channel_id=1, source_target_pairs={{0,2},{1,3},{2,0},{3,1},{4,6},{5,7},{6,4},{7,5},{8,10},{9,11},{10,... | collective-permute-start | bytes 786440 | tf_op jit(solution)/shard_map/ppermute | solution.py:25
  67.6 22.9 %collective-permute-start.21 = (bf16[1,128,2048]{2,1,0:T(8,128)(2,1)S(1)}, bf16[1,128,2048]{2,1,0:T(8,128)(2,1)S(1)}, u32[]{:S(2)}, u32[]{:S(2)}) collective-permute-start(bf16[1,128,2048]{2,1,0:T(8,128)(2,1)S(1)} %get-tuple-element.117), channel_id=1, source_target_pairs={{0,126},{1,127},{2,124},{3,125},{4,122},{5,123},{6,120},{7,121},{8... | collective-permute-start | bytes 1572872 | tf_op jit(solution)/shard_map/ppermute | solution.py:25
  72.1 12.6 %collective-permute-start.13 = (bf16[64,2048]{1,0:T(8,128)(2,1)S(1)}, bf16[64,2048]{1,0:T(8,128)(2,1)S(1)}, u32[]{:S(2)}, u32[]{:S(2)}) collective-permute-start(bf16[64,2048]{1,0:T(8,128)(2,1)S(1)} %collective-permute-done.12.refs_1_), channel_id=1, source_target_pairs={{0,2},{1,3},{2,0},{3,1},{4,6},{5,7},{6,4},{7,5},{8,10},{9,11},{10,... | collective-permute-start | bytes 786440 | tf_op jit(solution)/shard_map/ppermute | solution.py:25
  76.3 14.9 %collective-permute-start.20 = (bf16[64,2048]{1,0:T(8,128)(2,1)S(1)}, bf16[64,2048]{1,0:T(8,128)(2,1)S(1)}, u32[]{:S(2)}, u32[]{:S(2)}) collective-permute-start(bf16[64,2048]{1,0:T(8,128)(2,1)S(1)} %get-tuple-element.115), channel_id=1, source_target_pairs={{0,2},{1,3},{2,0},{3,1},{4,6},{5,7},{6,4},{7,5},{8,10},{9,11},{10,... | collective-permute-start | bytes 786440 | tf_op jit(solution)/shard_map/ppermute | solution.py:25
  77.9 17.3 %collective-permute-start.23 = (bf16[1,128,2048]{2,1,0:T(8,128)(2,1)S(1)}, bf16[1,128,2048]{2,1,0:T(8,128)(2,1)S(1)}, u32[]{:S(2)}, u32[]{:S(2)}) collective-permute-start(bf16[1,128,2048]{2,1,0:T(8,128)(2,1)S(1)} %get-tuple-element.123), channel_id=1, source_target_pairs={{0,126},{1,127},{2,124},{3,125},{4,122},{5,123},{6,120},{7,121},{8... | collective-permute-start | bytes 1572872 | tf_op jit(solution)/shard_map/ppermute | solution.py:25
  84.7 11.0 %collective-permute-start.22 = (bf16[64,2048]{1,0:T(8,128)(2,1)S(1)}, bf16[64,2048]{1,0:T(8,128)(2,1)S(1)}, u32[]{:S(2)}, u32[]{:S(2)}) collective-permute-start(bf16[64,2048]{1,0:T(8,128)(2,1)S(1)} %get-tuple-element.121), channel_id=1, source_target_pairs={{0,2},{1,3},{2,0},{3,1},{4,6},{5,7},{6,4},{7,5},{8,10},{9,11},{10,... | collective-permute-start | bytes 786440 | tf_op jit(solution)/shard_map/ppermute | solution.py:25
  88.8 9.4 %collective-permute-start.18 = (bf16[64,2048]{1,0:T(8,128)(2,1)S(1)}, bf16[64,2048]{1,0:T(8,128)(2,1)S(1)}, u32[]{:S(2)}, u32[]{:S(2)}) collective-permute-start(bf16[64,2048]{1,0:T(8,128)(2,1)S(1)} %get-tuple-element.109), channel_id=1, source_target_pairs={{0,2},{1,3},{2,0},{3,1},{4,6},{5,7},{6,4},{7,5},{8,10},{9,11},{10,... | collective-permute-start | bytes 786440 | tf_op jit(solution)/shard_map/ppermute | solution.py:25
  (1 other events, 5.3 us)
